TPU v7x, 32 devices: a whole 2x2x4 slice. The times are simulated.
32 devices in a mesh: groups: 2 (over x), node: 8 (over z, y), local: 2 (over core).
Axes of the slice: x: 2, y: 2, z: 4, core: 2. Of those that a mesh axis runs over, the one named last changes fastest.
Arguments:
- tokens: bfloat16 [2, 1024, 3584], P(None, ('groups', 'node', 'local')), parts along dimension 1, may hold values from -6 to 6
- expert_ids: int32 [2, 1024, 4], P(None, ('groups', 'node', 'local')), parts along dimension 1, may hold values from 0 to 7, all different within a row; in each aligned block of 32 rows (0 to 31, 32 to 63, ..., all dimensions but the last counted through in order) at most 20 rows name the same one
- gate_fixed: int32 [2, 1024, 4], P(None, ('groups', 'node', 'local')), parts along dimension 1, may hold values from 6554 to 65536
- w_gate: bfloat16 [8, 3584, 1024], P('node', None, 'local'), may hold values from -0.09375 to 0.09375
- w_up: bfloat16 [8, 3584, 1024], P('node', None, 'local'), may hold values from -0.09375 to 0.09375
- w_down: bfloat16 [8, 1024, 3584], P('node', 'local'), may hold values from -0.1875 to 0.1875
Outputs:
- moe_out: bfloat16 [2, 1024, 3584], P(None, ('groups', 'node', 'local')), parts along dimension 1
There are 2 independent parts, one for each index of `groups`. A program takes and returns all parts, laid end to end along the dimension named above; an argument that names none is the same for every part. Nothing has to cross between parts.
Inputs may be any that keep to these rules, and one draw needn't show every extreme that they name: `expert_ids`: each row names 4 different experts. Within each step, among the 32 rows of one device, no expert is named by more than 20 rows, a bound that some block reaches.
All inputs are finite; a program needn't handle non-finite values.
Results may differ from a plain program's by a relative error of at most 0.0057.
Values may be sent and summed in bfloat16 or wider, within the bound.
No kernel may reach another device: no remote copies, remote signals or barrier semaphores. Data moves between devices by JAX's collectives and lax.ppermute only.
A program may use at most 128 MiB of HBM per device.

v0:
```python
import jax
import jax.numpy as jnp
from jax import lax
from jax.sharding import PartitionSpec as P


def per_device(tokens, expert_ids, gate_fixed, w_gate, w_up, w_down):
    step_count, tok_rows, model_width = tokens.shape
    top_count = expert_ids.shape[2]
    node_count = lax.axis_size("node")
    halves = lax.axis_size("local")
    capacity = max(2, min(tok_rows, 5 * tok_rows * top_count // (4 * node_count)))
    gate_mat = w_gate[0]
    up_mat = w_up[0]
    down_mat = w_down[0]
    outputs = []
    for step_index in range(step_count):
        flat_ids = expert_ids[step_index].reshape(-1)
        hits_table = (flat_ids[:, None] == jnp.arange(node_count, dtype=jnp.int32)[None, :]).astype(
            jnp.int32
        )
        earlier = jnp.cumsum(hits_table, axis=0) - hits_table
        slot_index = jnp.sum(earlier * hits_table, axis=1)
        place_position = flat_ids * capacity + slot_index
        source = jnp.arange(tok_rows * top_count, dtype=jnp.int32) // top_count
        send_rows = jnp.zeros((node_count * capacity, model_width), jnp.bfloat16)
        send_rows = send_rows.at[place_position].set(tokens[step_index][source])
        send_rows, position = (send_rows.reshape(node_count, capacity, model_width), place_position)
        copies = jnp.broadcast_to(send_rows[:, None], (node_count, halves) + send_rows.shape[1:])
        copies = copies.reshape((node_count * halves,) + send_rows.shape[1:])
        received = lax.all_to_all(
            copies, ("node", "local"), split_axis=0, concat_axis=0, tiled=True
        )
        slot_count = received.shape[1]
        ordered = received.reshape(node_count, halves, slot_count, model_width).transpose(
            1, 0, 2, 3
        )
        ordered = ordered.reshape(halves * node_count * slot_count, model_width)
        gate_act = jnp.dot(ordered, gate_mat, preferred_element_type=jnp.float32)
        up_act = jnp.dot(ordered, up_mat, preferred_element_type=jnp.float32)
        hidden = (jax.nn.silu(gate_act) * up_act).astype(jnp.bfloat16)
        row_count = hidden.shape[0] // halves
        own_rows = lax.psum_scatter(
            jnp.dot(hidden, down_mat, preferred_element_type=jnp.float32),
            "local",
            scatter_dimension=0,
            tiled=True,
        )
        outgoing = own_rows.astype(jnp.bfloat16).reshape(
            node_count, row_count // node_count, model_width
        )
        picked = lax.all_to_all(outgoing, "node", split_axis=0, concat_axis=0, tiled=True).reshape(
            node_count * capacity, model_width
        )[position]
        weights = gate_fixed[step_index].reshape(-1).astype(jnp.float32) / 65536.0
        summed = (picked.astype(jnp.float32) * weights[:, None]).reshape(
            tok_rows, top_count, model_width
        )
        outputs.append(jnp.sum(summed, axis=1).astype(jnp.bfloat16))
    return jnp.stack(outputs)


def solution(mesh):
    in_specs = (
        P(None, ("groups", "node", "local"), None),
        P(None, ("groups", "node", "local"), None),
        P(None, ("groups", "node", "local"), None),
        P("node", None, "local"),
        P("node", None, "local"),
        P("node", "local", None),
    )
    out_specs = P(None, ("groups", "node", "local"), None)
    return jax.shard_map(
        per_device, mesh=mesh, in_specs=in_specs, out_specs=out_specs, check_vma=False
    )
```

profile of v0, /device:TPU:0, one launch (start us, length us, event | category | flops | bytes accessed | tf_op | source)
XLA Modules:
  0.0 288.3 jit_solution(3682835285373463534)
XLA Ops:
  6.5 0.7 fusion.53
  7.3 0.1 eq.30
  7.5 0.2 reduce_window_sum.17
  7.7 0.2 select_reduce_fusion.1
  8.0 0.1 mul.64
  8.1 1.1 slice_bitcast_fusion.1
  9.2 4.9 %scatter_custom_fusion = bf16[160,3584]{1,0:T(8,128)(2,1)S(1)} fusion(s32[128]{0:T(128)S(1)} %fusion.49, bf16[32,3584]{1,0:T(8,128)(2,1)S(1)} %get-tuple-element.5, s32[1024]{0:T(1024)S(1)} %pad_clamp_fusion.2, bf16[]{:T(256)} %constant.34.clone.1), kind=kCustom, calls=%fused_computation.28 | custom fusion | bytes 1146882 | tf_op jit(solution)/shard_map/scatter | solution.py:27
  14.1 0.3 broadcast_in_dim.8
  14.4 0.2 broadcast_in_dim.9
  14.6 70.4 %all_to_all.20 = bf16[16,20,3584]{2,1,0:T(8,128)(2,1)S(1)} all-to-all(bf16[16,20,3584]{2,1,0:T(8,128)(2,1)S(1)} %bitcast.69), channel_id=1, replica_groups=mesh['groups'=2,'node'=8,'local'=2] {'node','local'}, dimensions={0} | all-to-all | bytes 4587520 | tf_op jit(solution)/shard_map/all_to_all | solution.py:31
  85.0 2.2 copy.44
  87.2 1.3 copy.32
  88.5 2.1 reshape.187
  90.6 5.1 %fusion.10 = f32[320,512]{1,0:T(8,128)} fusion(bf16[320,3584]{1,0:T(8,128)(2,1)} %reshape.187, bf16[1,3584,512]{2,1,0:T(8,128)(2,1)} %param.9), kind=kOutput, calls=%fused_computation.16 | convolution fusion | flops 1174405120 | bytes 6619136 | tf_op jit(solution)/shard_map/dot_general | solution.py:39
  95.7 8.0 %fusion.2 = f32[320,3584]{1,0:T(8,128)} fusion(bf16[1,512,3584]{2,1,0:T(8,128)(2,1)} %param.11, bf16[320,3584]{1,0:T(8,128)(2,1)S(1)} %copy-done.1, bf16[1,3584,512]{2,1,0:T(8,128)(2,1)} %param.10, f32[320,512]{1,0:T(8,128)} %fusion.10), kind=kOutput, calls=%fused_computation.8 | convolution fusion | flops 2349793280 | bytes 14876672 | tf_op jit(solution)/shard_map/dot_general | solution.py:44
  103.8 0.2 reduce-scatter.5.cloned.1.call-start
  104.1 0.1 eq.34
  104.3 0.2 reduce_window_sum.18
  104.6 0.1 mul.71
  104.7 0.2 select_reduce_fusion
  104.9 4.9 %scatter_custom_fusion.1 = bf16[160,3584]{1,0:T(8,128)(2,1)S(1)} fusion(s32[128]{0:T(128)S(1)} %fusion.50, bf16[32,3584]{1,0:T(8,128)(2,1)S(1)} %get-tuple-element.6, s32[1024]{0:T(1024)S(1)} %pad_clamp_fusion.2, bf16[]{:T(256)} %constant.34.clone.1), kind=kCustom, calls=%fused_computation.26 | custom fusion | bytes 1146882 | tf_op jit(solution)/shard_map/scatter | solution.py:27
  109.8 0.3 broadcast_in_dim.10
  110.1 0.2 broadcast_in_dim.11
  110.3 66.4 %all_to_all.21 = bf16[16,20,3584]{2,1,0:T(8,128)(2,1)S(1)} all-to-all(bf16[16,20,3584]{2,1,0:T(8,128)(2,1)S(1)} %bitcast.71), channel_id=1, replica_groups=mesh['groups'=2,'node'=8,'local'=2] {'node','local'}, dimensions={0} | all-to-all | bytes 4587520 | tf_op jit(solution)/shard_map/all_to_all | solution.py:31
  176.7 2.2 copy.43
  179.0 1.3 copy.37
  180.3 2.1 reshape.192
  182.4 4.2 %fusion.8 = f32[320,512]{1,0:T(8,128)S(1)} fusion(bf16[320,3584]{1,0:T(8,128)(2,1)} %reshape.192, bf16[1,3584,512]{2,1,0:T(8,128)(2,1)} %param.9), kind=kOutput, calls=%fused_computation.14 | convolution fusion | flops 1174405120 | bytes 6619136 | tf_op jit(solution)/shard_map/dot_general | solution.py:39
  186.6 7.9 %fusion = f32[320,3584]{1,0:T(8,128)} fusion(bf16[1,512,3584]{2,1,0:T(8,128)(2,1)} %param.11, bf16[320,3584]{1,0:T(8,128)(2,1)S(1)} %copy-done.2, bf16[1,3584,512]{2,1,0:T(8,128)(2,1)} %param.10, f32[320,512]{1,0:T(8,128)S(1)} %fusion.8), kind=kOutput, calls=%fused_computation.6 | convolution fusion | flops 2349793280 | bytes 14876672 | tf_op jit(solution)/shard_map/dot_general | solution.py:44
  194.6 1.8 convert_element_type.76
  196.4 1.2 reshape.188
  197.6 3.8 %all-to-all-start.1 = ((bf16[8,20,3584]{2,1,0:T(8,128)(2,1)}), bf16[8,20,3584]{2,1,0:T(8,128)(2,1)S(1)}, u32[]{:S(2)}, u32[]{:S(2)}) async-start(bf16[8,20,3584]{2,1,0:T(8,128)(2,1)} %reshape.188), calls=%async_computation.2 | async-start | bytes 2752512 | tf_op jit(solution)/shard_map/all_to_all | solution.py:52
  201.4 4.5 %reduce-scatter.5.cloned.1.call-done = f32[160,3584]{1,0:T(8,128)} async-done(((f32[320,3584]{1,0:T(8,128)}), f32[160,3584]{1,0:T(8,128)}) %reduce-scatter.5.cloned.1.call-update) | async-done | bytes 2293776 | tf_op jit(solution)/shard_map/reduce_scatter | solution.py:43
  206.0 1.8 convert_element_type.84
  207.7 1.2 reshape.193
  209.0 25.7 %all-to-all-done.1 = bf16[8,20,3584]{2,1,0:T(8,128)(2,1)S(1)} async-done(((bf16[8,20,3584]{2,1,0:T(8,128)(2,1)}), bf16[8,20,3584]{2,1,0:T(8,128)(2,1)S(1)}, u32[]{:S(2)}, u32[]{:S(2)}) %all-to-all-start.1) | async-done | bytes 1146912 | tf_op jit(solution)/shard_map/all_to_all | solution.py:52
  234.7 4.3 %all-to-all-start.3 = ((bf16[8,20,3584]{2,1,0:T(8,128)(2,1)}), bf16[8,20,3584]{2,1,0:T(8,128)(2,1)}, u32[]{:S(2)}, u32[]{:S(2)}) async-start(bf16[8,20,3584]{2,1,0:T(8,128)(2,1)} %reshape.193), calls=%async_computation.5 | async-start | bytes 2752512 | tf_op jit(solution)/shard_map/all_to_all | solution.py:52
  239.2 0.3 reshape.189
  239.5 1.1 gather_fusion
  240.6 0.6 reshape.195
  241.2 30.5 %all-to-all-done.3 = bf16[8,20,3584]{2,1,0:T(8,128)(2,1)} async-done(((bf16[8,20,3584]{2,1,0:T(8,128)(2,1)}), bf16[8,20,3584]{2,1,0:T(8,128)(2,1)}, u32[]{:S(2)}, u32[]{:S(2)}) %all-to-all-start.3) | async-done | bytes 1146912 | tf_op jit(solution)/shard_map/all_to_all | solution.py:52
  271.7 1.4 reshape.194
  273.1 2.1 gather_fusion.1
  275.2 2.7 reshape.196
  277.9 1.2 multiply_reduce_fusion.1
  279.2 0.3 copy-done
  279.4 1.2 multiply_reduce_fusion
  280.7 0.8 pad_maximum_fusion
  (26 shorter events, 0.8 us)
Async XLA Ops:
  6.5 188.1 %reduce-scatter.3.cloned.1.call-start = ((), (), s32[]{:S(2)}) async-start(), calls=%async_computation.6 | async-start | bytes 6881280 | tf_op jit(solution)/shard_map/reduce_scatter | solution.py:43
  90.6 5.1 %copy-start.1 = (bf16[320,3584]{1,0:T(8,128)(2,1)S(1)}, bf16[320,3584]{1,0:T(8,128)(2,1)}, u32[]{:S(2)}) copy-start(bf16[320,3584]{1,0:T(8,128)(2,1)} %reshape.187) | copy-start | bytes 6881284
  103.8 102.2 %reduce-scatter.5.cloned.1.call-start = ((), (), s32[]{:S(2)}) async-start(), calls=%async_computation.7 | async-start | bytes 6881280 | tf_op jit(solution)/shard_map/reduce_scatter | solution.py:43
  182.4 4.2 %copy-start.2 = (bf16[320,3584]{1,0:T(8,128)(2,1)S(1)}, bf16[320,3584]{1,0:T(8,128)(2,1)}, u32[]{:S(2)}) copy-start(bf16[320,3584]{1,0:T(8,128)(2,1)} %reshape.192) | copy-start | bytes 6881284
  197.6 37.1 %all-to-all-start.1 = ((bf16[8,20,3584]{2,1,0:T(8,128)(2,1)}), bf16[8,20,3584]{2,1,0:T(8,128)(2,1)S(1)}, u32[]{:S(2)}, u32[]{:S(2)}) async-start(bf16[8,20,3584]{2,1,0:T(8,128)(2,1)} %reshape.188), calls=%async_computation.2 | async-start | bytes 2752512 | tf_op jit(solution)/shard_map/all_to_all | solution.py:52
  207.7 31.2 %copy-start.3 = (s32[2,32,4]{1,2,0:T(4,128)S(1)}, s32[2,32,4]{1,2,0:T(4,128)}, u32[]{:S(2)}) copy-start(s32[2,32,4]{1,2,0:T(4,128)} %param.8) | copy-start | bytes 3076
  234.7 37.0 %all-to-all-start.3 = ((bf16[8,20,3584]{2,1,0:T(8,128)(2,1)}), bf16[8,20,3584]{2,1,0:T(8,128)(2,1)}, u32[]{:S(2)}, u32[]{:S(2)}) async-start(bf16[8,20,3584]{2,1,0:T(8,128)(2,1)} %reshape.193), calls=%async_computation.5 | async-start | bytes 2752512 | tf_op jit(solution)/shard_map/all_to_all | solution.py:52
  277.9 1.5 copy-start
Sparse Core Ops, SparseCore 0:
  103.9 11.2 reduce-scatter.2
  194.7 11.2 reduce-scatter.4
where the time goes:
time: 289 us; the launch traced here: 288 us
  blocking collectives  137 us (47%)
  waiting for transfers between devices  60.8 us (21%)
  local copies, waits for them, and re-layouts  35 us (12%)
  matrix products  25.3 us (9%)
  between operations  13.7 us (5%)
  other arithmetic  8.43 us (3%)
  starting transfers between devices  8.31 us (3%)
    all_to_all x2, blocking collectives, per_device(): lax.all_to_all(copies, ('node', 'local'), split_axis=0, concat_axis=0, ti...  137 us
    all_to_all x2, waiting for transfers between devices, per_device(): lax.all_to_all(outgoing, 'node', split_axis=0, concat_axis=0, tiled=True)  56.2 us
    dot_general x2, matrix products, per_device(): jnp.dot(hidden, down_mat, preferred_element_type=jnp.float32)  16 us
    scatter x2, local copies, waits for them, and re-layouts, per_device(): send_rows = send_rows.at[place_position].set(tokens[step_index][source])  9.79 us
    dot_general x2, matrix products, per_device(): gate_act = jnp.dot(ordered, gate_mat, preferred_element_type=jnp.float32)  9.29 us
    all_to_all x2, starting transfers between devices, per_device(): lax.all_to_all(outgoing, 'node', split_axis=0, concat_axis=0, tiled=True)  8.09 us
  transfers between devices with their start and end apart: 4, of which 3 were waited for; matrix products, arithmetic and copies ran while one was open for 11% of the time, Pallas kernels for 0%

commit v1 on v0

v1 whole, which is shorter than its diff:
```python
import jax
import jax.numpy as jnp
from jax import lax
from jax.sharding import PartitionSpec as P


def ring_order(node_count, group_count):
    if group_count == 2:
        return list(range(0, node_count, 2)) + list(range(node_count - 1, 0, -2))
    return list(range(node_count))


def per_device(order, tokens, expert_ids, gate_fixed, w_gate, w_up, w_down):
    step_count, tok_rows, width = tokens.shape
    n = len(order)
    half = n // 2
    me = lax.axis_index("node")
    core = lax.axis_index("local")
    gate_mat, up_mat, down_mat = w_gate[0], w_up[0], w_down[0]

    def shift(value, distance):
        return lax.ppermute(value, "node", [(order[i], order[(i + distance) % n]) for i in range(n)])

    def swap(value):
        return lax.ppermute(value, "local", [(0, 1), (1, 0)])

    routes = jnp.stack([expert_ids, gate_fixed])
    routes = jnp.concatenate([routes.reshape(-1, 128), swap(routes.reshape(-1, 128))])
    route_from = {0: routes}
    for distance in range(1, n):
        route_from[distance] = shift(routes, distance)

    def weights_of(distance, step):
        table = route_from[distance % n].reshape(2, 2, step_count, tok_rows, -1)[:, :, step]
        hit = table[:, 0] == me
        return jnp.sum(jnp.where(hit, table[:, 1], 0), axis=-1).astype(jnp.float32) / 65536.0

    arrived = {(0, s): tokens[s] for s in range(step_count)}
    plus = {s: tokens[s] for s in range(step_count)}
    minus = dict(plus)
    for hop in range(1, half + 1):
        for s in range(step_count):
            if hop < half or s % 2 == 0:
                plus[s] = shift(plus[s], 1)
                arrived[hop, s] = plus[s]
            if hop < half or s % 2 == 1:
                minus[s] = shift(minus[s], -1)
                arrived[-hop if hop < half else hop, s] = minus[s]

    def experts(keys):
        rows = jnp.concatenate([arrived[k] for k in keys])
        other = swap(rows)
        factor = jnp.stack([weights_of(*k) for k in keys], axis=1).reshape(2, -1, 1)
        rows = jnp.concatenate([rows, other])
        factor = factor.reshape(-1, 1)
        gate_act = jnp.dot(rows, gate_mat, preferred_element_type=jnp.float32)
        up_act = jnp.dot(rows, up_mat, preferred_element_type=jnp.float32)
        hidden = (jax.nn.silu(gate_act) * up_act * factor).astype(jnp.bfloat16)
        part = jnp.dot(hidden, down_mat, preferred_element_type=jnp.float32)
        mine, theirs = jnp.split(part, 2)
        total = mine + swap(theirs.astype(jnp.bfloat16)).astype(jnp.float32)
        total = total.reshape(len(keys), tok_rows, width)
        return {k: total[i] for i, k in enumerate(keys)}

    partial = {}
    for hop in range(half + 1):
        places = [hop] if hop in (0, half) else [hop, -hop]
        partial.update(experts([(p, s) for p in places for s in range(step_count)]))

    def add(running, key):
        value = partial[key] if running is None else partial[key] + running.astype(jnp.float32)
        return value.astype(jnp.bfloat16)

    ahead = {s: None for s in range(step_count)}
    back = {s: None for s in range(step_count)}
    for hop in range(half, 0, -1):
        for s in range(step_count):
            if hop < half or s % 2 == 0:
                ahead[s] = shift(add(ahead[s], (-hop if hop < half else hop, s)), 1)
            if hop < half or s % 2 == 1:
                back[s] = shift(add(back[s], (hop, s)), -1)
    outputs = []
    for s in range(step_count):
        total = partial[0, s] + ahead[s].astype(jnp.float32) + back[s].astype(jnp.float32)
        outputs.append(total.astype(jnp.bfloat16))
    return jnp.stack(outputs)


def solution(mesh):
    order = ring_order(mesh.shape["node"], mesh.shape["groups"])
    rows = P(None, ("groups", "node", "local"), None)
    in_specs = (rows, rows, rows, P("node", None, "local"), P("node", None, "local"), P("node", "local", None))

    def call(*arrays):
        return per_device(order, *arrays)

    return jax.shard_map(call, mesh=mesh, in_specs=in_specs, out_specs=rows, check_vma=False)
```

time: 289 us -> 197 us (0.68)
  blocking collectives: 137 us -> 0 us
  starting transfers between devices: 8.31 us -> 40.9 us
  matrix products: 25.3 us -> 45.9 us
  waiting for transfers between devices: 60.8 us -> 77.3 us
  local copies, waits for them, and re-layouts: 35 us -> 20.4 us
  between operations: 13.7 us -> 0.75 us
  other arithmetic: 8.43 us -> 11.5 us
    all_to_all x2 -> x0, blocking collectives: 137 us -> none  [per_device(): lax.all_to_all(copies, ('node', 'local'), split_axis=0, concat_axis=0, ti...]
    ppermute x0 -> x46, waiting for transfers between devices: none -> 77.3 us  [the longest x35 76.1 us: shift(): lax.ppermute(value, 'node', [(order[i], order[(i + distance) % n]) for i...]
    all_to_all x2 -> x0, waiting for transfers between devices: 56.2 us -> none  [per_device(): lax.all_to_all(outgoing, 'node', split_axis=0, concat_axis=0, tiled=True)]
    ppermute x0 -> x46, starting transfers between devices: none -> 40.9 us  [the longest x35 39.4 us: shift(): lax.ppermute(value, 'node', [(order[i], order[(i + distance) % n]) for i...]
    dot_general x4 -> x10, matrix products: 25.3 us -> 45.9 us  [the longest x5 33.7 us: experts(): part = jnp.dot(hidden, down_mat, preferred_element_type=jnp.float32)]
    reshape x8 -> x9, local copies, waits for them, and re-layouts: 12.9 us -> 1.15 us  [the longest x8 1.04 us: weights_of(): route_from[distance % n].reshape(2, 2, step_count, tok_rows, -1)[:, :, step]]
    scatter x2 -> x0, local copies, waits for them, and re-layouts: 9.79 us -> none  [per_device(): send_rows = send_rows.at[place_position].set(tokens[step_index][source])]
    split x0 -> x5, local copies, waits for them, and re-layouts: none -> 8.83 us  [experts(): mine, theirs = jnp.split(part, 2)]
  transfers between devices with their start and end apart: 4 -> 46, of which waited for: 3 -> 29; matrix products, arithmetic and copies ran while one was open for 11% -> 37% of each run, Pallas kernels for 0% -> 0%
where the time goes in v1:
time: 197 us
  waiting for transfers between devices  77.3 us (39%)
  matrix products  45.9 us (23%)
  starting transfers between devices  40.9 us (21%)
  local copies, waits for them, and re-layouts  20.4 us (10%)
  other arithmetic  11.5 us (6%)
    ppermute x35, waiting for transfers between devices, shift(): lax.ppermute(value, 'node', [(order[i], order[(i + distance) % n]) for i...  76.1 us
    ppermute x35, starting transfers between devices, shift(): lax.ppermute(value, 'node', [(order[i], order[(i + distance) % n]) for i...  39.4 us
    dot_general x5, matrix products, experts(): part = jnp.dot(hidden, down_mat, preferred_element_type=jnp.float32)  33.7 us
    dot_general x5, matrix products, experts(): up_act = jnp.dot(rows, up_mat, preferred_element_type=jnp.float32)  12.3 us
    split x5, local copies, waits for them, and re-layouts, experts(): mine, theirs = jnp.split(part, 2)  8.83 us
    concatenate x4, local copies, waits for them, and re-layouts, experts(): rows = jnp.concatenate([rows, other])  5.71 us
  transfers between devices with their start and end apart: 46, of which 29 were waited for; matrix products, arithmetic and copies ran while one was open for 37% of the time, Pallas kernels for 0%

profile of v1, /device:TPU:0, one launch (start us, length us, event | category | flops | bytes accessed | tf_op | source)
XLA Modules:
  0.0 196.8 jit_solution(15280269240848810523)
XLA Ops:
  1.1 3.1 %collective-permute-start.3 = (bf16[32,3584]{1,0:T(8,128)(2,1)S(1)}, bf16[32,3584]{1,0:T(8,128)(2,1)S(1)}, u32[]{:S(2)}, u32[]{:S(2)}) collective-permute-start(bf16[32,3584]{1,0:T(8,128)(2,1)S(1)} %get-tuple-element.24), channel_id=1, source_target_pairs={{0,4},{4,8},{8,12},{12,14},{14,10},{10,6},{6,2},{2,0},{1,5},{5,9},... | collective-permute-start | bytes 688136 | tf_op jit(solution)/shard_map/ppermute | solution.py:22
  4.2 2.0 %collective-permute-start.4 = (bf16[32,3584]{1,0:T(8,128)(2,1)S(1)}, bf16[32,3584]{1,0:T(8,128)(2,1)S(1)}, u32[]{:S(2)}, u32[]{:S(2)}) collective-permute-start(bf16[32,3584]{1,0:T(8,128)(2,1)S(1)} %get-tuple-element.23), channel_id=1, source_target_pairs={{0,4},{4,8},{8,12},{12,14},{14,10},{10,6},{6,2},{2,0},{1,5},{5,9},... | collective-permute-start | bytes 688136 | tf_op jit(solution)/shard_map/ppermute | solution.py:22
  8.3 4.0 %collective-permute-start.25 = (s32[8,128]{1,0:T(8,128)S(1)}, s32[8,128]{1,0:T(8,128)S(1)}, u32[]{:S(2)}, u32[]{:S(2)}) collective-permute-start(s32[8,128]{1,0:T(8,128)S(1)} %pad_add_fusion.1), channel_id=1, source_target_pairs={{0,10},{4,6},{8,2},{12,0},{14,4},{10,8},{6,12},{2,14},{1,11},{5,7}... | collective-permute-start | bytes 12296 | tf_op jit(solution)/shard_map/ppermute | solution.py:22
  12.8 5.5 %collective-permute-done.25 = s32[8,128]{1,0:T(8,128)S(1)} collective-permute-done((s32[8,128]{1,0:T(8,128)S(1)}, s32[8,128]{1,0:T(8,128)S(1)}, u32[]{:S(2)}, u32[]{:S(2)}) %collective-permute-start.25) | collective-permute-done | bytes 4128 | tf_op jit(solution)/shard_map/ppermute | solution.py:22
  20.1 3.6 %collective-permute-done.24 = s32[8,128]{1,0:T(8,128)S(1)} collective-permute-done((s32[8,128]{1,0:T(8,128)S(1)}, s32[8,128]{1,0:T(8,128)S(1)}, u32[]{:S(2)}, u32[]{:S(2)}) %collective-permute-start.24) | collective-permute-done | bytes 4128 | tf_op jit(solution)/shard_map/ppermute | solution.py:22
  25.3 4.7 %collective-permute-done.30 = s32[8,128]{1,0:T(8,128)S(1)} collective-permute-done((s32[8,128]{1,0:T(8,128)S(1)}, s32[8,128]{1,0:T(8,128)S(1)}, u32[]{:S(2)}, u32[]{:S(2)}) %collective-permute-start.30) | collective-permute-done | bytes 4128 | tf_op jit(solution)/shard_map/ppermute | solution.py:22
  30.3 4.2 %collective-permute-done.17 = s32[8,128]{1,0:T(8,128)S(1)} collective-permute-done((s32[8,128]{1,0:T(8,128)S(1)}, s32[8,128]{1,0:T(8,128)S(1)}, u32[]{:S(2)}, u32[]{:S(2)}) %collective-permute-start.17) | collective-permute-done | bytes 4128 | tf_op jit(solution)/shard_map/ppermute | solution.py:22
  34.8 4.2 %collective-permute-done.16 = s32[8,128]{1,0:T(8,128)S(1)} collective-permute-done((s32[8,128]{1,0:T(8,128)S(1)}, s32[8,128]{1,0:T(8,128)S(1)}, u32[]{:S(2)}, u32[]{:S(2)}) %collective-permute-start.16) | collective-permute-done | bytes 4128 | tf_op jit(solution)/shard_map/ppermute | solution.py:22
  39.8 2.8 %collective-permute-done.9 = s32[8,128]{1,0:T(8,128)S(1)} collective-permute-done((s32[8,128]{1,0:T(8,128)S(1)}, s32[8,128]{1,0:T(8,128)S(1)}, u32[]{:S(2)}, u32[]{:S(2)}) %collective-permute-start.9) | collective-permute-done | bytes 4128 | tf_op jit(solution)/shard_map/ppermute | solution.py:22
  43.2 3.0 %collective-permute-done.8 = s32[8,128]{1,0:T(8,128)S(1)} collective-permute-done((s32[8,128]{1,0:T(8,128)S(1)}, s32[8,128]{1,0:T(8,128)S(1)}, u32[]{:S(2)}, u32[]{:S(2)}) %collective-permute-start.8) | collective-permute-done | bytes 4128 | tf_op jit(solution)/shard_map/ppermute | solution.py:22
  48.8 2.0 %collective-permute-start.14 = (bf16[32,3584]{1,0:T(8,128)(2,1)S(1)}, bf16[32,3584]{1,0:T(8,128)(2,1)S(1)}, u32[]{:S(2)}, u32[]{:S(2)}) collective-permute-start(bf16[32,3584]{1,0:T(8,128)(2,1)S(1)} %collective-permute-done.6), channel_id=1, source_target_pairs={{0,2},{4,0},{8,4},{12,8},{14,12},{10,14},{6,10},{2,6},{1,3},{5,1},... | collective-permute-start | bytes 688136 | tf_op jit(solution)/shard_map/ppermute | solution.py:22
  51.9 3.2 %collective-permute-done.11 = bf16[32,3584]{1,0:T(8,128)(2,1)S(1)} collective-permute-done((bf16[32,3584]{1,0:T(8,128)(2,1)S(1)}, bf16[32,3584]{1,0:T(8,128)(2,1)S(1)}, u32[]{:S(2)}, u32[]{:S(2)}) %collective-permute-start.11) | collective-permute-done | bytes 229408 | tf_op jit(solution)/shard_map/ppermute | solution.py:22
  55.0 4.5 %collective-permute-done.12 = bf16[32,3584]{1,0:T(8,128)(2,1)S(1)} collective-permute-done((bf16[32,3584]{1,0:T(8,128)(2,1)S(1)}, bf16[32,3584]{1,0:T(8,128)(2,1)S(1)}, u32[]{:S(2)}, u32[]{:S(2)}) %collective-permute-start.12) | collective-permute-done | bytes 229408 | tf_op jit(solution)/shard_map/ppermute | solution.py:22
  60.9 1.7 fusion.18
  62.6 4.6 %fusion.8 = f32[128,3584]{1,0:T(8,128)S(1)} fusion(bf16[1,512,3584]{2,1,0:T(8,128)(2,1)} %param.11, f32[128,512]{1,0:T(8,128)S(1)} %fusion.18, bf16[1,3584,512]{2,1,0:T(8,128)(2,1)} %param.9, bf16[64,3584]{1,0:T(8,128)(2,1)} %collective-permute-done, bf16[32,3584]{1,0:T(8,128)(2,1)S(1)} %get-tuple-element.23, bf16[32,3584]{1,0:T(8,128)(2,1)S(1)} %get-tuple-element.24, ...), kind=kOutput, calls=%fused_computation.8 | convolution fusion | flops 942735360 | bytes 10355200 | tf_op jit(solution)/shard_map/dot_general | solution.py:59
  68.5 1.8 collective-permute-start.19
  70.7 6.2 %collective-permute-done.19 = bf16[32,3584]{1,0:T(8,128)(2,1)S(1)} collective-permute-done((bf16[32,3584]{1,0:T(8,128)(2,1)S(1)}, bf16[32,3584]{1,0:T(8,128)(2,1)S(1)}, u32[]{:S(2)}, u32[]{:S(2)}) %collective-permute-start.19) | collective-permute-done | bytes 229408 | tf_op jit(solution)/shard_map/ppermute | solution.py:22
  76.9 1.5 collective-permute-start.21
  78.4 2.4 %collective-permute-done.20 = bf16[32,3584]{1,0:T(8,128)(2,1)S(1)} collective-permute-done((bf16[32,3584]{1,0:T(8,128)(2,1)S(1)}, bf16[32,3584]{1,0:T(8,128)(2,1)S(1)}, u32[]{:S(2)}, u32[]{:S(2)}) %collective-permute-start.20) | collective-permute-done | bytes 229408 | tf_op jit(solution)/shard_map/ppermute | solution.py:22
  80.9 1.5 collective-permute-start.22
  83.2 1.8 collective-permute-start.27
  85.0 2.9 %collective-permute-done.22 = bf16[32,3584]{1,0:T(8,128)(2,1)S(1)} collective-permute-done((bf16[32,3584]{1,0:T(8,128)(2,1)S(1)}, bf16[32,3584]{1,0:T(8,128)(2,1)S(1)}, u32[]{:S(2)}, u32[]{:S(2)}) %collective-permute-start.22) | collective-permute-done | bytes 229408 | tf_op jit(solution)/shard_map/ppermute | solution.py:22
  87.9 1.5 collective-permute-start.28
  90.5 3.4 %collective-permute-done.28 = bf16[32,3584]{1,0:T(8,128)(2,1)S(1)} collective-permute-done((bf16[32,3584]{1,0:T(8,128)(2,1)S(1)}, bf16[32,3584]{1,0:T(8,128)(2,1)S(1)}, u32[]{:S(2)}, u32[]{:S(2)}) %collective-permute-start.28) | collective-permute-done | bytes 229408 | tf_op jit(solution)/shard_map/ppermute | solution.py:22
  98.5 7.7 %fusion.6 = f32[256,3584]{1,0:T(8,128)} fusion(bf16[1,512,3584]{2,1,0:T(8,128)(2,1)} %param.11, f32[256,512]{1,0:T(8,128)S(1)} %fusion.16, bf16[256,3584]{1,0:T(8,128)(2,1)} %copy-done.7, bf16[1,3584,512]{2,1,0:T(8,128)(2,1)} %param.9, f32[256]{0:T(256)S(1)} %mul.89), kind=kOutput, calls=%fused_computation.6 | convolution fusion | flops 1879965696 | bytes 13370368 | tf_op jit(solution)/shard_map/dot_general | solution.py:59
  106.2 2.6 %split.69 = bf16[128,3584]{1,0:T(8,128)(2,1)} slice(f32[256,3584]{1,0:T(8,128)} %fusion.6), slice={[128:256], [0:3584]} | slice | bytes 1835008 | tf_op jit(solution)/shard_map/split | solution.py:60
  109.8 2.7 %fusion.10 = f32[128,512]{1,0:T(8,128)S(1)} fusion(bf16[128,3584]{1,0:T(8,128)(2,1)S(1)} %constant_dynamic-update-slice_fusion.15, bf16[1,3584,512]{2,1,0:T(8,128)(2,1)} %param.10), kind=kOutput, calls=%fused_computation.10 | convolution fusion | flops 469762048 | bytes 4849664 | tf_op jit(solution)/shard_map/dot_general | solution.py:57
  112.5 5.8 %fusion = f32[128,3584]{1,0:T(8,128)} fusion(bf16[1,512,3584]{2,1,0:T(8,128)(2,1)} %param.11, f32[128,512]{1,0:T(8,128)S(1)} %fusion.10, bf16[128,3584]{1,0:T(8,128)(2,1)S(1)} %constant_dynamic-update-slice_fusion.15, bf16[1,3584,512]{2,1,0:T(8,128)(2,1)} %param.9, f32[128]{0:T(128)S(1)} %mul.104), kind=kOutput, calls=%fused_computation | convolution fusion | flops 939982848 | bytes 10355200 | tf_op jit(solution)/shard_map/dot_general | solution.py:59
  118.2 2.0 %split.70 = bf16[64,3584]{1,0:T(8,128)(2,1)} slice(f32[128,3584]{1,0:T(8,128)} %fusion), slice={[64:128], [0:3584]} | slice | bytes 917504 | tf_op jit(solution)/shard_map/split | solution.py:60
  120.7 2.2 %constant_dynamic-update-slice_fusion.5 = bf16[256,3584]{1,0:T(8,128)(2,1)} fusion(bf16[256,3584]{1,0:T(8,128)(2,1)} %copy-done.11, bf16[128,3584]{1,0:T(8,128)(2,1)} %collective-permute-done.15), kind=kLoop, calls=%fused_computation.114 | loop fusion | bytes 1835008 | tf_op jit(solution)/shard_map/concatenate | solution.py:54
  122.9 3.7 %fusion.14 = f32[256,512]{1,0:T(8,128)S(1)} fusion(bf16[256,3584]{1,0:T(8,128)(2,1)} %constant_dynamic-update-slice_fusion.5, bf16[1,3584,512]{2,1,0:T(8,128)(2,1)} %param.10), kind=kOutput, calls=%fused_computation.14 | convolution fusion | flops 939524096 | bytes 6029312 | tf_op jit(solution)/shard_map/dot_general | solution.py:57
  126.6 7.7 %fusion.4 = f32[256,3584]{1,0:T(8,128)} fusion(bf16[1,512,3584]{2,1,0:T(8,128)(2,1)} %param.11, f32[256,512]{1,0:T(8,128)S(1)} %fusion.14, bf16[256,3584]{1,0:T(8,128)(2,1)} %constant_dynamic-update-slice_fusion.5, bf16[1,3584,512]{2,1,0:T(8,128)(2,1)} %param.9, f32[256]{0:T(256)S(1)} %mul.94), kind=kOutput, calls=%fused_computation.4 | convolution fusion | flops 1879965696 | bytes 13370368 | tf_op jit(solution)/shard_map/dot_general | solution.py:59
  134.4 1.7 split.68
  138.9 3.1 %fusion.12 = f32[256,512]{1,0:T(8,128)S(1)} fusion(bf16[256,3584]{1,0:T(8,128)(2,1)S(1)} %constant_dynamic-update-slice_fusion.10, bf16[1,3584,512]{2,1,0:T(8,128)(2,1)} %param.10), kind=kOutput, calls=%fused_computation.12 | convolution fusion | flops 939524096 | bytes 6029312 | tf_op jit(solution)/shard_map/dot_general | solution.py:57
  142.0 7.9 %fusion.2 = f32[256,3584]{1,0:T(8,128)} fusion(bf16[1,512,3584]{2,1,0:T(8,128)(2,1)} %param.11, f32[256,512]{1,0:T(8,128)S(1)} %fusion.12, bf16[256,3584]{1,0:T(8,128)(2,1)} %copy-done.10, bf16[1,3584,512]{2,1,0:T(8,128)(2,1)} %param.9, f32[256]{0:T(256)S(1)} %mul.99), kind=kOutput, calls=%fused_computation.2 | convolution fusion | flops 1879965696 | bytes 13370368 | tf_op jit(solution)/shard_map/dot_general | solution.py:59
  149.9 1.7 split.67
  153.4 1.8 collective-permute-start.32
  155.7 5.5 %collective-permute-done.32 = bf16[32,3584]{1,0:T(8,128)(2,1)S(1)} collective-permute-done((bf16[32,3584]{1,0:T(8,128)(2,1)S(1)}, bf16[32,3584]{1,0:T(8,128)(2,1)S(1)}, u32[]{:S(2)}, u32[]{:S(2)}) %collective-permute-start.32) | collective-permute-done | bytes 229408 | tf_op jit(solution)/shard_map/ppermute | solution.py:22
  163.1 1.7 collective-permute-start.43
  165.2 1.7 collective-permute-start.39
  168.3 3.0 %collective-permute-done.33 = bf16[32,3584]{1,0:T(8,128)(2,1)S(1)} collective-permute-done((bf16[32,3584]{1,0:T(8,128)(2,1)S(1)}, bf16[32,3584]{1,0:T(8,128)(2,1)S(1)}, u32[]{:S(2)}, u32[]{:S(2)}) %collective-permute-start.33) | collective-permute-done | bytes 229408 | tf_op jit(solution)/shard_map/ppermute | solution.py:22
  171.7 3.0 %collective-permute-done.36 = bf16[32,3584]{1,0:T(8,128)(2,1)S(1)} collective-permute-done((bf16[32,3584]{1,0:T(8,128)(2,1)S(1)}, bf16[32,3584]{1,0:T(8,128)(2,1)S(1)}, u32[]{:S(2)}, u32[]{:S(2)}) %collective-permute-start.36) | collective-permute-done | bytes 229408 | tf_op jit(solution)/shard_map/ppermute | solution.py:22
  175.2 1.7 collective-permute-start.37
  177.2 1.7 collective-permute-start.44
  179.1 3.9 %collective-permute-done.34 = bf16[32,3584]{1,0:T(8,128)(2,1)S(1)} collective-permute-done((bf16[32,3584]{1,0:T(8,128)(2,1)S(1)}, bf16[32,3584]{1,0:T(8,128)(2,1)S(1)}, u32[]{:S(2)}, u32[]{:S(2)}) %collective-permute-start.34) | collective-permute-done | bytes 229408 | tf_op jit(solution)/shard_map/ppermute | solution.py:22
  183.3 2.2 %collective-permute-done.40 = bf16[32,3584]{1,0:T(8,128)(2,1)S(1)} collective-permute-done((bf16[32,3584]{1,0:T(8,128)(2,1)S(1)}, bf16[32,3584]{1,0:T(8,128)(2,1)S(1)}, u32[]{:S(2)}, u32[]{:S(2)}) %collective-permute-start.40) | collective-permute-done | bytes 229408 | tf_op jit(solution)/shard_map/ppermute | solution.py:22
  191.1 2.0 collective-permute-done.35
  193.3 2.2 %collective-permute-done.41 = bf16[32,3584]{1,0:T(8,128)(2,1)S(1)} collective-permute-done((bf16[32,3584]{1,0:T(8,128)(2,1)S(1)}, bf16[32,3584]{1,0:T(8,128)(2,1)S(1)}, u32[]{:S(2)}, u32[]{:S(2)}) %collective-permute-start.41) | collective-permute-done | bytes 229408 | tf_op jit(solution)/shard_map/ppermute | solution.py:22
  (180 shorter events, 41.2 us)
Async XLA Ops:
  1.1 45.6 %collective-permute-start.3 = (bf16[32,3584]{1,0:T(8,128)(2,1)S(1)}, bf16[32,3584]{1,0:T(8,128)(2,1)S(1)}, u32[]{:S(2)}, u32[]{:S(2)}) collective-permute-start(bf16[32,3584]{1,0:T(8,128)(2,1)S(1)} %get-tuple-element.24), channel_id=1, source_target_pairs={{0,4},{4,8},{8,12},{12,14},{14,10},{10,6},{6,2},{2,0},{1,5},{5,9},... | collective-permute-start | bytes 688136 | tf_op jit(solution)/shard_map/ppermute | solution.py:22
  4.2 43.1 %collective-permute-start.5 = (bf16[32,3584]{1,0:T(8,128)(2,1)S(1)}, bf16[32,3584]{1,0:T(8,128)(2,1)S(1)}, u32[]{:S(2)}, u32[]{:S(2)}) collective-permute-start(bf16[32,3584]{1,0:T(8,128)(2,1)S(1)} %get-tuple-element.24), channel_id=1, source_target_pairs={{0,2},{4,0},{8,4},{12,8},{14,12},{10,14},{6,10},{2,6},{1,3},{5,1},... | collective-permute-start | bytes 688136 | tf_op jit(solution)/shard_map/ppermute | solution.py:22
  4.2 42.5 %collective-permute-start.4 = (bf16[32,3584]{1,0:T(8,128)(2,1)S(1)}, bf16[32,3584]{1,0:T(8,128)(2,1)S(1)}, u32[]{:S(2)}, u32[]{:S(2)}) collective-permute-start(bf16[32,3584]{1,0:T(8,128)(2,1)S(1)} %get-tuple-element.23), channel_id=1, source_target_pairs={{0,4},{4,8},{8,12},{12,14},{14,10},{10,6},{6,2},{2,0},{1,5},{5,9},... | collective-permute-start | bytes 688136 | tf_op jit(solution)/shard_map/ppermute | solution.py:22
  6.2 42.6 %collective-permute-start.6 = (bf16[32,3584]{1,0:T(8,128)(2,1)S(1)}, bf16[32,3584]{1,0:T(8,128)(2,1)S(1)}, u32[]{:S(2)}, u32[]{:S(2)}) collective-permute-start(bf16[32,3584]{1,0:T(8,128)(2,1)S(1)} %get-tuple-element.23), channel_id=1, source_target_pairs={{0,2},{4,0},{8,4},{12,8},{14,12},{10,14},{6,10},{2,6},{1,3},{5,1},... | collective-permute-start | bytes 688136 | tf_op jit(solution)/shard_map/ppermute | solution.py:22
  7.1 1.2 collective-permute-start.1
  8.3 9.9 %collective-permute-start.25 = (s32[8,128]{1,0:T(8,128)S(1)}, s32[8,128]{1,0:T(8,128)S(1)}, u32[]{:S(2)}, u32[]{:S(2)}) collective-permute-start(s32[8,128]{1,0:T(8,128)S(1)} %pad_add_fusion.1), channel_id=1, source_target_pairs={{0,10},{4,6},{8,2},{12,0},{14,4},{10,8},{6,12},{2,14},{1,11},{5,7}... | collective-permute-start | bytes 12296 | tf_op jit(solution)/shard_map/ppermute | solution.py:22
  18.3 5.4 %collective-permute-start.24 = (s32[8,128]{1,0:T(8,128)S(1)}, s32[8,128]{1,0:T(8,128)S(1)}, u32[]{:S(2)}, u32[]{:S(2)}) collective-permute-start(s32[8,128]{1,0:T(8,128)S(1)} %pad_add_fusion.1), channel_id=1, source_target_pairs={{0,12},{4,14},{8,10},{12,6},{14,2},{10,0},{6,4},{2,8},{1,13},{5,15... | collective-permute-start | bytes 12296 | tf_op jit(solution)/shard_map/ppermute | solution.py:22
  23.7 6.3 %collective-permute-start.30 = (s32[8,128]{1,0:T(8,128)S(1)}, s32[8,128]{1,0:T(8,128)S(1)}, u32[]{:S(2)}, u32[]{:S(2)}) collective-permute-start(s32[8,128]{1,0:T(8,128)S(1)} %pad_add_fusion.1), channel_id=1, source_target_pairs={{0,14},{4,10},{8,6},{12,2},{14,0},{10,4},{6,8},{2,12},{1,15},{5,11... | collective-permute-start | bytes 12296 | tf_op jit(solution)/shard_map/ppermute | solution.py:22
  30.0 4.5 %collective-permute-start.17 = (s32[8,128]{1,0:T(8,128)S(1)}, s32[8,128]{1,0:T(8,128)S(1)}, u32[]{:S(2)}, u32[]{:S(2)}) collective-permute-start(s32[8,128]{1,0:T(8,128)S(1)} %pad_add_fusion.1), channel_id=1, source_target_pairs={{0,6},{4,2},{8,0},{12,4},{14,8},{10,12},{6,14},{2,10},{1,7},{5,3},... | collective-permute-start | bytes 12296 | tf_op jit(solution)/shard_map/ppermute | solution.py:22
  34.5 4.5 %collective-permute-start.16 = (s32[8,128]{1,0:T(8,128)S(1)}, s32[8,128]{1,0:T(8,128)S(1)}, u32[]{:S(2)}, u32[]{:S(2)}) collective-permute-start(s32[8,128]{1,0:T(8,128)S(1)} %pad_add_fusion.1), channel_id=1, source_target_pairs={{0,8},{4,12},{8,14},{12,10},{14,6},{10,2},{6,0},{2,4},{1,9},{5,13}... | collective-permute-start | bytes 12296 | tf_op jit(solution)/shard_map/ppermute | solution.py:22
  39.0 3.6 %collective-permute-start.9 = (s32[8,128]{1,0:T(8,128)S(1)}, s32[8,128]{1,0:T(8,128)S(1)}, u32[]{:S(2)}, u32[]{:S(2)}) collective-permute-start(s32[8,128]{1,0:T(8,128)S(1)} %pad_add_fusion.1), channel_id=1, source_target_pairs={{0,2},{4,0},{8,4},{12,8},{14,12},{10,14},{6,10},{2,6},{1,3},{5,1},... | collective-permute-start | bytes 12296 | tf_op jit(solution)/shard_map/ppermute | solution.py:22
  42.6 3.6 %collective-permute-start.8 = (s32[8,128]{1,0:T(8,128)S(1)}, s32[8,128]{1,0:T(8,128)S(1)}, u32[]{:S(2)}, u32[]{:S(2)}) collective-permute-start(s32[8,128]{1,0:T(8,128)S(1)} %pad_add_fusion.1), channel_id=1, source_target_pairs={{0,4},{4,8},{8,12},{12,14},{14,10},{10,6},{6,2},{2,0},{1,5},{5,9},... | collective-permute-start | bytes 12296 | tf_op jit(solution)/shard_map/ppermute | solution.py:22
  46.2 14.7 %collective-permute-start = (bf16[64,3584]{1,0:T(8,128)(2,1)S(1)}, bf16[64,3584]{1,0:T(8,128)(2,1)}, u32[]{:S(2)}, u32[]{:S(2)}) collective-permute-start(bf16[64,3584]{1,0:T(8,128)(2,1)S(1)} %pad_maximum_fusion.4), channel_id=1, source_target_pairs={{0,1},{1,0},{2,3},{3,2},{4,5},{5,4},{6,7},{7,6},{8,9},{9,8},{10,11... | collective-permute-start | bytes 1376264 | tf_op jit(solution)/shard_map/ppermute | solution.py:25
  46.6 8.4 %collective-permute-start.11 = (bf16[32,3584]{1,0:T(8,128)(2,1)S(1)}, bf16[32,3584]{1,0:T(8,128)(2,1)S(1)}, u32[]{:S(2)}, u32[]{:S(2)}) collective-permute-start(bf16[32,3584]{1,0:T(8,128)(2,1)S(1)} %collective-permute-done.3), channel_id=1, source_target_pairs={{0,4},{4,8},{8,12},{12,14},{14,10},{10,6},{6,2},{2,0},{1,5},{5,9},... | collective-permute-start | bytes 688136 | tf_op jit(solution)/shard_map/ppermute | solution.py:22
  46.7 12.9 %collective-permute-start.12 = (bf16[32,3584]{1,0:T(8,128)(2,1)S(1)}, bf16[32,3584]{1,0:T(8,128)(2,1)S(1)}, u32[]{:S(2)}, u32[]{:S(2)}) collective-permute-start(bf16[32,3584]{1,0:T(8,128)(2,1)S(1)} %collective-permute-done.4), channel_id=1, source_target_pairs={{0,4},{4,8},{8,12},{12,14},{14,10},{10,6},{6,2},{2,0},{1,5},{5,9},... | collective-permute-start | bytes 688136 | tf_op jit(solution)/shard_map/ppermute | solution.py:22
  47.2 12.3 %collective-permute-start.13 = (bf16[32,3584]{1,0:T(8,128)(2,1)S(1)}, bf16[32,3584]{1,0:T(8,128)(2,1)S(1)}, u32[]{:S(2)}, u32[]{:S(2)}) collective-permute-start(bf16[32,3584]{1,0:T(8,128)(2,1)S(1)} %collective-permute-done.5), channel_id=1, source_target_pairs={{0,2},{4,0},{8,4},{12,8},{14,12},{10,14},{6,10},{2,6},{1,3},{5,1},... | collective-permute-start | bytes 688136 | tf_op jit(solution)/shard_map/ppermute | solution.py:22
  48.8 11.1 %collective-permute-start.14 = (bf16[32,3584]{1,0:T(8,128)(2,1)S(1)}, bf16[32,3584]{1,0:T(8,128)(2,1)S(1)}, u32[]{:S(2)}, u32[]{:S(2)}) collective-permute-start(bf16[32,3584]{1,0:T(8,128)(2,1)S(1)} %collective-permute-done.6), channel_id=1, source_target_pairs={{0,2},{4,0},{8,4},{12,8},{14,12},{10,14},{6,10},{2,6},{1,3},{5,1},... | collective-permute-start | bytes 688136 | tf_op jit(solution)/shard_map/ppermute | solution.py:22
  55.0 39.8 %collective-permute-start.7 = (bf16[128,3584]{1,0:T(8,128)(2,1)}, bf16[128,3584]{1,0:T(8,128)(2,1)}, u32[]{:S(2)}, u32[]{:S(2)}) collective-permute-start(bf16[128,3584]{1,0:T(8,128)(2,1)} %pad_maximum_fusion.1), channel_id=1, source_target_pairs={{0,1},{1,0},{2,3},{3,2},{4,5},{5,4},{6,7},{7,6},{8,9},{9,8},{10,11... | collective-permute-start | bytes 2752520 | tf_op jit(solution)/shard_map/ppermute | solution.py:25
  60.9 59.9 %collective-permute-start.15 = (bf16[128,3584]{1,0:T(8,128)(2,1)}, bf16[128,3584]{1,0:T(8,128)(2,1)}, u32[]{:S(2)}, u32[]{:S(2)}) collective-permute-start(bf16[128,3584]{1,0:T(8,128)(2,1)} %pad_maximum_fusion.2), channel_id=1, source_target_pairs={{0,1},{1,0},{2,3},{3,2},{4,5},{5,4},{6,7},{7,6},{8,9},{9,8},{10,11... | collective-permute-start | bytes 2752520 | tf_op jit(solution)/shard_map/ppermute | solution.py:25
  68.0 122.0 %collective-permute-start.2 = (bf16[64,3584]{1,0:T(8,128)(2,1)}, bf16[64,3584]{1,0:T(8,128)(2,1)}, u32[]{:S(2)}, u32[]{:S(2)}) collective-permute-start(bf16[64,3584]{1,0:T(8,128)(2,1)} %split.71), channel_id=1, source_target_pairs={{0,1},{1,0},{2,3},{3,2},{4,5},{5,4},{6,7},{7,6},{8,9},{9,8},{10,11... | collective-permute-start | bytes 1376264 | tf_op jit(solution)/shard_map/ppermute | solution.py:25
  68.5 8.5 %collective-permute-start.19 = (bf16[32,3584]{1,0:T(8,128)(2,1)S(1)}, bf16[32,3584]{1,0:T(8,128)(2,1)S(1)}, u32[]{:S(2)}, u32[]{:S(2)}) collective-permute-start(bf16[32,3584]{1,0:T(8,128)(2,1)S(1)} %collective-permute-done.11), channel_id=1, source_target_pairs={{0,4},{4,8},{8,12},{12,14},{14,10},{10,6},{6,2},{2,0},{1,5},{5,9},... | collective-permute-start | bytes 688136 | tf_op jit(solution)/shard_map/ppermute | solution.py:22
  70.2 10.7 %collective-permute-start.20 = (bf16[32,3584]{1,0:T(8,128)(2,1)S(1)}, bf16[32,3584]{1,0:T(8,128)(2,1)S(1)}, u32[]{:S(2)}, u32[]{:S(2)}) collective-permute-start(bf16[32,3584]{1,0:T(8,128)(2,1)S(1)} %collective-permute-done.12), channel_id=1, source_target_pairs={{0,4},{4,8},{8,12},{12,14},{14,10},{10,6},{6,2},{2,0},{1,5},{5,9},... | collective-permute-start | bytes 688136 | tf_op jit(solution)/shard_map/ppermute | solution.py:22
  70.7 17.2 %copy-start.11 = (bf16[256,3584]{1,0:T(8,128)(2,1)}, bf16[256,3584]{1,0:T(8,128)(2,1)S(1)}, u32[]{:S(2)}) copy-start(bf16[256,3584]{1,0:T(8,128)(2,1)S(1)} %constant_dynamic-update-slice_fusion.6) | copy-start | bytes 5505028
  76.9 6.3 %collective-permute-start.21 = (bf16[32,3584]{1,0:T(8,128)(2,1)S(1)}, bf16[32,3584]{1,0:T(8,128)(2,1)S(1)}, u32[]{:S(2)}, u32[]{:S(2)}) collective-permute-start(bf16[32,3584]{1,0:T(8,128)(2,1)S(1)} %collective-permute-done.13), channel_id=1, source_target_pairs={{0,2},{4,0},{8,4},{12,8},{14,12},{10,14},{6,10},{2,6},{1,3},{5,1},... | collective-permute-start | bytes 688136 | tf_op jit(solution)/shard_map/ppermute | solution.py:22
  80.9 7.0 %collective-permute-start.22 = (bf16[32,3584]{1,0:T(8,128)(2,1)S(1)}, bf16[32,3584]{1,0:T(8,128)(2,1)S(1)}, u32[]{:S(2)}, u32[]{:S(2)}) collective-permute-start(bf16[32,3584]{1,0:T(8,128)(2,1)S(1)} %collective-permute-done.14), channel_id=1, source_target_pairs={{0,2},{4,0},{8,4},{12,8},{14,12},{10,14},{6,10},{2,6},{1,3},{5,1},... | collective-permute-start | bytes 688136 | tf_op jit(solution)/shard_map/ppermute | solution.py:22
  83.2 7.3 %collective-permute-start.27 = (bf16[32,3584]{1,0:T(8,128)(2,1)S(1)}, bf16[32,3584]{1,0:T(8,128)(2,1)S(1)}, u32[]{:S(2)}, u32[]{:S(2)}) collective-permute-start(bf16[32,3584]{1,0:T(8,128)(2,1)S(1)} %collective-permute-done.19), channel_id=1, source_target_pairs={{0,4},{4,8},{8,12},{12,14},{14,10},{10,6},{6,2},{2,0},{1,5},{5,9},... | collective-permute-start | bytes 688136 | tf_op jit(solution)/shard_map/ppermute | solution.py:22
  87.9 6.1 %collective-permute-start.28 = (bf16[32,3584]{1,0:T(8,128)(2,1)S(1)}, bf16[32,3584]{1,0:T(8,128)(2,1)S(1)}, u32[]{:S(2)}, u32[]{:S(2)}) collective-permute-start(bf16[32,3584]{1,0:T(8,128)(2,1)S(1)} %collective-permute-done.22), channel_id=1, source_target_pairs={{0,2},{4,0},{8,4},{12,8},{14,12},{10,14},{6,10},{2,6},{1,3},{5,1},... | collective-permute-start | bytes 688136 | tf_op jit(solution)/shard_map/ppermute | solution.py:22
  90.4 45.7 %collective-permute-start.23 = (bf16[128,3584]{1,0:T(8,128)(2,1)}, bf16[128,3584]{1,0:T(8,128)(2,1)}, u32[]{:S(2)}, u32[]{:S(2)}) collective-permute-start(bf16[128,3584]{1,0:T(8,128)(2,1)} %pad_maximum_fusion.3), channel_id=1, source_target_pairs={{0,1},{1,0},{2,3},{3,2},{4,5},{5,4},{6,7},{7,6},{8,9},{9,8},{10,11... | collective-permute-start | bytes 2752520 | tf_op jit(solution)/shard_map/ppermute | solution.py:25
  94.7 14.0 %collective-permute-start.29 = (bf16[64,3584]{1,0:T(8,128)(2,1)}, bf16[64,3584]{1,0:T(8,128)(2,1)}, u32[]{:S(2)}, u32[]{:S(2)}) collective-permute-start(bf16[64,3584]{1,0:T(8,128)(2,1)} %pad_maximum_fusion.5), channel_id=1, source_target_pairs={{0,1},{1,0},{2,3},{3,2},{4,5},{5,4},{6,7},{7,6},{8,9},{9,8},{10,11... | collective-permute-start | bytes 1376264 | tf_op jit(solution)/shard_map/ppermute | solution.py:25
  120.2 31.7 %collective-permute-start.31 = (bf16[64,3584]{1,0:T(8,128)(2,1)}, bf16[64,3584]{1,0:T(8,128)(2,1)}, u32[]{:S(2)}, u32[]{:S(2)}) collective-permute-start(bf16[64,3584]{1,0:T(8,128)(2,1)} %split.70), channel_id=1, source_target_pairs={{0,1},{1,0},{2,3},{3,2},{4,5},{5,4},{6,7},{7,6},{8,9},{9,8},{10,11... | collective-permute-start | bytes 1376264 | tf_op jit(solution)/shard_map/ppermute | solution.py:25
  136.1 29.1 %collective-permute-start.18 = (bf16[128,3584]{1,0:T(8,128)(2,1)S(1)}, bf16[128,3584]{1,0:T(8,128)(2,1)}, u32[]{:S(2)}, u32[]{:S(2)}) collective-permute-start(bf16[128,3584]{1,0:T(8,128)(2,1)S(1)} %split.68), channel_id=1, source_target_pairs={{0,1},{1,0},{2,3},{3,2},{4,5},{5,4},{6,7},{7,6},{8,9},{9,8},{10,11... | collective-permute-start | bytes 2752520 | tf_op jit(solution)/shard_map/ppermute | solution.py:25
  151.6 3.8 %collective-permute-start.26 = (bf16[128,3584]{1,0:T(8,128)(2,1)S(1)}, bf16[128,3584]{1,0:T(8,128)(2,1)S(1)}, u32[]{:S(2)}, u32[]{:S(2)}) collective-permute-start(bf16[128,3584]{1,0:T(8,128)(2,1)S(1)} %split.67), channel_id=1, source_target_pairs={{0,1},{1,0},{2,3},{3,2},{4,5},{5,4},{6,7},{7,6},{8,9},{9,8},{10,11... | collective-permute-start | bytes 2752520 | tf_op jit(solution)/shard_map/ppermute | solution.py:25
  153.4 7.8 %collective-permute-start.32 = (bf16[32,3584]{1,0:T(8,128)(2,1)S(1)}, bf16[32,3584]{1,0:T(8,128)(2,1)S(1)}, u32[]{:S(2)}, u32[]{:S(2)}) collective-permute-start(bf16[32,3584]{1,0:T(8,128)(2,1)S(1)} %get-tuple-element.21), channel_id=1, source_target_pairs={{0,4},{4,8},{8,12},{12,14},{14,10},{10,6},{6,2},{2,0},{1,5},{5,9},... | collective-permute-start | bytes 688136 | tf_op jit(solution)/shard_map/ppermute | solution.py:22
  155.2 7.5 %collective-permute-start.42 = (bf16[32,3584]{1,0:T(8,128)(2,1)S(1)}, bf16[32,3584]{1,0:T(8,128)(2,1)S(1)}, u32[]{:S(2)}, u32[]{:S(2)}) collective-permute-start(bf16[32,3584]{1,0:T(8,128)(2,1)S(1)} %get-tuple-element.22), channel_id=1, source_target_pairs={{0,2},{4,0},{8,4},{12,8},{14,12},{10,14},{6,10},{2,6},{1,3},{5,1},... | collective-permute-start | bytes 688136 | tf_op jit(solution)/shard_map/ppermute | solution.py:22
  155.5 11.5 %copy-start.1 = (f32[256,3584]{1,0:T(8,128)S(1)}, f32[256,3584]{1,0:T(8,128)}, u32[]{:S(2)}) copy-start(f32[256,3584]{1,0:T(8,128)} %fusion.4) | copy-start | bytes 11010052
  162.7 8.6 %collective-permute-start.33 = (bf16[32,3584]{1,0:T(8,128)(2,1)S(1)}, bf16[32,3584]{1,0:T(8,128)(2,1)S(1)}, u32[]{:S(2)}, u32[]{:S(2)}) collective-permute-start(bf16[32,3584]{1,0:T(8,128)(2,1)S(1)} %get-tuple-element.15), channel_id=1, source_target_pairs={{0,4},{4,8},{8,12},{12,14},{14,10},{10,6},{6,2},{2,0},{1,5},{5,9},... | collective-permute-start | bytes 688136 | tf_op jit(solution)/shard_map/ppermute | solution.py:22
  163.1 8.5 %collective-permute-start.43 = (bf16[32,3584]{1,0:T(8,128)(2,1)S(1)}, bf16[32,3584]{1,0:T(8,128)(2,1)S(1)}, u32[]{:S(2)}, u32[]{:S(2)}) collective-permute-start(bf16[32,3584]{1,0:T(8,128)(2,1)S(1)} %get-tuple-element.16), channel_id=1, source_target_pairs={{0,2},{4,0},{8,4},{12,8},{14,12},{10,14},{6,10},{2,6},{1,3},{5,1},... | collective-permute-start | bytes 688136 | tf_op jit(solution)/shard_map/ppermute | solution.py:22
  164.8 9.8 %collective-permute-start.36 = (bf16[32,3584]{1,0:T(8,128)(2,1)S(1)}, bf16[32,3584]{1,0:T(8,128)(2,1)S(1)}, u32[]{:S(2)}, u32[]{:S(2)}) collective-permute-start(bf16[32,3584]{1,0:T(8,128)(2,1)S(1)} %get-tuple-element.19), channel_id=1, source_target_pairs={{0,2},{4,0},{8,4},{12,8},{14,12},{10,14},{6,10},{2,6},{1,3},{5,1},... | collective-permute-start | bytes 688136 | tf_op jit(solution)/shard_map/ppermute | solution.py:22
  165.2 9.4 %collective-permute-start.39 = (bf16[32,3584]{1,0:T(8,128)(2,1)S(1)}, bf16[32,3584]{1,0:T(8,128)(2,1)S(1)}, u32[]{:S(2)}, u32[]{:S(2)}) collective-permute-start(bf16[32,3584]{1,0:T(8,128)(2,1)S(1)} %get-tuple-element.20), channel_id=1, source_target_pairs={{0,4},{4,8},{8,12},{12,14},{14,10},{10,6},{6,2},{2,0},{1,5},{5,9},... | collective-permute-start | bytes 688136 | tf_op jit(solution)/shard_map/ppermute | solution.py:22
  171.3 5.9 %collective-permute-start.10 = (bf16[128,3584]{1,0:T(8,128)(2,1)S(1)}, bf16[128,3584]{1,0:T(8,128)(2,1)S(1)}, u32[]{:S(2)}, u32[]{:S(2)}) collective-permute-start(bf16[128,3584]{1,0:T(8,128)(2,1)S(1)} %copy-done.12), channel_id=1, source_target_pairs={{0,1},{1,0},{2,3},{3,2},{4,5},{5,4},{6,7},{7,6},{8,9},{9,8},{10,11... | collective-permute-start | bytes 2752520 | tf_op jit(solution)/shard_map/ppermute | solution.py:25
  174.8 8.2 %collective-permute-start.34 = (bf16[32,3584]{1,0:T(8,128)(2,1)S(1)}, bf16[32,3584]{1,0:T(8,128)(2,1)S(1)}, u32[]{:S(2)}, u32[]{:S(2)}) collective-permute-start(bf16[32,3584]{1,0:T(8,128)(2,1)S(1)} %get-tuple-element.11), channel_id=1, source_target_pairs={{0,4},{4,8},{8,12},{12,14},{14,10},{10,6},{6,2},{2,0},{1,5},{5,9},... | collective-permute-start | bytes 688136 | tf_op jit(solution)/shard_map/ppermute | solution.py:22
  175.2 8.0 %collective-permute-start.37 = (bf16[32,3584]{1,0:T(8,128)(2,1)S(1)}, bf16[32,3584]{1,0:T(8,128)(2,1)S(1)}, u32[]{:S(2)}, u32[]{:S(2)}) collective-permute-start(bf16[32,3584]{1,0:T(8,128)(2,1)S(1)} %get-tuple-element.14), channel_id=1, source_target_pairs={{0,2},{4,0},{8,4},{12,8},{14,12},{10,14},{6,10},{2,6},{1,3},{5,1},... | collective-permute-start | bytes 688136 | tf_op jit(solution)/shard_map/ppermute | solution.py:22
  176.9 8.5 %collective-permute-start.40 = (bf16[32,3584]{1,0:T(8,128)(2,1)S(1)}, bf16[32,3584]{1,0:T(8,128)(2,1)S(1)}, u32[]{:S(2)}, u32[]{:S(2)}) collective-permute-start(bf16[32,3584]{1,0:T(8,128)(2,1)S(1)} %get-tuple-element.13), channel_id=1, source_target_pairs={{0,4},{4,8},{8,12},{12,14},{14,10},{10,6},{6,2},{2,0},{1,5},{5,9},... | collective-permute-start | bytes 688136 | tf_op jit(solution)/shard_map/ppermute | solution.py:22
  177.2 8.5 %collective-permute-start.44 = (bf16[32,3584]{1,0:T(8,128)(2,1)S(1)}, bf16[32,3584]{1,0:T(8,128)(2,1)S(1)}, u32[]{:S(2)}, u32[]{:S(2)}) collective-permute-start(bf16[32,3584]{1,0:T(8,128)(2,1)S(1)} %get-tuple-element.12), channel_id=1, source_target_pairs={{0,2},{4,0},{8,4},{12,8},{14,12},{10,14},{6,10},{2,6},{1,3},{5,1},... | collective-permute-start | bytes 688136 | tf_op jit(solution)/shard_map/ppermute | solution.py:22
  185.9 7.2 %collective-permute-start.35 = (bf16[32,3584]{1,0:T(8,128)(2,1)S(1)}, bf16[32,3584]{1,0:T(8,128)(2,1)S(1)}, u32[]{:S(2)}, u32[]{:S(2)}) collective-permute-start(bf16[32,3584]{1,0:T(8,128)(2,1)S(1)} %get-tuple-element.7), channel_id=1, source_target_pairs={{0,4},{4,8},{8,12},{12,14},{14,10},{10,6},{6,2},{2,0},{1,5},{5,9},... | collective-permute-start | bytes 688136 | tf_op jit(solution)/shard_map/ppermute | solution.py:22
  186.8 6.6 %collective-permute-start.38 = (bf16[32,3584]{1,0:T(8,128)(2,1)S(1)}, bf16[32,3584]{1,0:T(8,128)(2,1)S(1)}, u32[]{:S(2)}, u32[]{:S(2)}) collective-permute-start(bf16[32,3584]{1,0:T(8,128)(2,1)S(1)} %get-tuple-element.10), channel_id=1, source_target_pairs={{0,2},{4,0},{8,4},{12,8},{14,12},{10,14},{6,10},{2,6},{1,3},{5,1},... | collective-permute-start | bytes 688136 | tf_op jit(solution)/shard_map/ppermute | solution.py:22
  188.0 7.5 %collective-permute-start.41 = (bf16[32,3584]{1,0:T(8,128)(2,1)S(1)}, bf16[32,3584]{1,0:T(8,128)(2,1)S(1)}, u32[]{:S(2)}, u32[]{:S(2)}) collective-permute-start(bf16[32,3584]{1,0:T(8,128)(2,1)S(1)} %get-tuple-element.9), channel_id=1, source_target_pairs={{0,4},{4,8},{8,12},{12,14},{14,10},{10,6},{6,2},{2,0},{1,5},{5,9},... | collective-permute-start | bytes 688136 | tf_op jit(solution)/shard_map/ppermute | solution.py:22
  188.8 7.0 %collective-permute-start.45 = (bf16[32,3584]{1,0:T(8,128)(2,1)S(1)}, bf16[32,3584]{1,0:T(8,128)(2,1)S(1)}, u32[]{:S(2)}, u32[]{:S(2)}) collective-permute-start(bf16[32,3584]{1,0:T(8,128)(2,1)S(1)} %get-tuple-element.8), channel_id=1, source_target_pairs={{0,2},{4,0},{8,4},{12,8},{14,12},{10,14},{6,10},{2,6},{1,3},{5,1},... | collective-permute-start | bytes 688136 | tf_op jit(solution)/shard_map/ppermute | solution.py:22
  (11 other events, 64.0 us)

commit v2 on v1

v2 whole, which is shorter than its diff:
```python
import functools

import jax
import jax.numpy as jnp
from jax import lax
from jax.experimental import pallas as pl
from jax.experimental.pallas import tpu as pltpu
from jax.sharding import PartitionSpec as P

TILE = 256
VMEM_LIMIT = 16 * 2**20
LANES = 128


def ring_order(node_count, group_count):
    if group_count == 2:
        return list(range(0, node_count, 2)) + list(range(node_count - 1, 0, -2))
    return list(range(node_count))


def experts_kernel(pieces, n, me, *refs):
    inputs, (w_gate, w_up, w_down) = refs[:pieces], refs[pieces : pieces + 3]
    mine, theirs, rows, hidden = refs[pieces + 3 :]
    width, units = w_gate.shape
    half = mine.shape[0]
    place = 0
    for piece in inputs:
        rows[pl.ds(place, piece.shape[0])] = piece[...]
        place += piece.shape[0]
    table = rows[:, width:].astype(jnp.float32)
    lane = lax.broadcasted_iota(jnp.int32, table.shape, 1)
    scale = jnp.where(lane == me[0], 1.0 / 256.0, jnp.where(lane == me[0] + n, 1.0 / 65536.0, 0.0))
    factor = jnp.sum(table * scale, axis=1, keepdims=True)
    for start in range(0, units, TILE):
        part = pl.ds(start, TILE)
        gate_act = jnp.dot(rows[:, :width], w_gate[:, part], preferred_element_type=jnp.float32)
        up_act = jnp.dot(rows[:, :width], w_up[:, part], preferred_element_type=jnp.float32)
        silu = gate_act / (1.0 + jnp.exp(-gate_act))
        hidden[:, part] = (silu * up_act * factor).astype(jnp.bfloat16)
    for start in range(0, width, TILE):
        part = pl.ds(start, TILE)
        product = jnp.dot(hidden[...], w_down[:, part], preferred_element_type=jnp.float32)
        mine[:, part] = product[:half].astype(mine.dtype)
        theirs[:, part] = product[half:].astype(jnp.bfloat16)


def run_experts(inputs, me, n, w_gate, w_up, w_down):
    total, message = sum(x.shape[0] for x in inputs), inputs[0].shape[1]
    width, units = w_gate.shape
    vmem = pl.BlockSpec(memory_space=pltpu.VMEM)
    return pl.pallas_call(
        functools.partial(experts_kernel, len(inputs), n),
        out_shape=(
            jax.ShapeDtypeStruct((total // 2, width), jnp.float32),
            jax.ShapeDtypeStruct((total // 2, width), jnp.bfloat16),
        ),
        in_specs=[pl.BlockSpec(memory_space=pltpu.SMEM)] + [vmem] * (len(inputs) + 3),
        out_specs=(vmem, vmem),
        scratch_shapes=[pltpu.VMEM((total, message), jnp.bfloat16), pltpu.VMEM((total, units), jnp.bfloat16)],
        compiler_params=pltpu.CompilerParams(vmem_limit_bytes=VMEM_LIMIT),
        cost_estimate=pl.CostEstimate(flops=6 * total * width * units, bytes_accessed=0, transcendentals=0),
    )(me, *inputs, w_gate, w_up, w_down)


def per_device(order, tokens, expert_ids, gate_fixed, w_gate, w_up, w_down):
    step_count, tok_rows, width = tokens.shape
    n = len(order)
    half = n // 2
    rows = step_count * tok_rows
    cut = step_count // 2 * tok_rows
    me = lax.axis_index("node").astype(jnp.int32).reshape(1)
    matrices = (w_gate[0], w_up[0], w_down[0])

    def shift(value, distance):
        return lax.ppermute(value, "node", [(order[i], order[(i + distance) % n]) for i in range(n)])

    def swap(value):
        return lax.ppermute(value, "local", [(0, 1), (1, 0)])

    experts = lax.broadcasted_iota(jnp.int32, (1, 1, n), 2)
    hit = expert_ids.reshape(rows, -1, 1) == experts
    weight = jnp.sum(jnp.where(hit, gate_fixed.reshape(rows, -1, 1), 0), axis=1)
    table = jnp.concatenate([weight >> 8, weight & 255], axis=1).astype(jnp.bfloat16)
    table = jnp.pad(table, ((0, 0), (0, -2 * n % LANES)))
    own = jnp.concatenate([tokens.reshape(rows, width), table], axis=1)

    plus, minus = shift(own, 1), shift(own, -1)
    results = {0: run_experts([own, swap(own)], me, n, *matrices)}
    for hop in range(1, half):
        plus, minus, results[hop - 1] = lax.optimization_barrier((plus, minus, results[hop - 1]))
        if hop + 1 < half:
            next_plus, next_minus = shift(plus, 1), shift(minus, -1)
        else:
            next_plus, next_minus = shift(plus[:cut], 1), shift(minus[cut:], -1)
        results[hop] = run_experts([plus, minus, swap(plus), swap(minus)], me, n, *matrices)
        plus, minus = next_plus, next_minus
    plus, minus, results[half - 1] = lax.optimization_barrier((plus, minus, results[half - 1]))
    results[half] = run_experts([plus, minus, swap(plus), swap(minus)], me, n, *matrices)

    def local_sum(hop):
        mine, theirs = results[hop]
        return mine + swap(theirs).astype(jnp.float32)

    far = local_sum(half).astype(jnp.bfloat16)
    ahead, back = shift(far[:cut], 1), shift(far[cut:], -1)
    for hop in range(half - 1, 0, -1):
        total = local_sum(hop)
        to_back, to_ahead = total[:rows], total[rows:]
        if hop == half - 1:
            ahead = jnp.concatenate([to_ahead[:cut] + ahead.astype(jnp.float32), to_ahead[cut:]])
            back = jnp.concatenate([to_back[:cut], to_back[cut:] + back.astype(jnp.float32)])
        else:
            ahead = to_ahead + ahead.astype(jnp.float32)
            back = to_back + back.astype(jnp.float32)
        ahead, back = shift(ahead.astype(jnp.bfloat16), 1), shift(back.astype(jnp.bfloat16), -1)
    total = local_sum(0) + ahead.astype(jnp.float32) + back.astype(jnp.float32)
    return total.astype(jnp.bfloat16).reshape(tokens.shape)


def solution(mesh):
    order = ring_order(mesh.shape["node"], mesh.shape["groups"])
    rows = P(None, ("groups", "node", "local"), None)
    in_specs = (rows, rows, rows, P("node", None, "local"), P("node", None, "local"), P("node", "local", None))
    return jax.shard_map(
        functools.partial(per_device, order), mesh=mesh, in_specs=in_specs, out_specs=rows, check_vma=False
    )
```

time: 197 us -> 111 us (0.56)
  matrix products: 45.9 us -> 0 us
  starting transfers between devices: 40.9 us -> 20 us
  Pallas kernels: 0 us -> 12.9 us
  local copies, waits for them, and re-layouts: 20.4 us -> 7.86 us
  waiting for transfers between devices: 77.3 us -> 66.3 us
  other arithmetic: 11.5 us -> 3.27 us
    dot_general x10 -> x0, matrix products: 45.9 us -> none  [the longest x5 33.7 us: experts(): part = jnp.dot(hidden, down_mat, preferred_element_type=jnp.float32)]
    ppermute x35 -> x16, starting transfers between devices: 39.4 us -> 16.2 us  [shift(): lax.ppermute(value, 'node', [(order[i], order[(i + distance) % n]) for i...]
    ppermute x35 -> x16, waiting for transfers between devices: 76.1 us -> 60.5 us  [shift(): lax.ppermute(value, 'node', [(order[i], order[(i + distance) % n]) for i...]
    pallas_call x0 -> x5, Pallas kernels: none -> 12.9 us  [run_experts(): pl.pallas_call(functools.partial(experts_kernel, len(inputs), n), out_sha...]
    split x5 -> x0, local copies, waits for them, and re-layouts: 8.83 us -> none  [experts(): mine, theirs = jnp.split(part, 2)]
    concatenate x4 -> x1, local copies, waits for them, and re-layouts: 5.71 us -> 0.1 us  [per_device(): jnp.concatenate([weight >> 8, weight & 255], axis=1).astype(jnp.bfloat16)]
    ppermute x11 -> x14, waiting for transfers between devices: 1.12 us -> 5.86 us  [swap(): return lax.ppermute(value, 'local', [(0, 1), (1, 0)])]
    unnamed x40 -> x10, local copies, waits for them, and re-layouts: 3 us -> 7.5 us
  transfers between devices with their start and end apart: 46 -> 30, of which waited for: 29 -> 20; matrix products, arithmetic and copies ran while one was open for 37% -> 1% of each run, Pallas kernels for 0% -> 10%
where the time goes in v2:
time: 111 us; the launch traced here: 110 us
  waiting for transfers between devices  66.3 us (60%)
  starting transfers between devices  20 us (18%)
  Pallas kernels  12.9 us (12%)
  local copies, waits for them, and re-layouts  7.86 us (7%)
  other arithmetic  3.27 us (3%)
    ppermute x16, waiting for transfers between devices, shift(): lax.ppermute(value, 'node', [(order[i], order[(i + distance) % n]) for i...  60.5 us
    ppermute x16, starting transfers between devices, shift(): lax.ppermute(value, 'node', [(order[i], order[(i + distance) % n]) for i...  16.2 us
    pallas_call x5, Pallas kernels, run_experts(): pl.pallas_call(functools.partial(experts_kernel, len(inputs), n), out_sha...  12.9 us
    unnamed x10, local copies, waits for them, and re-layouts  7.5 us
    ppermute x14, waiting for transfers between devices, swap(): return lax.ppermute(value, 'local', [(0, 1), (1, 0)])  5.86 us
    ppermute x14, starting transfers between devices, swap(): return lax.ppermute(value, 'local', [(0, 1), (1, 0)])  3.82 us
  transfers between devices with their start and end apart: 30, of which 20 were waited for; matrix products, arithmetic and copies ran while one was open for 1% of the time, Pallas kernels for 10%

profile of v2, /device:TPU:0, one launch (start us, length us, event | category | flops | bytes accessed | tf_op | source)
XLA Modules:
  0.0 110.5 jit_solution(8723935712689319476)
XLA Ops:
  0.0 0.7 copy.17
  0.8 0.7 copy.16
  1.7 1.1 fusion.5.refs_0_
  2.7 0.5 collective-permute-start.2
  3.3 2.6 %collective-permute-start = (bf16[64,3712]{1,0:T(8,128)(2,1)S(1)}, bf16[64,3712]{1,0:T(8,128)(2,1)S(1)}, u32[]{:S(2)}, u32[]{:S(2)}) collective-permute-start(bf16[64,3712]{1,0:T(8,128)(2,1)S(1)} %fusion.5.refs_0_), channel_id=1, source_target_pairs={{0,4},{4,8},{8,12},{12,14},{14,10},{10,6},{6,2},{2,0},{1,5},{5,9},... | collective-permute-start | bytes 1425416 | tf_op jit(solution)/shard_map/ppermute | solution.py:75
  5.9 2.0 %copy-done = bf16[1,3584,512]{2,1,0:T(8,128)(2,1)S(1)} copy-done((bf16[1,3584,512]{2,1,0:T(8,128)(2,1)S(1)}, bf16[1,3584,512]{2,1,0:T(8,128)(2,1)}, u32[]{:S(2)}) %copy-start) | copy-done | bytes 3670040
  8.0 2.0 %copy-done.2 = bf16[1,3584,512]{2,1,0:T(8,128)(2,1)S(1)} copy-done((bf16[1,3584,512]{2,1,0:T(8,128)(2,1)S(1)}, bf16[1,3584,512]{2,1,0:T(8,128)(2,1)}, u32[]{:S(2)}) %copy-start.2) | copy-done | bytes 3670040
  10.0 2.0 %copy-done.3 = bf16[1,512,3584]{2,1,0:T(8,128)(2,1)S(1)} copy-done((bf16[1,512,3584]{2,1,0:T(8,128)(2,1)S(1)}, bf16[1,512,3584]{2,1,0:T(8,128)(2,1)}, u32[]{:S(2)}) %copy-start.3) | copy-done | bytes 3670040
  12.0 1.8 %shard_map.64 = (f32[64,3584]{1,0:T(8,128)S(1)}, bf16[64,3584]{1,0:T(8,128)(2,1)S(1)}) custom-call(s32[1]{0:T(128)} %bitcast.1.me, bf16[64,3712]{1,0:T(8,128)(2,1)S(1)} %fusion.5.refs_0_, bf16[64,3712]{1,0:T(8,128)(2,1)S(1)} %collective-permute-done.2.refs_1_, bf16[3584,512]{1,0:T(8,128)(2,1)S(1)} %bitcast.10, bf16[3584,512]{1,0:T(8,128)(2,1)S(1)} %bitcast.15, ...), custom_call_target="tpu_custom_call" | custom-call | flops 1409286144 | tf_op jit(solution)/shard_map/pallas_call | solution.py:51
  13.9 3.5 %collective-permute-done.refs_0_ = bf16[64,3712]{1,0:T(8,128)(2,1)S(1)} collective-permute-done((bf16[64,3712]{1,0:T(8,128)(2,1)S(1)}, bf16[64,3712]{1,0:T(8,128)(2,1)S(1)}, u32[]{:S(2)}, u32[]{:S(2)}) %collective-permute-start) | collective-permute-done | bytes 475168 | tf_op jit(solution)/shard_map/ppermute | solution.py:75
  17.3 1.5 %collective-permute-done.1.refs_1_ = bf16[64,3712]{1,0:T(8,128)(2,1)S(1)} collective-permute-done((bf16[64,3712]{1,0:T(8,128)(2,1)S(1)}, bf16[64,3712]{1,0:T(8,128)(2,1)S(1)}, u32[]{:S(2)}, u32[]{:S(2)}) %collective-permute-start.1) | collective-permute-done | bytes 475168 | tf_op jit(solution)/shard_map/ppermute | solution.py:75
  18.8 0.5 collective-permute-start.7
  19.3 1.6 %collective-permute-start.4 = (bf16[64,3712]{1,0:T(8,128)(2,1)S(1)}, bf16[64,3712]{1,0:T(8,128)(2,1)S(1)}, u32[]{:S(2)}, u32[]{:S(2)}) collective-permute-start(bf16[64,3712]{1,0:T(8,128)(2,1)S(1)} %collective-permute-done.refs_0_), channel_id=1, source_target_pairs={{0,4},{4,8},{8,12},{12,14},{14,10},{10,6},{6,2},{2,0},{1,5},{5,9},... | collective-permute-start | bytes 1425416 | tf_op jit(solution)/shard_map/ppermute | solution.py:75
  20.9 0.4 collective-permute-start.5
  21.4 3.1 %shard_map.65 = (f32[128,3584]{1,0:T(8,128)S(1)}, bf16[128,3584]{1,0:T(8,128)(2,1)S(1)}) custom-call(s32[1]{0:T(128)} %bitcast.1.me, bf16[64,3712]{1,0:T(8,128)(2,1)S(1)} %collective-permute-done.refs_0_, bf16[64,3712]{1,0:T(8,128)(2,1)S(1)} %collective-permute-done.1.refs_1_, bf16[64,3712]{1,0:T(8,128)(2,1)S(1)} %collective-permute-done.6.refs_2_, ...), custom_call_target="tpu_custom_call" | custom-call | flops 2818572288 | tf_op jit(solution)/shard_map/pallas_call | solution.py:51
  24.5 7.6 %collective-permute-done.4.refs_0_ = bf16[64,3712]{1,0:T(8,128)(2,1)S(1)} collective-permute-done((bf16[64,3712]{1,0:T(8,128)(2,1)S(1)}, bf16[64,3712]{1,0:T(8,128)(2,1)S(1)}, u32[]{:S(2)}, u32[]{:S(2)}) %collective-permute-start.4) | collective-permute-done | bytes 475168 | tf_op jit(solution)/shard_map/ppermute | solution.py:75
  32.1 1.3 %collective-permute-done.5.refs_1_ = bf16[64,3712]{1,0:T(8,128)(2,1)S(1)} collective-permute-done((bf16[64,3712]{1,0:T(8,128)(2,1)S(1)}, bf16[64,3712]{1,0:T(8,128)(2,1)S(1)}, u32[]{:S(2)}, u32[]{:S(2)}) %collective-permute-start.5) | collective-permute-done | bytes 475168 | tf_op jit(solution)/shard_map/ppermute | solution.py:75
  33.4 0.5 collective-permute-start.12
  33.9 1.6 %collective-permute-start.9 = (bf16[64,3712]{1,0:T(8,128)(2,1)S(1)}, bf16[64,3712]{1,0:T(8,128)(2,1)S(1)}, u32[]{:S(2)}, u32[]{:S(2)}) collective-permute-start(bf16[64,3712]{1,0:T(8,128)(2,1)S(1)} %collective-permute-done.4.refs_0_), channel_id=1, source_target_pairs={{0,4},{4,8},{8,12},{12,14},{14,10},{10,6},{6,2},{2,0},{1,5},{5,9},... | collective-permute-start | bytes 1425416 | tf_op jit(solution)/shard_map/ppermute | solution.py:75
  35.5 0.4 collective-permute-start.10
  36.0 3.1 %shard_map.66 = (f32[128,3584]{1,0:T(8,128)S(1)}, bf16[128,3584]{1,0:T(8,128)(2,1)S(1)}) custom-call(s32[1]{0:T(128)} %bitcast.1.me, bf16[64,3712]{1,0:T(8,128)(2,1)S(1)} %collective-permute-done.4.refs_0_, bf16[64,3712]{1,0:T(8,128)(2,1)S(1)} %collective-permute-done.5.refs_1_, bf16[64,3712]{1,0:T(8,128)(2,1)S(1)} %collective-permute-done.11.refs_2_, ...), custom_call_target="tpu_custom_call" | custom-call | flops 2818572288 | tf_op jit(solution)/shard_map/pallas_call | solution.py:51
  39.1 7.6 %collective-permute-done.9.refs_0_ = bf16[64,3712]{1,0:T(8,128)(2,1)S(1)} collective-permute-done((bf16[64,3712]{1,0:T(8,128)(2,1)S(1)}, bf16[64,3712]{1,0:T(8,128)(2,1)S(1)}, u32[]{:S(2)}, u32[]{:S(2)}) %collective-permute-start.9) | collective-permute-done | bytes 475168 | tf_op jit(solution)/shard_map/ppermute | solution.py:75
  46.7 1.3 %collective-permute-done.10.refs_1_ = bf16[64,3712]{1,0:T(8,128)(2,1)S(1)} collective-permute-done((bf16[64,3712]{1,0:T(8,128)(2,1)S(1)}, bf16[64,3712]{1,0:T(8,128)(2,1)S(1)}, u32[]{:S(2)}, u32[]{:S(2)}) %collective-permute-start.10) | collective-permute-done | bytes 475168 | tf_op jit(solution)/shard_map/ppermute | solution.py:75
  48.0 0.5 collective-permute-start.17
  48.6 1.6 %collective-permute-start.14 = (bf16[32,3712]{1,0:T(8,128)(2,1)S(1)}, bf16[32,3712]{1,0:T(8,128)(2,1)S(1)}, u32[]{:S(2)}, u32[]{:S(2)}) collective-permute-start(bf16[32,3712]{1,0:T(8,128)(2,1)S(1)} %slice.46), channel_id=1, source_target_pairs={{0,4},{4,8},{8,12},{12,14},{14,10},{10,6},{6,2},{2,0},{1,5},{5,9},... | collective-permute-start | bytes 712712 | tf_op jit(solution)/shard_map/ppermute | solution.py:75
  50.1 0.5 collective-permute-start.15
  50.7 3.1 %shard_map.67 = (f32[128,3584]{1,0:T(8,128)S(1)}, bf16[128,3584]{1,0:T(8,128)(2,1)S(1)}) custom-call(s32[1]{0:T(128)} %bitcast.1.me, bf16[64,3712]{1,0:T(8,128)(2,1)S(1)} %collective-permute-done.9.refs_0_, bf16[64,3712]{1,0:T(8,128)(2,1)S(1)} %collective-permute-done.10.refs_1_, bf16[64,3712]{1,0:T(8,128)(2,1)S(1)} %collective-permute-done.16.refs_2_, ...), custom_call_target="tpu_custom_call" | custom-call | flops 2818572288 | tf_op jit(solution)/shard_map/pallas_call | solution.py:51
  53.8 2.5 %collective-permute-done.14.refs_0_ = bf16[32,3712]{1,0:T(8,128)(2,1)S(1)} collective-permute-done((bf16[32,3712]{1,0:T(8,128)(2,1)S(1)}, bf16[32,3712]{1,0:T(8,128)(2,1)S(1)}, u32[]{:S(2)}, u32[]{:S(2)}) %collective-permute-start.14) | collective-permute-done | bytes 237600 | tf_op jit(solution)/shard_map/ppermute | solution.py:75
  56.3 1.2 %collective-permute-done.15.refs_1_ = bf16[32,3712]{1,0:T(8,128)(2,1)S(1)} collective-permute-done((bf16[32,3712]{1,0:T(8,128)(2,1)S(1)}, bf16[32,3712]{1,0:T(8,128)(2,1)S(1)}, u32[]{:S(2)}, u32[]{:S(2)}) %collective-permute-start.15) | collective-permute-done | bytes 237600 | tf_op jit(solution)/shard_map/ppermute | solution.py:75
  57.5 0.5 collective-permute-start.20
  58.1 1.0 collective-permute-done.19.refs_2_
  59.4 1.8 %shard_map.68 = (f32[64,3584]{1,0:T(8,128)S(1)}, bf16[64,3584]{1,0:T(8,128)(2,1)S(1)}) custom-call(s32[1]{0:T(128)} %bitcast.1.me, bf16[32,3712]{1,0:T(8,128)(2,1)S(1)} %collective-permute-done.14.refs_0_, bf16[32,3712]{1,0:T(8,128)(2,1)S(1)} %collective-permute-done.15.refs_1_, bf16[32,3712]{1,0:T(8,128)(2,1)S(1)} %collective-permute-done.19.refs_2_, ...), custom_call_target="tpu_custom_call" | custom-call | flops 1409286144 | tf_op jit(solution)/shard_map/pallas_call | solution.py:51
  62.4 0.6 collective-permute-done.21
  63.2 0.6 collective-permute-start.22
  63.7 3.9 %collective-permute-done.18 = bf16[128,3584]{1,0:T(8,128)(2,1)S(1)} collective-permute-done((bf16[128,3584]{1,0:T(8,128)(2,1)S(1)}, bf16[128,3584]{1,0:T(8,128)(2,1)S(1)}, u32[]{:S(2)}, u32[]{:S(2)}) %collective-permute-start.18) | collective-permute-done | bytes 917536 | tf_op jit(solution)/shard_map/ppermute | solution.py:78
  67.6 0.5 collective-permute-start.26
  68.4 2.5 %collective-permute-done.22 = bf16[32,3584]{1,0:T(8,128)(2,1)S(1)} collective-permute-done((bf16[32,3584]{1,0:T(8,128)(2,1)S(1)}, bf16[32,3584]{1,0:T(8,128)(2,1)S(1)}, u32[]{:S(2)}, u32[]{:S(2)}) %collective-permute-start.22) | collective-permute-done | bytes 229408 | tf_op jit(solution)/shard_map/ppermute | solution.py:75
  70.9 4.4 %collective-permute-done.26 = bf16[32,3584]{1,0:T(8,128)(2,1)S(1)} collective-permute-done((bf16[32,3584]{1,0:T(8,128)(2,1)S(1)}, bf16[32,3584]{1,0:T(8,128)(2,1)S(1)}, u32[]{:S(2)}, u32[]{:S(2)}) %collective-permute-start.26) | collective-permute-done | bytes 229408 | tf_op jit(solution)/shard_map/ppermute | solution.py:75
  75.5 0.6 collective-permute-start.23
  76.1 1.6 %collective-permute-start.27 = (bf16[64,3584]{1,0:T(8,128)(2,1)S(1)}, bf16[64,3584]{1,0:T(8,128)(2,1)S(1)}, u32[]{:S(2)}, u32[]{:S(2)}) collective-permute-start(bf16[64,3584]{1,0:T(8,128)(2,1)S(1)} %pad_maximum_fusion.1), channel_id=1, source_target_pairs={{0,2},{4,0},{8,4},{12,8},{14,12},{10,14},{6,10},{2,6},{1,3},{5,1},... | collective-permute-start | bytes 1376264 | tf_op jit(solution)/shard_map/ppermute | solution.py:75
  77.8 9.4 %collective-permute-done.23 = bf16[64,3584]{1,0:T(8,128)(2,1)S(1)} collective-permute-done((bf16[64,3584]{1,0:T(8,128)(2,1)S(1)}, bf16[64,3584]{1,0:T(8,128)(2,1)S(1)}, u32[]{:S(2)}, u32[]{:S(2)}) %collective-permute-start.23) | collective-permute-done | bytes 458784 | tf_op jit(solution)/shard_map/ppermute | solution.py:75
  87.8 0.5 collective-permute-start.24
  88.2 1.6 %collective-permute-start.28 = (bf16[64,3584]{1,0:T(8,128)(2,1)S(1)}, bf16[64,3584]{1,0:T(8,128)(2,1)S(1)}, u32[]{:S(2)}, u32[]{:S(2)}) collective-permute-start(bf16[64,3584]{1,0:T(8,128)(2,1)S(1)} %get-tuple-element.62), channel_id=1, source_target_pairs={{0,2},{4,0},{8,4},{12,8},{14,12},{10,14},{6,10},{2,6},{1,3},{5,1},... | collective-permute-start | bytes 1376264 | tf_op jit(solution)/shard_map/ppermute | solution.py:75
  90.0 8.4 %collective-permute-done.24 = bf16[64,3584]{1,0:T(8,128)(2,1)S(1)} collective-permute-done((bf16[64,3584]{1,0:T(8,128)(2,1)S(1)}, bf16[64,3584]{1,0:T(8,128)(2,1)S(1)}, u32[]{:S(2)}, u32[]{:S(2)}) %collective-permute-start.24) | collective-permute-done | bytes 458784 | tf_op jit(solution)/shard_map/ppermute | solution.py:75
  98.8 1.6 %collective-permute-start.29 = (bf16[64,3584]{1,0:T(8,128)(2,1)S(1)}, bf16[64,3584]{1,0:T(8,128)(2,1)S(1)}, u32[]{:S(2)}, u32[]{:S(2)}) collective-permute-start(bf16[64,3584]{1,0:T(8,128)(2,1)S(1)} %get-tuple-element.60), channel_id=1, source_target_pairs={{0,2},{4,0},{8,4},{12,8},{14,12},{10,14},{6,10},{2,6},{1,3},{5,1},... | collective-permute-start | bytes 1376264 | tf_op jit(solution)/shard_map/ppermute | solution.py:75
  100.9 7.5 %collective-permute-done.29 = bf16[64,3584]{1,0:T(8,128)(2,1)S(1)} collective-permute-done((bf16[64,3584]{1,0:T(8,128)(2,1)S(1)}, bf16[64,3584]{1,0:T(8,128)(2,1)S(1)}, u32[]{:S(2)}, u32[]{:S(2)}) %collective-permute-start.29) | collective-permute-done | bytes 458784 | tf_op jit(solution)/shard_map/ppermute | solution.py:75
  108.4 1.1 collective-permute-done.25
  109.5 1.0 add_convert_fusion
  (48 shorter events, 4.3 us)
Async XLA Ops:
  2.7 3.2 %collective-permute-start.2 = (bf16[64,3712]{1,0:T(8,128)(2,1)S(1)}, bf16[64,3712]{1,0:T(8,128)(2,1)S(1)}, u32[]{:S(2)}, u32[]{:S(2)}) collective-permute-start(bf16[64,3712]{1,0:T(8,128)(2,1)S(1)} %fusion.5.refs_0_), channel_id=1, source_target_pairs={{0,1},{1,0},{2,3},{3,2},{4,5},{5,4},{6,7},{7,6},{8,9},{9,8},{10,11... | collective-permute-start | bytes 1425416 | tf_op jit(solution)/shard_map/ppermute | solution.py:78
  3.3 14.1 %collective-permute-start = (bf16[64,3712]{1,0:T(8,128)(2,1)S(1)}, bf16[64,3712]{1,0:T(8,128)(2,1)S(1)}, u32[]{:S(2)}, u32[]{:S(2)}) collective-permute-start(bf16[64,3712]{1,0:T(8,128)(2,1)S(1)} %fusion.5.refs_0_), channel_id=1, source_target_pairs={{0,4},{4,8},{8,12},{12,14},{14,10},{10,6},{6,2},{2,0},{1,5},{5,9},... | collective-permute-start | bytes 1425416 | tf_op jit(solution)/shard_map/ppermute | solution.py:75
  5.9 12.9 %collective-permute-start.1 = (bf16[64,3712]{1,0:T(8,128)(2,1)S(1)}, bf16[64,3712]{1,0:T(8,128)(2,1)S(1)}, u32[]{:S(2)}, u32[]{:S(2)}) collective-permute-start(bf16[64,3712]{1,0:T(8,128)(2,1)S(1)} %fusion.5.refs_0_), channel_id=1, source_target_pairs={{0,2},{4,0},{8,4},{12,8},{14,12},{10,14},{6,10},{2,6},{1,3},{5,1},... | collective-permute-start | bytes 1425416 | tf_op jit(solution)/shard_map/ppermute | solution.py:75
  5.9 2.0 %copy-start = (bf16[1,3584,512]{2,1,0:T(8,128)(2,1)S(1)}, bf16[1,3584,512]{2,1,0:T(8,128)(2,1)}, u32[]{:S(2)}) copy-start(bf16[1,3584,512]{2,1,0:T(8,128)(2,1)} %param.9) | copy-start | bytes 11010052
  8.0 2.0 %copy-start.2 = (bf16[1,3584,512]{2,1,0:T(8,128)(2,1)S(1)}, bf16[1,3584,512]{2,1,0:T(8,128)(2,1)}, u32[]{:S(2)}) copy-start(bf16[1,3584,512]{2,1,0:T(8,128)(2,1)} %param.10) | copy-start | bytes 11010052
  10.0 2.0 %copy-start.3 = (bf16[1,512,3584]{2,1,0:T(8,128)(2,1)S(1)}, bf16[1,512,3584]{2,1,0:T(8,128)(2,1)}, u32[]{:S(2)}) copy-start(bf16[1,512,3584]{2,1,0:T(8,128)(2,1)} %param.11) | copy-start | bytes 11010052
  12.0 9.3 %copy-start.1 = (bf16[1,3584,512]{2,1,0:T(8,128)(2,1)S(1)}, bf16[1,3584,512]{2,1,0:T(8,128)(2,1)}, u32[]{:S(2)}) copy-start(bf16[1,3584,512]{2,1,0:T(8,128)(2,1)} %param.9) | copy-start | bytes 11010052
  18.8 2.5 %collective-permute-start.6 = (bf16[64,3712]{1,0:T(8,128)(2,1)S(1)}, bf16[64,3712]{1,0:T(8,128)(2,1)S(1)}, u32[]{:S(2)}, u32[]{:S(2)}) collective-permute-start(bf16[64,3712]{1,0:T(8,128)(2,1)S(1)} %collective-permute-done.refs_0_), channel_id=1, source_target_pairs={{0,1},{1,0},{2,3},{3,2},{4,5},{5,4},{6,7},{7,6},{8,9},{9,8},{10,11... | collective-permute-start | bytes 1425416 | tf_op jit(solution)/shard_map/ppermute | solution.py:78
  18.8 2.5 %collective-permute-start.7 = (bf16[64,3712]{1,0:T(8,128)(2,1)S(1)}, bf16[64,3712]{1,0:T(8,128)(2,1)S(1)}, u32[]{:S(2)}, u32[]{:S(2)}) collective-permute-start(bf16[64,3712]{1,0:T(8,128)(2,1)S(1)} %collective-permute-done.1.refs_1_), channel_id=1, source_target_pairs={{0,1},{1,0},{2,3},{3,2},{4,5},{5,4},{6,7},{7,6},{8,9},{9,8},{10,11... | collective-permute-start | bytes 1425416 | tf_op jit(solution)/shard_map/ppermute | solution.py:78
  19.3 12.8 %collective-permute-start.4 = (bf16[64,3712]{1,0:T(8,128)(2,1)S(1)}, bf16[64,3712]{1,0:T(8,128)(2,1)S(1)}, u32[]{:S(2)}, u32[]{:S(2)}) collective-permute-start(bf16[64,3712]{1,0:T(8,128)(2,1)S(1)} %collective-permute-done.refs_0_), channel_id=1, source_target_pairs={{0,4},{4,8},{8,12},{12,14},{14,10},{10,6},{6,2},{2,0},{1,5},{5,9},... | collective-permute-start | bytes 1425416 | tf_op jit(solution)/shard_map/ppermute | solution.py:75
  20.9 12.5 %collective-permute-start.5 = (bf16[64,3712]{1,0:T(8,128)(2,1)S(1)}, bf16[64,3712]{1,0:T(8,128)(2,1)S(1)}, u32[]{:S(2)}, u32[]{:S(2)}) collective-permute-start(bf16[64,3712]{1,0:T(8,128)(2,1)S(1)} %collective-permute-done.1.refs_1_), channel_id=1, source_target_pairs={{0,2},{4,0},{8,4},{12,8},{14,12},{10,14},{6,10},{2,6},{1,3},{5,1},... | collective-permute-start | bytes 1425416 | tf_op jit(solution)/shard_map/ppermute | solution.py:75
  33.4 2.5 %collective-permute-start.11 = (bf16[64,3712]{1,0:T(8,128)(2,1)S(1)}, bf16[64,3712]{1,0:T(8,128)(2,1)S(1)}, u32[]{:S(2)}, u32[]{:S(2)}) collective-permute-start(bf16[64,3712]{1,0:T(8,128)(2,1)S(1)} %collective-permute-done.4.refs_0_), channel_id=1, source_target_pairs={{0,1},{1,0},{2,3},{3,2},{4,5},{5,4},{6,7},{7,6},{8,9},{9,8},{10,11... | collective-permute-start | bytes 1425416 | tf_op jit(solution)/shard_map/ppermute | solution.py:78
  33.4 2.5 %collective-permute-start.12 = (bf16[64,3712]{1,0:T(8,128)(2,1)S(1)}, bf16[64,3712]{1,0:T(8,128)(2,1)S(1)}, u32[]{:S(2)}, u32[]{:S(2)}) collective-permute-start(bf16[64,3712]{1,0:T(8,128)(2,1)S(1)} %collective-permute-done.5.refs_1_), channel_id=1, source_target_pairs={{0,1},{1,0},{2,3},{3,2},{4,5},{5,4},{6,7},{7,6},{8,9},{9,8},{10,11... | collective-permute-start | bytes 1425416 | tf_op jit(solution)/shard_map/ppermute | solution.py:78
  33.9 12.8 %collective-permute-start.9 = (bf16[64,3712]{1,0:T(8,128)(2,1)S(1)}, bf16[64,3712]{1,0:T(8,128)(2,1)S(1)}, u32[]{:S(2)}, u32[]{:S(2)}) collective-permute-start(bf16[64,3712]{1,0:T(8,128)(2,1)S(1)} %collective-permute-done.4.refs_0_), channel_id=1, source_target_pairs={{0,4},{4,8},{8,12},{12,14},{14,10},{10,6},{6,2},{2,0},{1,5},{5,9},... | collective-permute-start | bytes 1425416 | tf_op jit(solution)/shard_map/ppermute | solution.py:75
  35.5 12.5 %collective-permute-start.10 = (bf16[64,3712]{1,0:T(8,128)(2,1)S(1)}, bf16[64,3712]{1,0:T(8,128)(2,1)S(1)}, u32[]{:S(2)}, u32[]{:S(2)}) collective-permute-start(bf16[64,3712]{1,0:T(8,128)(2,1)S(1)} %collective-permute-done.5.refs_1_), channel_id=1, source_target_pairs={{0,2},{4,0},{8,4},{12,8},{14,12},{10,14},{6,10},{2,6},{1,3},{5,1},... | collective-permute-start | bytes 1425416 | tf_op jit(solution)/shard_map/ppermute | solution.py:75
  48.0 2.6 %collective-permute-start.16 = (bf16[64,3712]{1,0:T(8,128)(2,1)S(1)}, bf16[64,3712]{1,0:T(8,128)(2,1)S(1)}, u32[]{:S(2)}, u32[]{:S(2)}) collective-permute-start(bf16[64,3712]{1,0:T(8,128)(2,1)S(1)} %collective-permute-done.9.refs_0_), channel_id=1, source_target_pairs={{0,1},{1,0},{2,3},{3,2},{4,5},{5,4},{6,7},{7,6},{8,9},{9,8},{10,11... | collective-permute-start | bytes 1425416 | tf_op jit(solution)/shard_map/ppermute | solution.py:78
  48.0 2.6 %collective-permute-start.17 = (bf16[64,3712]{1,0:T(8,128)(2,1)S(1)}, bf16[64,3712]{1,0:T(8,128)(2,1)S(1)}, u32[]{:S(2)}, u32[]{:S(2)}) collective-permute-start(bf16[64,3712]{1,0:T(8,128)(2,1)S(1)} %collective-permute-done.10.refs_1_), channel_id=1, source_target_pairs={{0,1},{1,0},{2,3},{3,2},{4,5},{5,4},{6,7},{7,6},{8,9},{9,8},{10,11... | collective-permute-start | bytes 1425416 | tf_op jit(solution)/shard_map/ppermute | solution.py:78
  48.6 7.7 %collective-permute-start.14 = (bf16[32,3712]{1,0:T(8,128)(2,1)S(1)}, bf16[32,3712]{1,0:T(8,128)(2,1)S(1)}, u32[]{:S(2)}, u32[]{:S(2)}) collective-permute-start(bf16[32,3712]{1,0:T(8,128)(2,1)S(1)} %slice.46), channel_id=1, source_target_pairs={{0,4},{4,8},{8,12},{12,14},{14,10},{10,6},{6,2},{2,0},{1,5},{5,9},... | collective-permute-start | bytes 712712 | tf_op jit(solution)/shard_map/ppermute | solution.py:75
  50.1 7.4 %collective-permute-start.15 = (bf16[32,3712]{1,0:T(8,128)(2,1)S(1)}, bf16[32,3712]{1,0:T(8,128)(2,1)S(1)}, u32[]{:S(2)}, u32[]{:S(2)}) collective-permute-start(bf16[32,3712]{1,0:T(8,128)(2,1)S(1)} %slice.47), channel_id=1, source_target_pairs={{0,2},{4,0},{8,4},{12,8},{14,12},{10,14},{6,10},{2,6},{1,3},{5,1},... | collective-permute-start | bytes 712712 | tf_op jit(solution)/shard_map/ppermute | solution.py:75
  57.5 1.5 %collective-permute-start.19 = (bf16[32,3712]{1,0:T(8,128)(2,1)S(1)}, bf16[32,3712]{1,0:T(8,128)(2,1)S(1)}, u32[]{:S(2)}, u32[]{:S(2)}) collective-permute-start(bf16[32,3712]{1,0:T(8,128)(2,1)S(1)} %collective-permute-done.14.refs_0_), channel_id=1, source_target_pairs={{0,1},{1,0},{2,3},{3,2},{4,5},{5,4},{6,7},{7,6},{8,9},{9,8},{10,11... | collective-permute-start | bytes 712712 | tf_op jit(solution)/shard_map/ppermute | solution.py:78
  57.5 1.8 %collective-permute-start.20 = (bf16[32,3712]{1,0:T(8,128)(2,1)S(1)}, bf16[32,3712]{1,0:T(8,128)(2,1)S(1)}, u32[]{:S(2)}, u32[]{:S(2)}) collective-permute-start(bf16[32,3712]{1,0:T(8,128)(2,1)S(1)} %collective-permute-done.15.refs_1_), channel_id=1, source_target_pairs={{0,1},{1,0},{2,3},{3,2},{4,5},{5,4},{6,7},{7,6},{8,9},{9,8},{10,11... | collective-permute-start | bytes 712712 | tf_op jit(solution)/shard_map/ppermute | solution.py:78
  61.1 1.9 %collective-permute-start.21 = (bf16[64,3584]{1,0:T(8,128)(2,1)S(1)}, bf16[64,3584]{1,0:T(8,128)(2,1)S(1)}, u32[]{:S(2)}, u32[]{:S(2)}) collective-permute-start(bf16[64,3584]{1,0:T(8,128)(2,1)S(1)} %get-tuple-element.56), channel_id=1, source_target_pairs={{0,1},{1,0},{2,3},{3,2},{4,5},{5,4},{6,7},{7,6},{8,9},{9,8},{10,11... | collective-permute-start | bytes 1376264 | tf_op jit(solution)/shard_map/ppermute | solution.py:78
  61.4 39.5 %collective-permute-start.3 = (bf16[64,3584]{1,0:T(8,128)(2,1)S(1)}, bf16[64,3584]{1,0:T(8,128)(2,1)S(1)}, u32[]{:S(2)}, u32[]{:S(2)}) collective-permute-start(bf16[64,3584]{1,0:T(8,128)(2,1)S(1)} %get-tuple-element.34), channel_id=1, source_target_pairs={{0,1},{1,0},{2,3},{3,2},{4,5},{5,4},{6,7},{7,6},{8,9},{9,8},{10,11... | collective-permute-start | bytes 1376264 | tf_op jit(solution)/shard_map/ppermute | solution.py:78
  61.7 28.1 %collective-permute-start.8 = (bf16[128,3584]{1,0:T(8,128)(2,1)S(1)}, bf16[128,3584]{1,0:T(8,128)(2,1)S(1)}, u32[]{:S(2)}, u32[]{:S(2)}) collective-permute-start(bf16[128,3584]{1,0:T(8,128)(2,1)S(1)} %get-tuple-element.40), channel_id=1, source_target_pairs={{0,1},{1,0},{2,3},{3,2},{4,5},{5,4},{6,7},{7,6},{8,9},{9,8},{10,11... | collective-permute-start | bytes 2752520 | tf_op jit(solution)/shard_map/ppermute | solution.py:78
  61.9 15.7 %collective-permute-start.13 = (bf16[128,3584]{1,0:T(8,128)(2,1)S(1)}, bf16[128,3584]{1,0:T(8,128)(2,1)S(1)}, u32[]{:S(2)}, u32[]{:S(2)}) collective-permute-start(bf16[128,3584]{1,0:T(8,128)(2,1)S(1)} %get-tuple-element.46), channel_id=1, source_target_pairs={{0,1},{1,0},{2,3},{3,2},{4,5},{5,4},{6,7},{7,6},{8,9},{9,8},{10,11... | collective-permute-start | bytes 2752520 | tf_op jit(solution)/shard_map/ppermute | solution.py:78
  62.2 5.4 %collective-permute-start.18 = (bf16[128,3584]{1,0:T(8,128)(2,1)S(1)}, bf16[128,3584]{1,0:T(8,128)(2,1)S(1)}, u32[]{:S(2)}, u32[]{:S(2)}) collective-permute-start(bf16[128,3584]{1,0:T(8,128)(2,1)S(1)} %get-tuple-element.52), channel_id=1, source_target_pairs={{0,1},{1,0},{2,3},{3,2},{4,5},{5,4},{6,7},{7,6},{8,9},{9,8},{10,11... | collective-permute-start | bytes 2752520 | tf_op jit(solution)/shard_map/ppermute | solution.py:78
  63.2 7.7 %collective-permute-start.22 = (bf16[32,3584]{1,0:T(8,128)(2,1)S(1)}, bf16[32,3584]{1,0:T(8,128)(2,1)S(1)}, u32[]{:S(2)}, u32[]{:S(2)}) collective-permute-start(bf16[32,3584]{1,0:T(8,128)(2,1)S(1)} %get-tuple-element.67), channel_id=1, source_target_pairs={{0,4},{4,8},{8,12},{12,14},{14,10},{10,6},{6,2},{2,0},{1,5},{5,9},... | collective-permute-start | bytes 688136 | tf_op jit(solution)/shard_map/ppermute | solution.py:75
  67.6 7.7 %collective-permute-start.26 = (bf16[32,3584]{1,0:T(8,128)(2,1)S(1)}, bf16[32,3584]{1,0:T(8,128)(2,1)S(1)}, u32[]{:S(2)}, u32[]{:S(2)}) collective-permute-start(bf16[32,3584]{1,0:T(8,128)(2,1)S(1)} %get-tuple-element.68), channel_id=1, source_target_pairs={{0,2},{4,0},{8,4},{12,8},{14,12},{10,14},{6,10},{2,6},{1,3},{5,1},... | collective-permute-start | bytes 688136 | tf_op jit(solution)/shard_map/ppermute | solution.py:75
  75.5 11.8 %collective-permute-start.23 = (bf16[64,3584]{1,0:T(8,128)(2,1)S(1)}, bf16[64,3584]{1,0:T(8,128)(2,1)S(1)}, u32[]{:S(2)}, u32[]{:S(2)}) collective-permute-start(bf16[64,3584]{1,0:T(8,128)(2,1)S(1)} %pad_maximum_fusion), channel_id=1, source_target_pairs={{0,4},{4,8},{8,12},{12,14},{14,10},{10,6},{6,2},{2,0},{1,5},{5,9},... | collective-permute-start | bytes 1376264 | tf_op jit(solution)/shard_map/ppermute | solution.py:75
  76.1 11.5 %collective-permute-start.27 = (bf16[64,3584]{1,0:T(8,128)(2,1)S(1)}, bf16[64,3584]{1,0:T(8,128)(2,1)S(1)}, u32[]{:S(2)}, u32[]{:S(2)}) collective-permute-start(bf16[64,3584]{1,0:T(8,128)(2,1)S(1)} %pad_maximum_fusion.1), channel_id=1, source_target_pairs={{0,2},{4,0},{8,4},{12,8},{14,12},{10,14},{6,10},{2,6},{1,3},{5,1},... | collective-permute-start | bytes 1376264 | tf_op jit(solution)/shard_map/ppermute | solution.py:75
  87.8 10.6 %collective-permute-start.24 = (bf16[64,3584]{1,0:T(8,128)(2,1)S(1)}, bf16[64,3584]{1,0:T(8,128)(2,1)S(1)}, u32[]{:S(2)}, u32[]{:S(2)}) collective-permute-start(bf16[64,3584]{1,0:T(8,128)(2,1)S(1)} %get-tuple-element.61), channel_id=1, source_target_pairs={{0,4},{4,8},{8,12},{12,14},{14,10},{10,6},{6,2},{2,0},{1,5},{5,9},... | collective-permute-start | bytes 1376264 | tf_op jit(solution)/shard_map/ppermute | solution.py:75
  88.2 10.4 %collective-permute-start.28 = (bf16[64,3584]{1,0:T(8,128)(2,1)S(1)}, bf16[64,3584]{1,0:T(8,128)(2,1)S(1)}, u32[]{:S(2)}, u32[]{:S(2)}) collective-permute-start(bf16[64,3584]{1,0:T(8,128)(2,1)S(1)} %get-tuple-element.62), channel_id=1, source_target_pairs={{0,2},{4,0},{8,4},{12,8},{14,12},{10,14},{6,10},{2,6},{1,3},{5,1},... | collective-permute-start | bytes 1376264 | tf_op jit(solution)/shard_map/ppermute | solution.py:75
  98.8 9.6 %collective-permute-start.29 = (bf16[64,3584]{1,0:T(8,128)(2,1)S(1)}, bf16[64,3584]{1,0:T(8,128)(2,1)S(1)}, u32[]{:S(2)}, u32[]{:S(2)}) collective-permute-start(bf16[64,3584]{1,0:T(8,128)(2,1)S(1)} %get-tuple-element.60), channel_id=1, source_target_pairs={{0,2},{4,0},{8,4},{12,8},{14,12},{10,14},{6,10},{2,6},{1,3},{5,1},... | collective-permute-start | bytes 1376264 | tf_op jit(solution)/shard_map/ppermute | solution.py:75
  100.5 9.0 %collective-permute-start.25 = (bf16[64,3584]{1,0:T(8,128)(2,1)S(1)}, bf16[64,3584]{1,0:T(8,128)(2,1)S(1)}, u32[]{:S(2)}, u32[]{:S(2)}) collective-permute-start(bf16[64,3584]{1,0:T(8,128)(2,1)S(1)} %get-tuple-element.59), channel_id=1, source_target_pairs={{0,4},{4,8},{8,12},{12,14},{14,10},{10,6},{6,2},{2,0},{1,5},{5,9},... | collective-permute-start | bytes 1376264 | tf_op jit(solution)/shard_map/ppermute | solution.py:75

commit v3 on v2

v3 whole, which is shorter than its diff:
```python
import functools

import jax
import jax.numpy as jnp
from jax import lax
from jax.experimental import pallas as pl
from jax.experimental.pallas import tpu as pltpu
from jax.sharding import PartitionSpec as P

TILE = 256
LANES = 128
LEAST_ROWS = 128
VMEM_LIMIT = 12 * 2**20
VMEM = pl.BlockSpec(memory_space=pltpu.VMEM)
PARAMS = pltpu.CompilerParams(vmem_limit_bytes=VMEM_LIMIT)
NO_COST = pl.CostEstimate(flops=0, bytes_accessed=0, transcendentals=0)


def ring_order(node_count, group_count):
    if group_count == 2:
        return list(range(0, node_count, 2)) + list(range(node_count - 1, 0, -2))
    return list(range(node_count))


def message_kernel(n, tokens, routes, message, semaphore):
    rows, width = tokens.shape
    copy = pltpu.make_async_copy(tokens, message.at[:, pl.ds(0, width)], semaphore)
    copy.start()
    lane = lax.broadcasted_iota(jnp.int32, (rows, message.shape[1] - width), 1)
    table = jnp.zeros(lane.shape, jnp.int32)
    for k in range(routes.shape[3]):
        expert, weight = (routes[i, :, :, k : k + 1].reshape(rows, 1) for i in range(2))
        table += jnp.where(lane == expert, weight >> 8, 0) + jnp.where(lane == expert + n, weight & 255, 0)
    message[:, width:] = table.astype(jnp.float32).astype(jnp.bfloat16)
    copy.wait()


def make_message(n, tokens, expert_ids, gate_fixed):
    rows, width = tokens.shape
    routes = jnp.stack([expert_ids, gate_fixed])
    return pl.pallas_call(
        functools.partial(message_kernel, n),
        out_shape=jax.ShapeDtypeStruct((rows, width + -(-2 * n // LANES) * LANES), jnp.bfloat16),
        in_specs=[pl.BlockSpec(memory_space=pl.ANY), VMEM],
        out_specs=VMEM,
        scratch_shapes=[pltpu.SemaphoreType.DMA],
        compiler_params=PARAMS,
        cost_estimate=NO_COST,
    )(tokens, routes)


def experts_kernel(pieces, n, me, *refs):
    inputs, matrices, outputs, (rows, hidden) = refs[:pieces], refs[pieces : pieces + 6], refs[pieces + 6 : -2], refs[-2:]
    width, units = matrices[0].shape
    place = 0
    for piece in inputs:
        rows[pl.ds(place, piece.shape[0])] = piece[...]
        place += piece.shape[0]
    table = rows[:, width:].astype(jnp.float32)
    lane = lax.broadcasted_iota(jnp.int32, table.shape, 1)
    scale = jnp.where(lane == me[0], 1.0 / 256.0, jnp.where(lane == me[0] + n, 1.0 / 65536.0, 0.0))
    factor = jnp.sum(table * scale, axis=1, keepdims=True)
    for side in range(2):
        w_gate, w_up = matrices[3 * side : 3 * side + 2]
        for start in range(0, units, TILE):
            part = pl.ds(start, TILE)
            gate_act = jnp.dot(rows[:, :width], w_gate[:, part], preferred_element_type=jnp.float32)
            up_act = jnp.dot(rows[:, :width], w_up[:, part], preferred_element_type=jnp.float32)
            silu = gate_act / (1.0 + jnp.exp(-gate_act))
            hidden[:, pl.ds(side * units + start, TILE)] = (silu * up_act * factor).astype(jnp.bfloat16)
    for start in range(0, width, TILE):
        part = pl.ds(start, TILE)
        product = jnp.dot(hidden[:, :units], matrices[2][:, part], preferred_element_type=jnp.float32)
        product += jnp.dot(hidden[:, units:], matrices[5][:, part], preferred_element_type=jnp.float32)
        place = 0
        for output in outputs:
            output[:, part] = product[place : place + output.shape[0]].astype(output.dtype)
            place += output.shape[0]


def run_experts(inputs, kinds, me, n, matrices):
    total, message = sum(x.shape[0] for x in inputs), inputs[0].shape[1]
    width, units = matrices[0].shape
    held = max(total, LEAST_ROWS)
    return pl.pallas_call(
        functools.partial(experts_kernel, len(inputs), n),
        out_shape=[jax.ShapeDtypeStruct((total // len(kinds), width), kind) for kind in kinds],
        in_specs=[pl.BlockSpec(memory_space=pltpu.SMEM)] + [VMEM] * (len(inputs) + 6),
        out_specs=[VMEM] * len(kinds),
        scratch_shapes=[pltpu.VMEM((held, message), jnp.bfloat16), pltpu.VMEM((held, 2 * units), jnp.bfloat16)],
        compiler_params=PARAMS,
        cost_estimate=NO_COST,
    )(me, *inputs, *matrices)


def keep_kernel(source, to, semaphore):
    copy = pltpu.make_async_copy(source, to, semaphore)
    copy.start()
    copy.wait()


def keep(value):
    return pl.pallas_call(
        keep_kernel,
        out_shape=jax.ShapeDtypeStruct(value.shape, value.dtype),
        in_specs=[pl.BlockSpec(memory_space=pl.ANY)],
        out_specs=VMEM,
        scratch_shapes=[pltpu.SemaphoreType.DMA],
        compiler_params=PARAMS,
        cost_estimate=NO_COST,
    )(value)


def add_kernel(*refs):
    refs[-1][...] = sum(ref[...].astype(jnp.float32) for ref in refs[:-1]).astype(jnp.bfloat16)


def add_up(*terms):
    return pl.pallas_call(
        add_kernel,
        out_shape=jax.ShapeDtypeStruct(terms[0].shape, jnp.bfloat16),
        in_specs=[VMEM] * len(terms),
        out_specs=VMEM,
        compiler_params=PARAMS,
        cost_estimate=NO_COST,
    )(*terms)


def finish_kernel(count, *refs):
    terms, out, sums, semaphores = refs[:-3], refs[-3], refs[-2], refs[-1]
    copies = []
    for s in range(count):
        sums[s] = sum(ref[...].astype(jnp.float32) for ref in terms[3 * s : 3 * s + 3]).astype(jnp.bfloat16)
        copies.append(pltpu.make_async_copy(sums.at[s], out.at[s], semaphores.at[s]))
        copies[-1].start()
    for copy in copies:
        copy.wait()


def finish(terms):
    shape = (len(terms), *terms[0][0].shape)
    return pl.pallas_call(
        functools.partial(finish_kernel, len(terms)),
        out_shape=jax.ShapeDtypeStruct(shape, jnp.bfloat16),
        in_specs=[VMEM] * (3 * len(terms)),
        out_specs=pl.BlockSpec(memory_space=pl.ANY),
        scratch_shapes=[pltpu.VMEM(shape, jnp.bfloat16), pltpu.SemaphoreType.DMA((len(terms),))],
        compiler_params=PARAMS,
        cost_estimate=NO_COST,
    )(*sum(terms, ()))


def per_device(order, tokens, expert_ids, gate_fixed, w_gate, w_up, w_down):
    step_count, tok_rows, width = tokens.shape
    steps = range(step_count)
    n = len(order)
    half = n // 2
    me = lax.axis_index("node").astype(jnp.int32).reshape(1)

    def shift(value, distance):
        return lax.ppermute(value, "node", [(order[i], order[(i + distance) % n]) for i in range(n)])

    def swap(value):
        return lax.ppermute(value, "local", [(0, 1), (1, 0)])

    def in_order(*arrays):
        nonlocal me
        me, *arrays = lax.optimization_barrier((me, *arrays))
        return arrays

    def far_ahead(s):
        return s % 2 == 0

    own = make_message(n, tokens.reshape(step_count * tok_rows, width), expert_ids, gate_fixed)
    whole = [shift(own, 1), shift(own, -1)]
    matrices = [w_gate[0], w_up[0], w_down[0]]
    arriving = [swap(matrix) for matrix in matrices]
    outputs = {}

    def load(count):
        for _ in range(count):
            matrices.extend(in_order(keep(*in_order(arriving.pop(0)))))

    def work(names, rows, kinds={}):
        kinds = [kinds.get(name, jnp.float32) for name in names]
        outputs.update(zip(names, in_order(*run_experts(in_order(*rows), kinds, me, n, matrices))))

    load(2)
    whole = in_order(*whole)
    came = {0: ([("own", 0, s) for s in steps], [own]), 1: ([(side, 1, s) for side in ("back", "ahead") for s in steps], whole)}
    plus, minus = {}, {}
    for s in steps:
        part = slice(s * tok_rows, (s + 1) * tok_rows)
        plus[s], minus[s] = shift(whole[0][part], 1), shift(whole[1][part], -1)
    load(1)
    for hop in range(2, half):
        came[hop] = ([], [])
        for s in steps:
            if s == step_count - 1 and hop > 2:
                work(*came.pop(hop - 1))
            plus[s], minus[s] = in_order(plus[s], minus[s])
            came[hop] = (came[hop][0] + [("back", hop, s), ("ahead", hop, s)], came[hop][1] + [plus[s], minus[s]])
            if hop + 1 < half or far_ahead(s):
                plus[s] = shift(plus[s], 1)
            if hop + 1 < half or not far_ahead(s):
                minus[s] = shift(minus[s], -1)
        if hop == 2:
            work(*came.pop(1))
    came[half] = ([("far", half, s) for s in steps], [plus[s] if far_ahead(s) else minus[s] for s in steps])

    longer = {s: ("ahead", 1) if far_ahead(s) else ("back", -1) for s in steps}
    shorter = {s: ("back", -1) if far_ahead(s) else ("ahead", 1) for s in steps}
    long, short = {}, {}
    work(*came[half - 1], {(shorter[s][0], half - 1, s): jnp.bfloat16 for s in steps})
    for s in steps:
        short[s] = shift(outputs[shorter[s][0], half - 1, s], shorter[s][1])
    work(*came[half], {("far", half, s): jnp.bfloat16 for s in steps})
    for s in steps:
        long[s] = shift(outputs["far", half, s], longer[s][1])

    def pass_on(sums, ways, hop):
        for s in steps:
            side, way = ways[s]
            sums[s] = shift(add_up(outputs[side, hop, s], sums[s]), way)

    for hop in range(half - 2, -1, -1):
        if hop == 0:
            outputs.update(zip(came[0][0], run_experts(came[0][1], [jnp.float32] * step_count, me, n, matrices)))
        else:
            pass_on(short, shorter, hop)
        pass_on(long, longer, hop + 1)
    return finish([(outputs["own", 0, s], short[s], long[s]) for s in steps])


def solution(mesh):
    order = ring_order(mesh.shape["node"], mesh.shape["groups"])
    rows = P(None, ("groups", "node", "local"), None)
    in_specs = (rows, rows, rows, P("node", None, "local"), P("node", None, "local"), P("node", "local", None))
    return jax.shard_map(
        functools.partial(per_device, order), mesh=mesh, in_specs=in_specs, out_specs=rows, check_vma=False
    )
```

time: 111 us -> 89.6 us (0.81)
  waiting for transfers between devices: 66.3 us -> 33.6 us
  Pallas kernels: 12.9 us -> 24.9 us
  starting transfers between devices: 20 us -> 28.6 us
  local copies, waits for them, and re-layouts: 7.86 us -> 1.2 us
  other arithmetic: 3.27 us -> 0.71 us
    ppermute x16 -> x26, waiting for transfers between devices: 60.5 us -> 29.3 us  [shift(): lax.ppermute(value, 'node', [(order[i], order[(i + distance) % n]) for i...]
    ppermute x16 -> x26, starting transfers between devices: 16.2 us -> 27.7 us  [shift(): lax.ppermute(value, 'node', [(order[i], order[(i + distance) % n]) for i...]
    pallas_call x0 -> x15, Pallas kernels: none -> 8.13 us  [the longest x3 6.51 us: keep(): pl.pallas_call(keep_kernel, out_shape=jax.ShapeDtypeStruct(value.shape, v...]
    unnamed x10 -> x8, local copies, waits for them, and re-layouts: 7.5 us -> 1.03 us
    pallas_call x5, Pallas kernels: 12.9 us -> 16.7 us  [run_experts(): pl.pallas_call(functools.partial(experts_kernel, len(inputs), n), out_sha...]
    ppermute x14 -> x3, starting transfers between devices: 3.82 us -> 0.96 us  [swap(): return lax.ppermute(value, 'local', [(0, 1), (1, 0)])]
    ppermute x14 -> x3, waiting for transfers between devices: 5.86 us -> 4.32 us  [swap(): return lax.ppermute(value, 'local', [(0, 1), (1, 0)])]
    convert_element_type x4 -> x0, other arithmetic: 1.39 us -> none  [the longest x1 1 us: per_device(): return total.astype(jnp.bfloat16).reshape(tokens.shape)]
  transfers between devices with their start and end apart: 30 -> 29, of which waited for: 20 -> 17; matrix products, arithmetic and copies ran while one was open for 1% -> 1% of each run, Pallas kernels for 10% -> 23%
where the time goes in v3:
time: 89.6 us; the launch traced here: 89.4 us
  waiting for transfers between devices  33.6 us (38%)
  starting transfers between devices  28.6 us (32%)
  Pallas kernels  24.9 us (28%)
  local copies, waits for them, and re-layouts  1.2 us (1%)
    ppermute x26, waiting for transfers between devices, shift(): lax.ppermute(value, 'node', [(order[i], order[(i + distance) % n]) for i...  29.3 us
    ppermute x26, starting transfers between devices, shift(): lax.ppermute(value, 'node', [(order[i], order[(i + distance) % n]) for i...  27.7 us
    pallas_call x5, Pallas kernels, run_experts(): pl.pallas_call(functools.partial(experts_kernel, len(inputs), n), out_sha...  16.7 us
    pallas_call x3, Pallas kernels, keep(): pl.pallas_call(keep_kernel, out_shape=jax.ShapeDtypeStruct(value.shape, v...  6.51 us
    ppermute x3, waiting for transfers between devices, swap(): return lax.ppermute(value, 'local', [(0, 1), (1, 0)])  4.32 us
  transfers between devices with their start and end apart: 29, of which 17 were waited for; matrix products, arithmetic and copies ran while one was open for 1% of the time, Pallas kernels for 23%

profile of v3, /device:TPU:0, one launch (start us, length us, event | category | flops | bytes accessed | tf_op | source)
XLA Modules:
  0.0 89.4 jit_solution(13467280337735866538)
XLA Ops:
  0.0 0.5 collective-permute-start
  0.5 0.5 collective-permute-start.4
  1.0 0.7 pad_add_fusion
  1.8 1.0 %copy-done.3 = bf16[2,32,3584]{2,1,0:T(8,128)(2,1)S(1)} copy-done((bf16[2,32,3584]{2,1,0:T(8,128)(2,1)S(1)}, bf16[2,32,3584]{2,1,0:T(8,128)(2,1)}, u32[]{:S(2)}) %copy-start.3) | copy-done | bytes 458776
  3.1 2.6 %collective-permute-start.2 = (bf16[64,3712]{1,0:T(8,128)(2,1)S(1)}, bf16[64,3712]{1,0:T(8,128)(2,1)S(1)}, u32[]{:S(2)}, u32[]{:S(2)}) collective-permute-start(bf16[64,3712]{1,0:T(8,128)(2,1)S(1)} %shard_map.66.refs_0_), channel_id=1, source_target_pairs={{0,4},{4,8},{8,12},{12,14},{14,10},{10,6},{6,2},{2,0},{1,5},{5,9},... | collective-permute-start | bytes 1425416 | tf_op jit(solution)/shard_map/ppermute | solution.py:161
  5.7 1.1 %collective-permute-done.source = bf16[3584,512]{1,0:T(8,128)(2,1)} collective-permute-done((bf16[3584,512]{1,0:T(8,128)(2,1)}, bf16[3584,512]{1,0:T(8,128)(2,1)}, u32[]{:S(2)}, u32[]{:S(2)}) %collective-permute-start) | collective-permute-done | bytes 3670048 | tf_op jit(solution)/shard_map/ppermute | solution.py:164
  6.8 2.0 %shard_map.64.refs_5_.refs_7_.refs_4_ = bf16[3584,512]{1,0:T(8,128)(2,1)S(1)} custom-call(bf16[3584,512]{1,0:T(8,128)(2,1)} %collective-permute-done.source), custom_call_target="tpu_custom_call" | custom-call | tf_op jit(solution)/shard_map/pallas_call | solution.py:103
  8.9 3.2 %collective-permute-done.1.source = bf16[3584,512]{1,0:T(8,128)(2,1)} collective-permute-done((bf16[3584,512]{1,0:T(8,128)(2,1)}, bf16[3584,512]{1,0:T(8,128)(2,1)}, u32[]{:S(2)}, u32[]{:S(2)}) %collective-permute-start.1) | collective-permute-done | bytes 3670048 | tf_op jit(solution)/shard_map/ppermute | solution.py:164
  12.1 2.2 %shard_map.65.refs_6_.refs_8_.refs_5_ = bf16[3584,512]{1,0:T(8,128)(2,1)S(1)} custom-call(bf16[3584,512]{1,0:T(8,128)(2,1)} %collective-permute-done.1.source), custom_call_target="tpu_custom_call" | custom-call | tf_op jit(solution)/shard_map/pallas_call | solution.py:103
  14.3 2.9 %collective-permute-done.2.refs_0_ = bf16[64,3712]{1,0:T(8,128)(2,1)S(1)} collective-permute-done((bf16[64,3712]{1,0:T(8,128)(2,1)S(1)}, bf16[64,3712]{1,0:T(8,128)(2,1)S(1)}, u32[]{:S(2)}, u32[]{:S(2)}) %collective-permute-start.2) | collective-permute-done | bytes 475168 | tf_op jit(solution)/shard_map/ppermute | solution.py:161
  17.2 1.5 %collective-permute-done.3.refs_1_ = bf16[64,3712]{1,0:T(8,128)(2,1)S(1)} collective-permute-done((bf16[64,3712]{1,0:T(8,128)(2,1)S(1)}, bf16[64,3712]{1,0:T(8,128)(2,1)S(1)}, u32[]{:S(2)}, u32[]{:S(2)}) %collective-permute-start.3) | collective-permute-done | bytes 475168 | tf_op jit(solution)/shard_map/ppermute | solution.py:161
  18.7 1.6 %collective-permute-start.5 = (bf16[32,3712]{1,0:T(8,128)(2,1)S(1)}, bf16[32,3712]{1,0:T(8,128)(2,1)S(1)}, u32[]{:S(2)}, u32[]{:S(2)}) collective-permute-start(bf16[32,3712]{1,0:T(8,128)(2,1)S(1)} %get-tuple-element.162), channel_id=1, source_target_pairs={{0,4},{4,8},{8,12},{12,14},{14,10},{10,6},{6,2},{2,0},{1,5},{5,9},... | collective-permute-start | bytes 712712 | tf_op jit(solution)/shard_map/ppermute | solution.py:161
  20.4 0.5 collective-permute-start.6
  20.9 1.6 %collective-permute-start.7 = (bf16[32,3712]{1,0:T(8,128)(2,1)S(1)}, bf16[32,3712]{1,0:T(8,128)(2,1)S(1)}, u32[]{:S(2)}, u32[]{:S(2)}) collective-permute-start(bf16[32,3712]{1,0:T(8,128)(2,1)S(1)} %get-tuple-element.161), channel_id=1, source_target_pairs={{0,4},{4,8},{8,12},{12,14},{14,10},{10,6},{6,2},{2,0},{1,5},{5,9},... | collective-permute-start | bytes 712712 | tf_op jit(solution)/shard_map/ppermute | solution.py:161
  22.5 0.4 collective-permute-start.8
  22.9 2.3 %shard_map.67.refs_7_.refs_9_.refs_6_ = bf16[512,3584]{1,0:T(8,128)(2,1)S(1)} custom-call(bf16[512,3584]{1,0:T(8,128)(2,1)} %collective-permute-done.4.source), custom_call_target="tpu_custom_call" | custom-call | tf_op jit(solution)/shard_map/pallas_call | solution.py:103
  25.2 2.3 %collective-permute-done.5.refs_0_ = bf16[32,3712]{1,0:T(8,128)(2,1)S(1)} collective-permute-done((bf16[32,3712]{1,0:T(8,128)(2,1)S(1)}, bf16[32,3712]{1,0:T(8,128)(2,1)S(1)}, u32[]{:S(2)}, u32[]{:S(2)}) %collective-permute-start.5) | collective-permute-done | bytes 237600 | tf_op jit(solution)/shard_map/ppermute | solution.py:161
  27.5 1.7 %collective-permute-done.6.refs_1_ = bf16[32,3712]{1,0:T(8,128)(2,1)S(1)} collective-permute-done((bf16[32,3712]{1,0:T(8,128)(2,1)S(1)}, bf16[32,3712]{1,0:T(8,128)(2,1)S(1)}, u32[]{:S(2)}, u32[]{:S(2)}) %collective-permute-start.6) | collective-permute-done | bytes 237600 | tf_op jit(solution)/shard_map/ppermute | solution.py:161
  29.2 0.4 collective-permute-start.10
  29.6 1.6 %collective-permute-start.9 = (bf16[32,3712]{1,0:T(8,128)(2,1)S(1)}, bf16[32,3712]{1,0:T(8,128)(2,1)S(1)}, u32[]{:S(2)}, u32[]{:S(2)}) collective-permute-start(bf16[32,3712]{1,0:T(8,128)(2,1)S(1)} %collective-permute-done.5.refs_0_), channel_id=1, source_target_pairs={{0,4},{4,8},{8,12},{12,14},{14,10},{10,6},{6,2},{2,0},{1,5},{5,9},... | collective-permute-start | bytes 712712 | tf_op jit(solution)/shard_map/ppermute | solution.py:161
  31.2 1.4 %collective-permute-done.7.refs_2_ = bf16[32,3712]{1,0:T(8,128)(2,1)S(1)} collective-permute-done((bf16[32,3712]{1,0:T(8,128)(2,1)S(1)}, bf16[32,3712]{1,0:T(8,128)(2,1)S(1)}, u32[]{:S(2)}, u32[]{:S(2)}) %collective-permute-start.7) | collective-permute-done | bytes 237600 | tf_op jit(solution)/shard_map/ppermute | solution.py:161
  32.6 1.7 %collective-permute-done.8.refs_3_ = bf16[32,3712]{1,0:T(8,128)(2,1)S(1)} collective-permute-done((bf16[32,3712]{1,0:T(8,128)(2,1)S(1)}, bf16[32,3712]{1,0:T(8,128)(2,1)S(1)}, u32[]{:S(2)}, u32[]{:S(2)}) %collective-permute-start.8) | collective-permute-done | bytes 237600 | tf_op jit(solution)/shard_map/ppermute | solution.py:161
  34.3 1.6 %collective-permute-start.11 = (bf16[32,3712]{1,0:T(8,128)(2,1)S(1)}, bf16[32,3712]{1,0:T(8,128)(2,1)S(1)}, u32[]{:S(2)}, u32[]{:S(2)}) collective-permute-start(bf16[32,3712]{1,0:T(8,128)(2,1)S(1)} %collective-permute-done.7.refs_2_), channel_id=1, source_target_pairs={{0,4},{4,8},{8,12},{12,14},{14,10},{10,6},{6,2},{2,0},{1,5},{5,9},... | collective-permute-start | bytes 712712 | tf_op jit(solution)/shard_map/ppermute | solution.py:161
  36.3 3.4 %shard_map.68 = (f32[32,3584]{1,0:T(8,128)S(1)}, f32[32,3584]{1,0:T(8,128)S(1)}, f32[32,3584]{1,0:T(8,128)S(1)}, f32[32,3584]{1,0:T(8,128)S(1)}) custom-call(s32[1]{0:T(128)} %bitcast.me, bf16[64,3712]{1,0:T(8,128)(2,1)S(1)} %collective-permute-done.2.refs_0_, bf16[64,3712]{1,0:T(8,128)(2,1)S(1)} %collective-permute-done.3.refs_1_, ...), custom_call_target="tpu_custom_call" | custom-call | tf_op jit(solution)/shard_map/pallas_call | solution.py:85
  39.7 3.3 %shard_map.69 = (f32[32,3584]{1,0:T(8,128)S(1)}, f32[32,3584]{1,0:T(8,128)S(1)}, f32[32,3584]{1,0:T(8,128)S(1)}, f32[32,3584]{1,0:T(8,128)S(1)}) custom-call(s32[1]{0:T(128)} %bitcast.me, bf16[32,3712]{1,0:T(8,128)(2,1)S(1)} %collective-permute-done.5.refs_0_, bf16[32,3712]{1,0:T(8,128)(2,1)S(1)} %collective-permute-done.6.refs_1_, ...), custom_call_target="tpu_custom_call" | custom-call | tf_op jit(solution)/shard_map/pallas_call | solution.py:85
  43.0 0.5 collective-permute-start.14
  43.5 1.6 %collective-permute-start.13 = (bf16[32,3712]{1,0:T(8,128)(2,1)S(1)}, bf16[32,3712]{1,0:T(8,128)(2,1)S(1)}, u32[]{:S(2)}, u32[]{:S(2)}) collective-permute-start(bf16[32,3712]{1,0:T(8,128)(2,1)S(1)} %collective-permute-done.9.refs_0_), channel_id=1, source_target_pairs={{0,4},{4,8},{8,12},{12,14},{14,10},{10,6},{6,2},{2,0},{1,5},{5,9},... | collective-permute-start | bytes 712712 | tf_op jit(solution)/shard_map/ppermute | solution.py:161
  45.1 3.3 %shard_map.70 = (bf16[32,3584]{1,0:T(8,128)(2,1)S(1)}, f32[32,3584]{1,0:T(8,128)S(1)}, f32[32,3584]{1,0:T(8,128)S(1)}, bf16[32,3584]{1,0:T(8,128)(2,1)S(1)}) custom-call(s32[1]{0:T(128)} %bitcast.me, bf16[32,3712]{1,0:T(8,128)(2,1)S(1)} %collective-permute-done.9.refs_0_, bf16[32,3712]{1,0:T(8,128)(2,1)S(1)} %collective-permute-done.10.refs_1_, ...), custom_call_target="tpu_custom_call" | custom-call | tf_op jit(solution)/shard_map/pallas_call | solution.py:85
  48.5 0.7 collective-permute-done.14.refs_1_
  49.2 0.4 collective-permute-done.13.refs_0_
  49.7 3.3 %shard_map.71 = (bf16[32,3584]{1,0:T(8,128)(2,1)S(1)}, bf16[32,3584]{1,0:T(8,128)(2,1)S(1)}) custom-call(s32[1]{0:T(128)} %bitcast.me, bf16[32,3712]{1,0:T(8,128)(2,1)S(1)} %collective-permute-done.13.refs_0_, bf16[32,3712]{1,0:T(8,128)(2,1)S(1)} %collective-permute-done.14.refs_1_, bf16[3584,512]{1,0:T(8,128)(2,1)S(1)} %bitcast.11, ...), custom_call_target="tpu_custom_call" | custom-call | tf_op jit(solution)/shard_map/pallas_call | solution.py:85
  53.3 1.7 %collective-permute-start.18 = (bf16[32,3584]{1,0:T(8,128)(2,1)S(1)}, bf16[32,3584]{1,0:T(8,128)(2,1)S(1)}, u32[]{:S(2)}, u32[]{:S(2)}) collective-permute-start(bf16[32,3584]{1,0:T(8,128)(2,1)S(1)} %get-tuple-element.150), channel_id=1, source_target_pairs={{0,4},{4,8},{8,12},{12,14},{14,10},{10,6},{6,2},{2,0},{1,5},{5,9},... | collective-permute-start | bytes 688136 | tf_op jit(solution)/shard_map/ppermute | solution.py:161
  55.1 1.6 %collective-permute-start.22 = (bf16[32,3584]{1,0:T(8,128)(2,1)S(1)}, bf16[32,3584]{1,0:T(8,128)(2,1)S(1)}, u32[]{:S(2)}, u32[]{:S(2)}) collective-permute-start(bf16[32,3584]{1,0:T(8,128)(2,1)S(1)} %get-tuple-element.154), channel_id=1, source_target_pairs={{0,4},{4,8},{8,12},{12,14},{14,10},{10,6},{6,2},{2,0},{1,5},{5,9},... | collective-permute-start | bytes 688136 | tf_op jit(solution)/shard_map/ppermute | solution.py:161
  57.1 4.5 %collective-permute-done.25.refs_1_ = bf16[32,3584]{1,0:T(8,128)(2,1)S(1)} collective-permute-done((bf16[32,3584]{1,0:T(8,128)(2,1)S(1)}, bf16[32,3584]{1,0:T(8,128)(2,1)S(1)}, u32[]{:S(2)}, u32[]{:S(2)}) %collective-permute-start.25) | collective-permute-done | bytes 229408 | tf_op jit(solution)/shard_map/ppermute | solution.py:161
  62.1 1.8 %collective-permute-start.19 = (bf16[32,3584]{1,0:T(8,128)(2,1)S(1)}, bf16[32,3584]{1,0:T(8,128)(2,1)S(1)}, u32[]{:S(2)}, u32[]{:S(2)}) collective-permute-start(bf16[32,3584]{1,0:T(8,128)(2,1)S(1)} %shard_map.75), channel_id=1, source_target_pairs={{0,4},{4,8},{8,12},{12,14},{14,10},{10,6},{6,2},{2,0},{1,5},{5,9},... | collective-permute-start | bytes 688136 | tf_op jit(solution)/shard_map/ppermute | solution.py:161
  63.8 3.0 %collective-permute-done.22.refs_1_ = bf16[32,3584]{1,0:T(8,128)(2,1)S(1)} collective-permute-done((bf16[32,3584]{1,0:T(8,128)(2,1)S(1)}, bf16[32,3584]{1,0:T(8,128)(2,1)S(1)}, u32[]{:S(2)}, u32[]{:S(2)}) %collective-permute-start.22) | collective-permute-done | bytes 229408 | tf_op jit(solution)/shard_map/ppermute | solution.py:161
  66.9 1.7 %collective-permute-start.23 = (bf16[32,3584]{1,0:T(8,128)(2,1)S(1)}, bf16[32,3584]{1,0:T(8,128)(2,1)S(1)}, u32[]{:S(2)}, u32[]{:S(2)}) collective-permute-start(bf16[32,3584]{1,0:T(8,128)(2,1)S(1)} %shard_map.78), channel_id=1, source_target_pairs={{0,4},{4,8},{8,12},{12,14},{14,10},{10,6},{6,2},{2,0},{1,5},{5,9},... | collective-permute-start | bytes 688136 | tf_op jit(solution)/shard_map/ppermute | solution.py:161
  69.1 2.4 %collective-permute-done.26.refs_1_ = bf16[32,3584]{1,0:T(8,128)(2,1)S(1)} collective-permute-done((bf16[32,3584]{1,0:T(8,128)(2,1)S(1)}, bf16[32,3584]{1,0:T(8,128)(2,1)S(1)}, u32[]{:S(2)}, u32[]{:S(2)}) %collective-permute-start.26) | collective-permute-done | bytes 229408 | tf_op jit(solution)/shard_map/ppermute | solution.py:161
  71.9 1.8 %collective-permute-start.20 = (bf16[32,3584]{1,0:T(8,128)(2,1)S(1)}, bf16[32,3584]{1,0:T(8,128)(2,1)S(1)}, u32[]{:S(2)}, u32[]{:S(2)}) collective-permute-start(bf16[32,3584]{1,0:T(8,128)(2,1)S(1)} %shard_map.76), channel_id=1, source_target_pairs={{0,4},{4,8},{8,12},{12,14},{14,10},{10,6},{6,2},{2,0},{1,5},{5,9},... | collective-permute-start | bytes 688136 | tf_op jit(solution)/shard_map/ppermute | solution.py:161
  73.7 3.0 %collective-permute-done.23.refs_1_ = bf16[32,3584]{1,0:T(8,128)(2,1)S(1)} collective-permute-done((bf16[32,3584]{1,0:T(8,128)(2,1)S(1)}, bf16[32,3584]{1,0:T(8,128)(2,1)S(1)}, u32[]{:S(2)}, u32[]{:S(2)}) %collective-permute-start.23) | collective-permute-done | bytes 229408 | tf_op jit(solution)/shard_map/ppermute | solution.py:161
  76.7 1.7 %collective-permute-start.24 = (bf16[32,3584]{1,0:T(8,128)(2,1)S(1)}, bf16[32,3584]{1,0:T(8,128)(2,1)S(1)}, u32[]{:S(2)}, u32[]{:S(2)}) collective-permute-start(bf16[32,3584]{1,0:T(8,128)(2,1)S(1)} %shard_map.79), channel_id=1, source_target_pairs={{0,4},{4,8},{8,12},{12,14},{14,10},{10,6},{6,2},{2,0},{1,5},{5,9},... | collective-permute-start | bytes 688136 | tf_op jit(solution)/shard_map/ppermute | solution.py:161
  78.9 2.8 %collective-permute-done.27.refs_1_ = bf16[32,3584]{1,0:T(8,128)(2,1)S(1)} collective-permute-done((bf16[32,3584]{1,0:T(8,128)(2,1)S(1)}, bf16[32,3584]{1,0:T(8,128)(2,1)S(1)}, u32[]{:S(2)}, u32[]{:S(2)}) %collective-permute-start.27) | collective-permute-done | bytes 229408 | tf_op jit(solution)/shard_map/ppermute | solution.py:161
  81.7 0.5 collective-permute-start.28
  82.3 1.6 %collective-permute-start.21 = (bf16[32,3584]{1,0:T(8,128)(2,1)S(1)}, bf16[32,3584]{1,0:T(8,128)(2,1)S(1)}, u32[]{:S(2)}, u32[]{:S(2)}) collective-permute-start(bf16[32,3584]{1,0:T(8,128)(2,1)S(1)} %shard_map.77), channel_id=1, source_target_pairs={{0,4},{4,8},{8,12},{12,14},{14,10},{10,6},{6,2},{2,0},{1,5},{5,9},... | collective-permute-start | bytes 688136 | tf_op jit(solution)/shard_map/ppermute | solution.py:161
  83.9 3.3 %shard_map.72 = (f32[32,3584]{1,0:T(8,128)S(1)}, f32[32,3584]{1,0:T(8,128)S(1)}) custom-call(s32[1]{0:T(128)} %bitcast.me, bf16[64,3712]{1,0:T(8,128)(2,1)S(1)} %shard_map.66.refs_0_, bf16[3584,512]{1,0:T(8,128)(2,1)S(1)} %bitcast.12, bf16[3584,512]{1,0:T(8,128)(2,1)S(1)} %bitcast.18, bf16[512,3584]{1,0:T(8,128)(2,1)S(1)} %bitcast.24, ...), custom_call_target="tpu_custom_call" | custom-call | tf_op jit(solution)/shard_map/pallas_call | solution.py:85
  87.3 0.5 collective-permute-done.28.refs_5_
  87.8 0.6 collective-permute-done.21.refs_2_
  88.3 0.8 shard_map.83
  (42 shorter events, 3.8 us)
Async XLA Ops:
  0.0 6.8 %collective-permute-start = (bf16[3584,512]{1,0:T(8,128)(2,1)}, bf16[3584,512]{1,0:T(8,128)(2,1)}, u32[]{:S(2)}, u32[]{:S(2)}) collective-permute-start(bf16[3584,512]{1,0:T(8,128)(2,1)} %bitcast.7), channel_id=1, source_target_pairs={{0,1},{1,0},{2,3},{3,2},{4,5},{5,4},{6,7},{7,6},{8,9},{9,8},{10,11... | collective-permute-start | bytes 11010056 | tf_op jit(solution)/shard_map/ppermute | solution.py:164
  0.5 11.6 %collective-permute-start.1 = (bf16[3584,512]{1,0:T(8,128)(2,1)}, bf16[3584,512]{1,0:T(8,128)(2,1)}, u32[]{:S(2)}, u32[]{:S(2)}) collective-permute-start(bf16[3584,512]{1,0:T(8,128)(2,1)} %bitcast.13), channel_id=1, source_target_pairs={{0,1},{1,0},{2,3},{3,2},{4,5},{5,4},{6,7},{7,6},{8,9},{9,8},{10,11... | collective-permute-start | bytes 11010056 | tf_op jit(solution)/shard_map/ppermute | solution.py:164
  0.5 22.4 %collective-permute-start.4 = (bf16[512,3584]{1,0:T(8,128)(2,1)}, bf16[512,3584]{1,0:T(8,128)(2,1)}, u32[]{:S(2)}, u32[]{:S(2)}) collective-permute-start(bf16[512,3584]{1,0:T(8,128)(2,1)} %bitcast.19), channel_id=1, source_target_pairs={{0,1},{1,0},{2,3},{3,2},{4,5},{5,4},{6,7},{7,6},{8,9},{9,8},{10,11... | collective-permute-start | bytes 11010056 | tf_op jit(solution)/shard_map/ppermute | solution.py:164
  1.8 1.0 %copy-start.3 = (bf16[2,32,3584]{2,1,0:T(8,128)(2,1)S(1)}, bf16[2,32,3584]{2,1,0:T(8,128)(2,1)}, u32[]{:S(2)}) copy-start(bf16[2,32,3584]{2,1,0:T(8,128)(2,1)} %param.6) | copy-start | bytes 1376260
  3.1 14.1 %collective-permute-start.2 = (bf16[64,3712]{1,0:T(8,128)(2,1)S(1)}, bf16[64,3712]{1,0:T(8,128)(2,1)S(1)}, u32[]{:S(2)}, u32[]{:S(2)}) collective-permute-start(bf16[64,3712]{1,0:T(8,128)(2,1)S(1)} %shard_map.66.refs_0_), channel_id=1, source_target_pairs={{0,4},{4,8},{8,12},{12,14},{14,10},{10,6},{6,2},{2,0},{1,5},{5,9},... | collective-permute-start | bytes 1425416 | tf_op jit(solution)/shard_map/ppermute | solution.py:161
  5.7 13.0 %collective-permute-start.3 = (bf16[64,3712]{1,0:T(8,128)(2,1)S(1)}, bf16[64,3712]{1,0:T(8,128)(2,1)S(1)}, u32[]{:S(2)}, u32[]{:S(2)}) collective-permute-start(bf16[64,3712]{1,0:T(8,128)(2,1)S(1)} %shard_map.66.refs_0_), channel_id=1, source_target_pairs={{0,2},{4,0},{8,4},{12,8},{14,12},{10,14},{6,10},{2,6},{1,3},{5,1},... | collective-permute-start | bytes 1425416 | tf_op jit(solution)/shard_map/ppermute | solution.py:161
  12.1 24.2 %copy-start.2 = (bf16[1,512,3584]{2,1,0:T(8,128)(2,1)S(1)}, bf16[1,512,3584]{2,1,0:T(8,128)(2,1)}, u32[]{:S(2)}) copy-start(bf16[1,512,3584]{2,1,0:T(8,128)(2,1)} %param.11) | copy-start | bytes 11010052
  18.7 8.8 %collective-permute-start.5 = (bf16[32,3712]{1,0:T(8,128)(2,1)S(1)}, bf16[32,3712]{1,0:T(8,128)(2,1)S(1)}, u32[]{:S(2)}, u32[]{:S(2)}) collective-permute-start(bf16[32,3712]{1,0:T(8,128)(2,1)S(1)} %get-tuple-element.162), channel_id=1, source_target_pairs={{0,4},{4,8},{8,12},{12,14},{14,10},{10,6},{6,2},{2,0},{1,5},{5,9},... | collective-permute-start | bytes 712712 | tf_op jit(solution)/shard_map/ppermute | solution.py:161
  20.4 8.8 %collective-permute-start.6 = (bf16[32,3712]{1,0:T(8,128)(2,1)S(1)}, bf16[32,3712]{1,0:T(8,128)(2,1)S(1)}, u32[]{:S(2)}, u32[]{:S(2)}) collective-permute-start(bf16[32,3712]{1,0:T(8,128)(2,1)S(1)} %get-tuple-element.160), channel_id=1, source_target_pairs={{0,2},{4,0},{8,4},{12,8},{14,12},{10,14},{6,10},{2,6},{1,3},{5,1},... | collective-permute-start | bytes 712712 | tf_op jit(solution)/shard_map/ppermute | solution.py:161
  20.9 11.7 %collective-permute-start.7 = (bf16[32,3712]{1,0:T(8,128)(2,1)S(1)}, bf16[32,3712]{1,0:T(8,128)(2,1)S(1)}, u32[]{:S(2)}, u32[]{:S(2)}) collective-permute-start(bf16[32,3712]{1,0:T(8,128)(2,1)S(1)} %get-tuple-element.161), channel_id=1, source_target_pairs={{0,4},{4,8},{8,12},{12,14},{14,10},{10,6},{6,2},{2,0},{1,5},{5,9},... | collective-permute-start | bytes 712712 | tf_op jit(solution)/shard_map/ppermute | solution.py:161
  22.5 13.8 %copy-start = (bf16[1,3584,512]{2,1,0:T(8,128)(2,1)S(1)}, bf16[1,3584,512]{2,1,0:T(8,128)(2,1)}, u32[]{:S(2)}) copy-start(bf16[1,3584,512]{2,1,0:T(8,128)(2,1)} %param.9) | copy-start | bytes 11010052
  22.5 13.8 %copy-start.1 = (bf16[1,3584,512]{2,1,0:T(8,128)(2,1)S(1)}, bf16[1,3584,512]{2,1,0:T(8,128)(2,1)}, u32[]{:S(2)}) copy-start(bf16[1,3584,512]{2,1,0:T(8,128)(2,1)} %param.10) | copy-start | bytes 11010052
  22.5 11.8 %collective-permute-start.8 = (bf16[32,3712]{1,0:T(8,128)(2,1)S(1)}, bf16[32,3712]{1,0:T(8,128)(2,1)S(1)}, u32[]{:S(2)}, u32[]{:S(2)}) collective-permute-start(bf16[32,3712]{1,0:T(8,128)(2,1)S(1)} %get-tuple-element.159), channel_id=1, source_target_pairs={{0,2},{4,0},{8,4},{12,8},{14,12},{10,14},{6,10},{2,6},{1,3},{5,1},... | collective-permute-start | bytes 712712 | tf_op jit(solution)/shard_map/ppermute | solution.py:161
  29.2 10.5 %collective-permute-start.10 = (bf16[32,3712]{1,0:T(8,128)(2,1)S(1)}, bf16[32,3712]{1,0:T(8,128)(2,1)S(1)}, u32[]{:S(2)}, u32[]{:S(2)}) collective-permute-start(bf16[32,3712]{1,0:T(8,128)(2,1)S(1)} %collective-permute-done.6.refs_1_), channel_id=1, source_target_pairs={{0,2},{4,0},{8,4},{12,8},{14,12},{10,14},{6,10},{2,6},{1,3},{5,1},... | collective-permute-start | bytes 712712 | tf_op jit(solution)/shard_map/ppermute | solution.py:161
  29.6 10.1 %collective-permute-start.9 = (bf16[32,3712]{1,0:T(8,128)(2,1)S(1)}, bf16[32,3712]{1,0:T(8,128)(2,1)S(1)}, u32[]{:S(2)}, u32[]{:S(2)}) collective-permute-start(bf16[32,3712]{1,0:T(8,128)(2,1)S(1)} %collective-permute-done.5.refs_0_), channel_id=1, source_target_pairs={{0,4},{4,8},{8,12},{12,14},{14,10},{10,6},{6,2},{2,0},{1,5},{5,9},... | collective-permute-start | bytes 712712 | tf_op jit(solution)/shard_map/ppermute | solution.py:161
  34.3 8.8 %collective-permute-start.11 = (bf16[32,3712]{1,0:T(8,128)(2,1)S(1)}, bf16[32,3712]{1,0:T(8,128)(2,1)S(1)}, u32[]{:S(2)}, u32[]{:S(2)}) collective-permute-start(bf16[32,3712]{1,0:T(8,128)(2,1)S(1)} %collective-permute-done.7.refs_2_), channel_id=1, source_target_pairs={{0,4},{4,8},{8,12},{12,14},{14,10},{10,6},{6,2},{2,0},{1,5},{5,9},... | collective-permute-start | bytes 712712 | tf_op jit(solution)/shard_map/ppermute | solution.py:161
  35.8 7.2 %collective-permute-start.12 = (bf16[32,3712]{1,0:T(8,128)(2,1)S(1)}, bf16[32,3712]{1,0:T(8,128)(2,1)S(1)}, u32[]{:S(2)}, u32[]{:S(2)}) collective-permute-start(bf16[32,3712]{1,0:T(8,128)(2,1)S(1)} %collective-permute-done.8.refs_3_), channel_id=1, source_target_pairs={{0,2},{4,0},{8,4},{12,8},{14,12},{10,14},{6,10},{2,6},{1,3},{5,1},... | collective-permute-start | bytes 712712 | tf_op jit(solution)/shard_map/ppermute | solution.py:161
  43.0 6.2 %collective-permute-start.14 = (bf16[32,3712]{1,0:T(8,128)(2,1)S(1)}, bf16[32,3712]{1,0:T(8,128)(2,1)S(1)}, u32[]{:S(2)}, u32[]{:S(2)}) collective-permute-start(bf16[32,3712]{1,0:T(8,128)(2,1)S(1)} %collective-permute-done.12.refs_3_), channel_id=1, source_target_pairs={{0,2},{4,0},{8,4},{12,8},{14,12},{10,14},{6,10},{2,6},{1,3},{5,1},... | collective-permute-start | bytes 712712 | tf_op jit(solution)/shard_map/ppermute | solution.py:161
  43.5 6.1 %collective-permute-start.13 = (bf16[32,3712]{1,0:T(8,128)(2,1)S(1)}, bf16[32,3712]{1,0:T(8,128)(2,1)S(1)}, u32[]{:S(2)}, u32[]{:S(2)}) collective-permute-start(bf16[32,3712]{1,0:T(8,128)(2,1)S(1)} %collective-permute-done.9.refs_0_), channel_id=1, source_target_pairs={{0,4},{4,8},{8,12},{12,14},{14,10},{10,6},{6,2},{2,0},{1,5},{5,9},... | collective-permute-start | bytes 712712 | tf_op jit(solution)/shard_map/ppermute | solution.py:161
  53.0 8.6 %collective-permute-start.25 = (bf16[32,3584]{1,0:T(8,128)(2,1)S(1)}, bf16[32,3584]{1,0:T(8,128)(2,1)S(1)}, u32[]{:S(2)}, u32[]{:S(2)}) collective-permute-start(bf16[32,3584]{1,0:T(8,128)(2,1)S(1)} %get-tuple-element.158), channel_id=1, source_target_pairs={{0,2},{4,0},{8,4},{12,8},{14,12},{10,14},{6,10},{2,6},{1,3},{5,1},... | collective-permute-start | bytes 688136 | tf_op jit(solution)/shard_map/ppermute | solution.py:161
  53.3 8.7 %collective-permute-start.18 = (bf16[32,3584]{1,0:T(8,128)(2,1)S(1)}, bf16[32,3584]{1,0:T(8,128)(2,1)S(1)}, u32[]{:S(2)}, u32[]{:S(2)}) collective-permute-start(bf16[32,3584]{1,0:T(8,128)(2,1)S(1)} %get-tuple-element.150), channel_id=1, source_target_pairs={{0,4},{4,8},{8,12},{12,14},{14,10},{10,6},{6,2},{2,0},{1,5},{5,9},... | collective-permute-start | bytes 688136 | tf_op jit(solution)/shard_map/ppermute | solution.py:161
  55.1 11.7 %collective-permute-start.22 = (bf16[32,3584]{1,0:T(8,128)(2,1)S(1)}, bf16[32,3584]{1,0:T(8,128)(2,1)S(1)}, u32[]{:S(2)}, u32[]{:S(2)}) collective-permute-start(bf16[32,3584]{1,0:T(8,128)(2,1)S(1)} %get-tuple-element.154), channel_id=1, source_target_pairs={{0,4},{4,8},{8,12},{12,14},{14,10},{10,6},{6,2},{2,0},{1,5},{5,9},... | collective-permute-start | bytes 688136 | tf_op jit(solution)/shard_map/ppermute | solution.py:161
  56.7 11.9 %collective-permute-start.15 = (bf16[32,3584]{1,0:T(8,128)(2,1)S(1)}, bf16[32,3584]{1,0:T(8,128)(2,1)S(1)}, u32[]{:S(2)}, u32[]{:S(2)}) collective-permute-start(bf16[32,3584]{1,0:T(8,128)(2,1)S(1)} %get-tuple-element.146), channel_id=1, source_target_pairs={{0,2},{4,0},{8,4},{12,8},{14,12},{10,14},{6,10},{2,6},{1,3},{5,1},... | collective-permute-start | bytes 688136 | tf_op jit(solution)/shard_map/ppermute | solution.py:161
  61.7 9.8 %collective-permute-start.26 = (bf16[32,3584]{1,0:T(8,128)(2,1)S(1)}, bf16[32,3584]{1,0:T(8,128)(2,1)S(1)}, u32[]{:S(2)}, u32[]{:S(2)}) collective-permute-start(bf16[32,3584]{1,0:T(8,128)(2,1)S(1)} %shard_map.80), channel_id=1, source_target_pairs={{0,2},{4,0},{8,4},{12,8},{14,12},{10,14},{6,10},{2,6},{1,3},{5,1},... | collective-permute-start | bytes 688136 | tf_op jit(solution)/shard_map/ppermute | solution.py:161
  62.1 9.8 %collective-permute-start.19 = (bf16[32,3584]{1,0:T(8,128)(2,1)S(1)}, bf16[32,3584]{1,0:T(8,128)(2,1)S(1)}, u32[]{:S(2)}, u32[]{:S(2)}) collective-permute-start(bf16[32,3584]{1,0:T(8,128)(2,1)S(1)} %shard_map.75), channel_id=1, source_target_pairs={{0,4},{4,8},{8,12},{12,14},{14,10},{10,6},{6,2},{2,0},{1,5},{5,9},... | collective-permute-start | bytes 688136 | tf_op jit(solution)/shard_map/ppermute | solution.py:161
  66.9 9.8 %collective-permute-start.23 = (bf16[32,3584]{1,0:T(8,128)(2,1)S(1)}, bf16[32,3584]{1,0:T(8,128)(2,1)S(1)}, u32[]{:S(2)}, u32[]{:S(2)}) collective-permute-start(bf16[32,3584]{1,0:T(8,128)(2,1)S(1)} %shard_map.78), channel_id=1, source_target_pairs={{0,4},{4,8},{8,12},{12,14},{14,10},{10,6},{6,2},{2,0},{1,5},{5,9},... | collective-permute-start | bytes 688136 | tf_op jit(solution)/shard_map/ppermute | solution.py:161
  68.7 9.8 %collective-permute-start.16 = (bf16[32,3584]{1,0:T(8,128)(2,1)S(1)}, bf16[32,3584]{1,0:T(8,128)(2,1)S(1)}, u32[]{:S(2)}, u32[]{:S(2)}) collective-permute-start(bf16[32,3584]{1,0:T(8,128)(2,1)S(1)} %shard_map.73), channel_id=1, source_target_pairs={{0,2},{4,0},{8,4},{12,8},{14,12},{10,14},{6,10},{2,6},{1,3},{5,1},... | collective-permute-start | bytes 688136 | tf_op jit(solution)/shard_map/ppermute | solution.py:161
  71.5 10.2 %collective-permute-start.27 = (bf16[32,3584]{1,0:T(8,128)(2,1)S(1)}, bf16[32,3584]{1,0:T(8,128)(2,1)S(1)}, u32[]{:S(2)}, u32[]{:S(2)}) collective-permute-start(bf16[32,3584]{1,0:T(8,128)(2,1)S(1)} %shard_map.81), channel_id=1, source_target_pairs={{0,2},{4,0},{8,4},{12,8},{14,12},{10,14},{6,10},{2,6},{1,3},{5,1},... | collective-permute-start | bytes 688136 | tf_op jit(solution)/shard_map/ppermute | solution.py:161
  71.9 10.3 %collective-permute-start.20 = (bf16[32,3584]{1,0:T(8,128)(2,1)S(1)}, bf16[32,3584]{1,0:T(8,128)(2,1)S(1)}, u32[]{:S(2)}, u32[]{:S(2)}) collective-permute-start(bf16[32,3584]{1,0:T(8,128)(2,1)S(1)} %shard_map.76), channel_id=1, source_target_pairs={{0,4},{4,8},{8,12},{12,14},{14,10},{10,6},{6,2},{2,0},{1,5},{5,9},... | collective-permute-start | bytes 688136 | tf_op jit(solution)/shard_map/ppermute | solution.py:161
  76.7 10.5 %collective-permute-start.24 = (bf16[32,3584]{1,0:T(8,128)(2,1)S(1)}, bf16[32,3584]{1,0:T(8,128)(2,1)S(1)}, u32[]{:S(2)}, u32[]{:S(2)}) collective-permute-start(bf16[32,3584]{1,0:T(8,128)(2,1)S(1)} %shard_map.79), channel_id=1, source_target_pairs={{0,4},{4,8},{8,12},{12,14},{14,10},{10,6},{6,2},{2,0},{1,5},{5,9},... | collective-permute-start | bytes 688136 | tf_op jit(solution)/shard_map/ppermute | solution.py:161
  78.5 8.8 %collective-permute-start.17 = (bf16[32,3584]{1,0:T(8,128)(2,1)S(1)}, bf16[32,3584]{1,0:T(8,128)(2,1)S(1)}, u32[]{:S(2)}, u32[]{:S(2)}) collective-permute-start(bf16[32,3584]{1,0:T(8,128)(2,1)S(1)} %shard_map.74), channel_id=1, source_target_pairs={{0,2},{4,0},{8,4},{12,8},{14,12},{10,14},{6,10},{2,6},{1,3},{5,1},... | collective-permute-start | bytes 688136 | tf_op jit(solution)/shard_map/ppermute | solution.py:161
  81.7 6.1 %collective-permute-start.28 = (bf16[32,3584]{1,0:T(8,128)(2,1)S(1)}, bf16[32,3584]{1,0:T(8,128)(2,1)S(1)}, u32[]{:S(2)}, u32[]{:S(2)}) collective-permute-start(bf16[32,3584]{1,0:T(8,128)(2,1)S(1)} %shard_map.82), channel_id=1, source_target_pairs={{0,2},{4,0},{8,4},{12,8},{14,12},{10,14},{6,10},{2,6},{1,3},{5,1},... | collective-permute-start | bytes 688136 | tf_op jit(solution)/shard_map/ppermute | solution.py:161
  82.3 6.1 %collective-permute-start.21 = (bf16[32,3584]{1,0:T(8,128)(2,1)S(1)}, bf16[32,3584]{1,0:T(8,128)(2,1)S(1)}, u32[]{:S(2)}, u32[]{:S(2)}) collective-permute-start(bf16[32,3584]{1,0:T(8,128)(2,1)S(1)} %shard_map.77), channel_id=1, source_target_pairs={{0,4},{4,8},{8,12},{12,14},{14,10},{10,6},{6,2},{2,0},{1,5},{5,9},... | collective-permute-start | bytes 688136 | tf_op jit(solution)/shard_map/ppermute | solution.py:161

commit v4 on v3

--- a/solution.py
+++ b/solution.py
@@ -111,54 +111,65 @@
     )(value)
 
 
-def add_kernel(*refs):
-    refs[-1][...] = sum(ref[...].astype(jnp.float32) for ref in refs[:-1]).astype(jnp.bfloat16)
-
-
-def add_up(*terms):
-    return pl.pallas_call(
-        add_kernel,
-        out_shape=jax.ShapeDtypeStruct(terms[0].shape, jnp.bfloat16),
-        in_specs=[VMEM] * len(terms),
-        out_specs=VMEM,
-        compiler_params=PARAMS,
-        cost_estimate=NO_COST,
-    )(*terms)
-
-
-def finish_kernel(count, *refs):
-    terms, out, sums, semaphores = refs[:-3], refs[-3], refs[-2], refs[-1]
+def add_kernel(places, mine, came, *sums):
+    size = sums[0].shape[0]
+    for place, to in zip(places, sums):
+        here = pl.ds(place * size, size)
+        there = here if came.shape == mine.shape else slice(None)
+        to[...] = (mine[here] + came[there].astype(jnp.float32)).astype(jnp.bfloat16)
+
+
+def add_up(terms, parts=1, only=None):
+    mine, came = terms
+    places = range(parts) if only is None else [only]
+    part = jax.ShapeDtypeStruct((mine.shape[0] // parts, mine.shape[1]), jnp.bfloat16)
+    return pl.pallas_call(
+        functools.partial(add_kernel, places),
+        out_shape=[part] * len(places),
+        in_specs=[VMEM] * 2,
+        out_specs=[VMEM] * len(places),
+        compiler_params=PARAMS,
+        cost_estimate=NO_COST,
+    )(mine, came)
+
+
+def finish_kernel(mine, other, *refs):
+    parts, out, total, semaphores = refs[:-3], refs[-3], refs[-2], refs[-1]
+    size = parts[0].shape[0]
     copies = []
-    for s in range(count):
-        sums[s] = sum(ref[...].astype(jnp.float32) for ref in terms[3 * s : 3 * s + 3]).astype(jnp.bfloat16)
-        copies.append(pltpu.make_async_copy(sums.at[s], out.at[s], semaphores.at[s]))
+    for i, part in enumerate(parts):
+        here = pl.ds(i * size, size)
+        total[here] = (mine[here] + other[here].astype(jnp.float32) + part[...].astype(jnp.float32)).astype(jnp.bfloat16)
+        copies.append(pltpu.make_async_copy(total.at[here], out.at[here], semaphores.at[i]))
         copies[-1].start()
     for copy in copies:
         copy.wait()
 
 
-def finish(terms):
-    shape = (len(terms), *terms[0][0].shape)
-    return pl.pallas_call(
-        functools.partial(finish_kernel, len(terms)),
-        out_shape=jax.ShapeDtypeStruct(shape, jnp.bfloat16),
-        in_specs=[VMEM] * (3 * len(terms)),
+def finish(mine, other, *parts):
+    return pl.pallas_call(
+        finish_kernel,
+        out_shape=jax.ShapeDtypeStruct(mine.shape, jnp.bfloat16),
+        in_specs=[VMEM] * (2 + len(parts)),
         out_specs=pl.BlockSpec(memory_space=pl.ANY),
-        scratch_shapes=[pltpu.VMEM(shape, jnp.bfloat16), pltpu.SemaphoreType.DMA((len(terms),))],
-        compiler_params=PARAMS,
-        cost_estimate=NO_COST,
-    )(*sum(terms, ()))
+        scratch_shapes=[pltpu.VMEM(mine.shape, jnp.bfloat16), pltpu.SemaphoreType.DMA((len(parts),))],
+        compiler_params=PARAMS,
+        cost_estimate=NO_COST,
+    )(mine, other, *parts)
 
 
 def per_device(order, tokens, expert_ids, gate_fixed, w_gate, w_up, w_down):
     step_count, tok_rows, width = tokens.shape
-    steps = range(step_count)
     n = len(order)
     half = n // 2
     me = lax.axis_index("node").astype(jnp.int32).reshape(1)
-
-    def shift(value, distance):
-        return lax.ppermute(value, "node", [(order[i], order[(i + distance) % n]) for i in range(n)])
+    ring = [(2 * order[i] + core, 2 * order[(i + 1 - 2 * core) % n] + core) for i in range(n) for core in range(2)]
+
+    def onward(value):
+        return lax.ppermute(value, ("node", "local"), ring)
+
+    def home(value):
+        return lax.ppermute(value, ("node", "local"), [(to, source) for source, to in ring])
 
     def swap(value):
         return lax.ppermute(value, "local", [(0, 1), (1, 0)])
@@ -168,68 +179,54 @@
         me, *arrays = lax.optimization_barrier((me, *arrays))
         return arrays
 
-    def far_ahead(s):
-        return s % 2 == 0
-
     own = make_message(n, tokens.reshape(step_count * tok_rows, width), expert_ids, gate_fixed)
-    whole = [shift(own, 1), shift(own, -1)]
+    other = swap(own)
+    long, short = onward(own), onward(other)
     matrices = [w_gate[0], w_up[0], w_down[0]]
-    arriving = [swap(matrix) for matrix in matrices]
+    arriving = [swap(lax.optimization_barrier((other, matrix))[1]) for matrix in matrices]
     outputs = {}
 
-    def load(count):
-        for _ in range(count):
-            matrices.extend(in_order(keep(*in_order(arriving.pop(0)))))
-
-    def work(names, rows, kinds={}):
-        kinds = [kinds.get(name, jnp.float32) for name in names]
-        outputs.update(zip(names, in_order(*run_experts(in_order(*rows), kinds, me, n, matrices))))
-
-    load(2)
-    whole = in_order(*whole)
-    came = {0: ([("own", 0, s) for s in steps], [own]), 1: ([(side, 1, s) for side in ("back", "ahead") for s in steps], whole)}
-    plus, minus = {}, {}
-    for s in steps:
-        part = slice(s * tok_rows, (s + 1) * tok_rows)
-        plus[s], minus[s] = shift(whole[0][part], 1), shift(whole[1][part], -1)
-    load(1)
-    for hop in range(2, half):
-        came[hop] = ([], [])
-        for s in steps:
-            if s == step_count - 1 and hop > 2:
-                work(*came.pop(hop - 1))
-            plus[s], minus[s] = in_order(plus[s], minus[s])
-            came[hop] = (came[hop][0] + [("back", hop, s), ("ahead", hop, s)], came[hop][1] + [plus[s], minus[s]])
-            if hop + 1 < half or far_ahead(s):
-                plus[s] = shift(plus[s], 1)
-            if hop + 1 < half or not far_ahead(s):
-                minus[s] = shift(minus[s], -1)
-        if hop == 2:
-            work(*came.pop(1))
-    came[half] = ([("far", half, s) for s in steps], [plus[s] if far_ahead(s) else minus[s] for s in steps])
-
-    longer = {s: ("ahead", 1) if far_ahead(s) else ("back", -1) for s in steps}
-    shorter = {s: ("back", -1) if far_ahead(s) else ("ahead", 1) for s in steps}
-    long, short = {}, {}
-    work(*came[half - 1], {(shorter[s][0], half - 1, s): jnp.bfloat16 for s in steps})
-    for s in steps:
-        short[s] = shift(outputs[shorter[s][0], half - 1, s], shorter[s][1])
-    work(*came[half], {("far", half, s): jnp.bfloat16 for s in steps})
-    for s in steps:
-        long[s] = shift(outputs["far", half, s], longer[s][1])
-
-    def pass_on(sums, ways, hop):
-        for s in steps:
-            side, way = ways[s]
-            sums[s] = shift(add_up(outputs[side, hop, s], sums[s]), way)
-
-    for hop in range(half - 2, -1, -1):
-        if hop == 0:
-            outputs.update(zip(came[0][0], run_experts(came[0][1], [jnp.float32] * step_count, me, n, matrices)))
+    def load():
+        matrices.extend(in_order(keep(*in_order(arriving.pop(0)))))
+
+    def work(hop, kinds, ordered=True):
+        rows = came[hop]
+        results = run_experts(in_order(*rows) if ordered else rows, kinds, me, n, matrices)
+        outputs[hop] = in_order(*results) if ordered else results
+
+    came = {0: [own]}
+    for hop in range(1, half):
+        (first,) = in_order(long)
+        long = onward(first)
+        if hop <= 2:
+            load()
         else:
-            pass_on(short, shorter, hop)
-        pass_on(long, longer, hop + 1)
-    return finish([(outputs["own", 0, s], short[s], long[s]) for s in steps])
+            work(hop - 1, [jnp.float32] * 2)
+        (second,) = in_order(short)
+        if hop + 1 < half:
+            short = onward(second)
+        came[hop] = [first, second]
+        if hop == 1:
+            load()
+        elif hop == 2:
+            work(1, [jnp.float32] * 2)
+    came[half] = [long]
+
+    work(half - 1, [jnp.float32, jnp.bfloat16])
+    short = home(outputs[half - 1][1])
+    work(half, [jnp.bfloat16])
+    long = home(outputs[half][0])
+    for hop in range(half - 1, 0, -1):
+        if hop > 1:
+            short = home(add_up([outputs[hop - 1][1], short])[0])
+        if hop > 2:
+            long = home(add_up([outputs[hop][0], long])[0])
+        elif hop == 2:
+            long = [home(part) for part in add_up([outputs[hop][0], long], 2)]
+        else:
+            long = [home(add_up([outputs[hop][0], part], 2, i)[0]) for i, part in enumerate(long)]
+    work(0, [jnp.float32], False)
+    return finish(outputs[0][0], swap(short), *long).reshape(tokens.shape)
 
 
 def solution(mesh):

time: 89.6 us -> 83.9 us (0.936)
  waiting for transfers between devices: 33.6 us -> 25.8 us
  starting transfers between devices: 28.6 us -> 32.1 us
  Pallas kernels: 24.9 us -> 23.6 us
    ppermute x26 -> x16, waiting for transfers between devices: 29.3 us -> 24.3 us  [the longest x9 16.7 us: home(): lax.ppermute(value, ('node', 'local'), [(to, source) for source, to in ri...]
    ppermute x26 -> x16, starting transfers between devices: 27.7 us -> 30.7 us  [the longest x9 16.1 us: home(): lax.ppermute(value, ('node', 'local'), [(to, source) for source, to in ri...]
    ppermute x3 -> x5, waiting for transfers between devices: 4.32 us -> 1.48 us  [swap(): return lax.ppermute(value, 'local', [(0, 1), (1, 0)])]
    pallas_call x5, Pallas kernels: 16.7 us -> 15.7 us  [run_experts(): pl.pallas_call(functools.partial(experts_kernel, len(inputs), n), out_sha...]
  transfers between devices with their start and end apart: 29 -> 21, of which waited for: 17 -> 13; matrix products, arithmetic and copies ran while one was open for 1% -> 0% of each run, Pallas kernels for 23% -> 27%
where the time goes in v4:
time: 83.9 us; the launch traced here: 83.7 us
  starting transfers between devices  32.1 us (38%)
  waiting for transfers between devices  25.8 us (31%)
  Pallas kernels  23.6 us (28%)
  local copies, waits for them, and re-layouts  1.14 us (1%)
    ppermute x9, waiting for transfers between devices, home(): lax.ppermute(value, ('node', 'local'), [(to, source) for source, to in ri...  16.7 us
    ppermute x9, starting transfers between devices, home(): lax.ppermute(value, ('node', 'local'), [(to, source) for source, to in ri...  16.1 us
    pallas_call x5, Pallas kernels, run_experts(): pl.pallas_call(functools.partial(experts_kernel, len(inputs), n), out_sha...  15.7 us
    ppermute x7, starting transfers between devices, onward(): return lax.ppermute(value, ('node', 'local'), ring)  14.5 us
    ppermute x7, waiting for transfers between devices, onward(): return lax.ppermute(value, ('node', 'local'), ring)  7.68 us
    pallas_call x3, Pallas kernels, keep(): pl.pallas_call(keep_kernel, out_shape=jax.ShapeDtypeStruct(value.shape, v...  6.29 us
  transfers between devices with their start and end apart: 21, of which 13 were waited for; matrix products, arithmetic and copies ran while one was open for 0% of the time, Pallas kernels for 27%

profile of v4, /device:TPU:0, one launch (start us, length us, event | category | flops | bytes accessed | tf_op | source)
XLA Modules:
  0.0 83.7 jit_solution(3381667084413058562)
XLA Ops:
  0.0 0.7 pad_add_fusion
  0.7 0.1 copy.9.routes
  0.8 1.0 %copy-done.3 = bf16[2,32,3584]{2,1,0:T(8,128)(2,1)S(1)} copy-done((bf16[2,32,3584]{2,1,0:T(8,128)(2,1)S(1)}, bf16[2,32,3584]{2,1,0:T(8,128)(2,1)}, u32[]{:S(2)}) %copy-start.3) | copy-done | bytes 458776
  1.8 0.3 shard_map.64.refs_0_
  2.1 0.5 collective-permute-start.1
  2.6 1.5 %collective-permute-done.1 = bf16[64,3712]{1,0:T(8,128)(2,1)S(1)} collective-permute-done((bf16[64,3712]{1,0:T(8,128)(2,1)S(1)}, bf16[64,3712]{1,0:T(8,128)(2,1)S(1)}, u32[]{:S(2)}, u32[]{:S(2)}) %collective-permute-start.1) | collective-permute-done | bytes 475168 | tf_op jit(solution)/shard_map/ppermute | solution.py:175
  4.1 0.4 collective-permute-start.2
  4.5 0.1 collective-permute-start.4
  4.6 0.4 collective-permute-start.6
  5.0 2.7 %collective-permute-start = (bf16[64,3712]{1,0:T(8,128)(2,1)S(1)}, bf16[64,3712]{1,0:T(8,128)(2,1)S(1)}, u32[]{:S(2)}, u32[]{:S(2)}) collective-permute-start(bf16[64,3712]{1,0:T(8,128)(2,1)S(1)} %shard_map.64.refs_0_), channel_id=1, source_target_pairs={{0,4},{1,3},{4,8},{5,1},{8,12},{9,5},{12,14},{13,9},{14,10},{15,13... | collective-permute-start | bytes 1425416 | tf_op jit(solution)/shard_map/ppermute | solution.py:169
  7.7 1.6 %collective-permute-start.3 = (bf16[64,3712]{1,0:T(8,128)(2,1)S(1)}, bf16[64,3712]{1,0:T(8,128)(2,1)S(1)}, u32[]{:S(2)}, u32[]{:S(2)}) collective-permute-start(bf16[64,3712]{1,0:T(8,128)(2,1)S(1)} %collective-permute-done.1), channel_id=1, source_target_pairs={{0,4},{1,3},{4,8},{5,1},{8,12},{9,5},{12,14},{13,9},{14,10},{15,13... | collective-permute-start | bytes 1425416 | tf_op jit(solution)/shard_map/ppermute | solution.py:169
  9.3 5.0 %collective-permute-done.refs_0_ = bf16[64,3712]{1,0:T(8,128)(2,1)S(1)} collective-permute-done((bf16[64,3712]{1,0:T(8,128)(2,1)S(1)}, bf16[64,3712]{1,0:T(8,128)(2,1)S(1)}, u32[]{:S(2)}, u32[]{:S(2)}) %collective-permute-start) | collective-permute-done | bytes 475168 | tf_op jit(solution)/shard_map/ppermute | solution.py:169
  14.3 2.1 %collective-permute-start.5 = (bf16[64,3712]{1,0:T(8,128)(2,1)S(1)}, bf16[64,3712]{1,0:T(8,128)(2,1)S(1)}, u32[]{:S(2)}, u32[]{:S(2)}) collective-permute-start(bf16[64,3712]{1,0:T(8,128)(2,1)S(1)} %collective-permute-done.refs_0_), channel_id=1, source_target_pairs={{0,4},{1,3},{4,8},{5,1},{8,12},{9,5},{12,14},{13,9},{14,10},{15,13... | collective-permute-start | bytes 1425416 | tf_op jit(solution)/shard_map/ppermute | solution.py:169
  16.3 2.0 %shard_map.65.refs_5_.refs_4_ = bf16[3584,512]{1,0:T(8,128)(2,1)S(1)} custom-call(bf16[3584,512]{1,0:T(8,128)(2,1)} %collective-permute-done.2.source), custom_call_target="tpu_custom_call" | custom-call | tf_op jit(solution)/shard_map/pallas_call | solution.py:103
  18.4 1.0 %collective-permute-done.3.refs_1_ = bf16[64,3712]{1,0:T(8,128)(2,1)S(1)} collective-permute-done((bf16[64,3712]{1,0:T(8,128)(2,1)S(1)}, bf16[64,3712]{1,0:T(8,128)(2,1)S(1)}, u32[]{:S(2)}, u32[]{:S(2)}) %collective-permute-start.3) | collective-permute-done | bytes 475168 | tf_op jit(solution)/shard_map/ppermute | solution.py:169
  19.4 2.1 %collective-permute-start.7 = (bf16[64,3712]{1,0:T(8,128)(2,1)S(1)}, bf16[64,3712]{1,0:T(8,128)(2,1)S(1)}, u32[]{:S(2)}, u32[]{:S(2)}) collective-permute-start(bf16[64,3712]{1,0:T(8,128)(2,1)S(1)} %collective-permute-done.3.refs_1_), channel_id=1, source_target_pairs={{0,4},{1,3},{4,8},{5,1},{8,12},{9,5},{12,14},{13,9},{14,10},{15,13... | collective-permute-start | bytes 1425416 | tf_op jit(solution)/shard_map/ppermute | solution.py:169
  21.4 2.2 %shard_map.66.refs_6_.refs_5_ = bf16[3584,512]{1,0:T(8,128)(2,1)S(1)} custom-call(bf16[3584,512]{1,0:T(8,128)(2,1)} %collective-permute-done.4.source), custom_call_target="tpu_custom_call" | custom-call | tf_op jit(solution)/shard_map/pallas_call | solution.py:103
  23.7 0.8 collective-permute-done.5.refs_0_
  24.4 2.1 %collective-permute-start.8 = (bf16[64,3712]{1,0:T(8,128)(2,1)S(1)}, bf16[64,3712]{1,0:T(8,128)(2,1)S(1)}, u32[]{:S(2)}, u32[]{:S(2)}) collective-permute-start(bf16[64,3712]{1,0:T(8,128)(2,1)S(1)} %collective-permute-done.5.refs_0_), channel_id=1, source_target_pairs={{0,4},{1,3},{4,8},{5,1},{8,12},{9,5},{12,14},{13,9},{14,10},{15,13... | collective-permute-start | bytes 1425416 | tf_op jit(solution)/shard_map/ppermute | solution.py:169
  26.5 2.0 %shard_map.67.refs_7_.refs_6_ = bf16[512,3584]{1,0:T(8,128)(2,1)S(1)} custom-call(bf16[512,3584]{1,0:T(8,128)(2,1)} %collective-permute-done.6.source), custom_call_target="tpu_custom_call" | custom-call | tf_op jit(solution)/shard_map/pallas_call | solution.py:103
  28.6 1.0 %collective-permute-done.7.refs_1_ = bf16[64,3712]{1,0:T(8,128)(2,1)S(1)} collective-permute-done((bf16[64,3712]{1,0:T(8,128)(2,1)S(1)}, bf16[64,3712]{1,0:T(8,128)(2,1)S(1)}, u32[]{:S(2)}, u32[]{:S(2)}) %collective-permute-start.7) | collective-permute-done | bytes 475168 | tf_op jit(solution)/shard_map/ppermute | solution.py:169
  29.5 2.1 %collective-permute-start.9 = (bf16[64,3712]{1,0:T(8,128)(2,1)S(1)}, bf16[64,3712]{1,0:T(8,128)(2,1)S(1)}, u32[]{:S(2)}, u32[]{:S(2)}) collective-permute-start(bf16[64,3712]{1,0:T(8,128)(2,1)S(1)} %collective-permute-done.7.refs_1_), channel_id=1, source_target_pairs={{0,4},{1,3},{4,8},{5,1},{8,12},{9,5},{12,14},{13,9},{14,10},{15,13... | collective-permute-start | bytes 1425416 | tf_op jit(solution)/shard_map/ppermute | solution.py:169
  31.6 3.1 %shard_map.68 = (f32[64,3584]{1,0:T(8,128)S(1)}, f32[64,3584]{1,0:T(8,128)S(1)}) custom-call(s32[1]{0:T(128)} %bitcast.me, bf16[64,3712]{1,0:T(8,128)(2,1)S(1)} %collective-permute-done.refs_0_, bf16[64,3712]{1,0:T(8,128)(2,1)S(1)} %collective-permute-done.3.refs_1_, bf16[3584,512]{1,0:T(8,128)(2,1)S(1)} %bitcast.9, bf16[3584,512]{1,0:T(8,128)(2,1)S(1)} %bitcast.15, ...), custom_call_target="tpu_custom_call" | custom-call | tf_op jit(solution)/shard_map/pallas_call | solution.py:85
  34.8 1.9 %collective-permute-start.10 = (bf16[64,3712]{1,0:T(8,128)(2,1)S(1)}, bf16[64,3712]{1,0:T(8,128)(2,1)S(1)}, u32[]{:S(2)}, u32[]{:S(2)}) collective-permute-start(bf16[64,3712]{1,0:T(8,128)(2,1)S(1)} %collective-permute-done.8.refs_0_), channel_id=1, source_target_pairs={{0,4},{1,3},{4,8},{5,1},{8,12},{9,5},{12,14},{13,9},{14,10},{15,13... | collective-permute-start | bytes 1425416 | tf_op jit(solution)/shard_map/ppermute | solution.py:169
  36.7 3.2 %shard_map.69 = (f32[64,3584]{1,0:T(8,128)S(1)}, f32[64,3584]{1,0:T(8,128)S(1)}) custom-call(s32[1]{0:T(128)} %bitcast.me, bf16[64,3712]{1,0:T(8,128)(2,1)S(1)} %collective-permute-done.5.refs_0_, bf16[64,3712]{1,0:T(8,128)(2,1)S(1)} %collective-permute-done.7.refs_1_, bf16[3584,512]{1,0:T(8,128)(2,1)S(1)} %bitcast.10, bf16[3584,512]{1,0:T(8,128)(2,1)S(1)} %bitcast.16, ...), custom_call_target="tpu_custom_call" | custom-call | tf_op jit(solution)/shard_map/pallas_call | solution.py:85
  39.9 3.2 %shard_map.70 = (f32[64,3584]{1,0:T(8,128)S(1)}, bf16[64,3584]{1,0:T(8,128)(2,1)S(1)}) custom-call(s32[1]{0:T(128)} %bitcast.me, bf16[64,3712]{1,0:T(8,128)(2,1)S(1)} %collective-permute-done.8.refs_0_, bf16[64,3712]{1,0:T(8,128)(2,1)S(1)} %collective-permute-done.9.refs_1_, bf16[3584,512]{1,0:T(8,128)(2,1)S(1)} %bitcast.11, bf16[3584,512]{1,0:T(8,128)(2,1)S(1)} %bitcast.17, ...), custom_call_target="tpu_custom_call" | custom-call | tf_op jit(solution)/shard_map/pallas_call | solution.py:85
  43.0 2.1 %collective-permute-start.11 = (bf16[64,3584]{1,0:T(8,128)(2,1)S(1)}, bf16[64,3584]{1,0:T(8,128)(2,1)S(1)}, u32[]{:S(2)}, u32[]{:S(2)}) collective-permute-start(bf16[64,3584]{1,0:T(8,128)(2,1)S(1)} %get-tuple-element.112), channel_id=1, source_target_pairs={{4,0},{3,1},{8,4},{1,5},{12,8},{5,9},{14,12},{9,13},{10,14},{13,15... | collective-permute-start | bytes 1376264 | tf_op jit(solution)/shard_map/ppermute | solution.py:172
  45.1 3.1 %shard_map.71 = bf16[64,3584]{1,0:T(8,128)(2,1)S(1)} custom-call(s32[1]{0:T(128)} %bitcast.me, bf16[64,3712]{1,0:T(8,128)(2,1)S(1)} %collective-permute-done.10.refs_0_, bf16[3584,512]{1,0:T(8,128)(2,1)S(1)} %bitcast.12, bf16[3584,512]{1,0:T(8,128)(2,1)S(1)} %bitcast.18, bf16[512,3584]{1,0:T(8,128)(2,1)S(1)} %bitcast.24, ...), custom_call_target="tpu_custom_call" | custom-call | tf_op jit(solution)/shard_map/pallas_call | solution.py:85
  48.3 1.7 %collective-permute-start.15 = (bf16[64,3584]{1,0:T(8,128)(2,1)S(1)}, bf16[64,3584]{1,0:T(8,128)(2,1)S(1)}, u32[]{:S(2)}, u32[]{:S(2)}) collective-permute-start(bf16[64,3584]{1,0:T(8,128)(2,1)S(1)} %shard_map.71), channel_id=1, source_target_pairs={{4,0},{3,1},{8,4},{1,5},{12,8},{5,9},{14,12},{9,13},{10,14},{13,15... | collective-permute-start | bytes 1376264 | tf_op jit(solution)/shard_map/ppermute | solution.py:172
  50.0 1.7 %collective-permute-done.11.came = bf16[64,3584]{1,0:T(8,128)(2,1)S(1)} collective-permute-done((bf16[64,3584]{1,0:T(8,128)(2,1)S(1)}, bf16[64,3584]{1,0:T(8,128)(2,1)S(1)}, u32[]{:S(2)}, u32[]{:S(2)}) %collective-permute-start.11) | collective-permute-done | bytes 458784 | tf_op jit(solution)/shard_map/ppermute | solution.py:172
  51.8 1.9 %collective-permute-start.12 = (bf16[64,3584]{1,0:T(8,128)(2,1)S(1)}, bf16[64,3584]{1,0:T(8,128)(2,1)S(1)}, u32[]{:S(2)}, u32[]{:S(2)}) collective-permute-start(bf16[64,3584]{1,0:T(8,128)(2,1)S(1)} %shard_map.73), channel_id=1, source_target_pairs={{4,0},{3,1},{8,4},{1,5},{12,8},{5,9},{14,12},{9,13},{10,14},{13,15... | collective-permute-start | bytes 1376264 | tf_op jit(solution)/shard_map/ppermute | solution.py:172
  53.7 3.1 %collective-permute-done.15.came = bf16[64,3584]{1,0:T(8,128)(2,1)S(1)} collective-permute-done((bf16[64,3584]{1,0:T(8,128)(2,1)S(1)}, bf16[64,3584]{1,0:T(8,128)(2,1)S(1)}, u32[]{:S(2)}, u32[]{:S(2)}) %collective-permute-start.15) | collective-permute-done | bytes 458784 | tf_op jit(solution)/shard_map/ppermute | solution.py:172
  56.8 0.1 shard_map.75
  56.9 1.8 %collective-permute-start.16 = (bf16[64,3584]{1,0:T(8,128)(2,1)S(1)}, bf16[64,3584]{1,0:T(8,128)(2,1)S(1)}, u32[]{:S(2)}, u32[]{:S(2)}) collective-permute-start(bf16[64,3584]{1,0:T(8,128)(2,1)S(1)} %shard_map.75), channel_id=1, source_target_pairs={{4,0},{3,1},{8,4},{1,5},{12,8},{5,9},{14,12},{9,13},{10,14},{13,15... | collective-permute-start | bytes 1376264 | tf_op jit(solution)/shard_map/ppermute | solution.py:172
  58.7 3.1 %collective-permute-done.12.came = bf16[64,3584]{1,0:T(8,128)(2,1)S(1)} collective-permute-done((bf16[64,3584]{1,0:T(8,128)(2,1)S(1)}, bf16[64,3584]{1,0:T(8,128)(2,1)S(1)}, u32[]{:S(2)}, u32[]{:S(2)}) %collective-permute-start.12) | collective-permute-done | bytes 458784 | tf_op jit(solution)/shard_map/ppermute | solution.py:172
  61.8 1.8 %collective-permute-start.13 = (bf16[64,3584]{1,0:T(8,128)(2,1)S(1)}, bf16[64,3584]{1,0:T(8,128)(2,1)S(1)}, u32[]{:S(2)}, u32[]{:S(2)}) collective-permute-start(bf16[64,3584]{1,0:T(8,128)(2,1)S(1)} %shard_map.74), channel_id=1, source_target_pairs={{4,0},{3,1},{8,4},{1,5},{12,8},{5,9},{14,12},{9,13},{10,14},{13,15... | collective-permute-start | bytes 1376264 | tf_op jit(solution)/shard_map/ppermute | solution.py:172
  63.6 3.1 %collective-permute-done.16.came = bf16[64,3584]{1,0:T(8,128)(2,1)S(1)} collective-permute-done((bf16[64,3584]{1,0:T(8,128)(2,1)S(1)}, bf16[64,3584]{1,0:T(8,128)(2,1)S(1)}, u32[]{:S(2)}, u32[]{:S(2)}) %collective-permute-start.16) | collective-permute-done | bytes 458784 | tf_op jit(solution)/shard_map/ppermute | solution.py:172
  66.6 0.1 shard_map.76
  66.7 1.8 %collective-permute-start.19 = (bf16[32,3584]{1,0:T(8,128)(2,1)S(1)}, bf16[32,3584]{1,0:T(8,128)(2,1)S(1)}, u32[]{:S(2)}, u32[]{:S(2)}) collective-permute-start(bf16[32,3584]{1,0:T(8,128)(2,1)S(1)} %get-tuple-element.118), channel_id=1, source_target_pairs={{4,0},{3,1},{8,4},{1,5},{12,8},{5,9},{14,12},{9,13},{10,14},{13,15... | collective-permute-start | bytes 688136 | tf_op jit(solution)/shard_map/ppermute | solution.py:172
  68.5 1.6 %collective-permute-start.17 = (bf16[32,3584]{1,0:T(8,128)(2,1)S(1)}, bf16[32,3584]{1,0:T(8,128)(2,1)S(1)}, u32[]{:S(2)}, u32[]{:S(2)}) collective-permute-start(bf16[32,3584]{1,0:T(8,128)(2,1)S(1)} %get-tuple-element.117), channel_id=1, source_target_pairs={{4,0},{3,1},{8,4},{1,5},{12,8},{5,9},{14,12},{9,13},{10,14},{13,15... | collective-permute-start | bytes 688136 | tf_op jit(solution)/shard_map/ppermute | solution.py:172
  70.1 1.5 %collective-permute-done.13 = bf16[64,3584]{1,0:T(8,128)(2,1)S(1)} collective-permute-done((bf16[64,3584]{1,0:T(8,128)(2,1)S(1)}, bf16[64,3584]{1,0:T(8,128)(2,1)S(1)}, u32[]{:S(2)}, u32[]{:S(2)}) %collective-permute-start.13) | collective-permute-done | bytes 458784 | tf_op jit(solution)/shard_map/ppermute | solution.py:172
  71.6 2.5 %collective-permute-done.19.came = bf16[32,3584]{1,0:T(8,128)(2,1)S(1)} collective-permute-done((bf16[32,3584]{1,0:T(8,128)(2,1)S(1)}, bf16[32,3584]{1,0:T(8,128)(2,1)S(1)}, u32[]{:S(2)}, u32[]{:S(2)}) %collective-permute-start.19) | collective-permute-done | bytes 229408 | tf_op jit(solution)/shard_map/ppermute | solution.py:172
  74.1 1.8 %collective-permute-start.20 = (bf16[32,3584]{1,0:T(8,128)(2,1)S(1)}, bf16[32,3584]{1,0:T(8,128)(2,1)S(1)}, u32[]{:S(2)}, u32[]{:S(2)}) collective-permute-start(bf16[32,3584]{1,0:T(8,128)(2,1)S(1)} %shard_map.78), channel_id=1, source_target_pairs={{4,0},{3,1},{8,4},{1,5},{12,8},{5,9},{14,12},{9,13},{10,14},{13,15... | collective-permute-start | bytes 688136 | tf_op jit(solution)/shard_map/ppermute | solution.py:172
  75.8 0.7 collective-permute-done.17.came
  76.5 1.8 %collective-permute-start.18 = (bf16[32,3584]{1,0:T(8,128)(2,1)S(1)}, bf16[32,3584]{1,0:T(8,128)(2,1)S(1)}, u32[]{:S(2)}, u32[]{:S(2)}) collective-permute-start(bf16[32,3584]{1,0:T(8,128)(2,1)S(1)} %shard_map.77), channel_id=1, source_target_pairs={{4,0},{3,1},{8,4},{1,5},{12,8},{5,9},{14,12},{9,13},{10,14},{13,15... | collective-permute-start | bytes 688136 | tf_op jit(solution)/shard_map/ppermute | solution.py:172
  78.3 3.1 %shard_map.72.mine = f32[64,3584]{1,0:T(8,128)S(1)} custom-call(s32[1]{0:T(128)} %bitcast.me, bf16[64,3712]{1,0:T(8,128)(2,1)S(1)} %shard_map.64.refs_0_, bf16[3584,512]{1,0:T(8,128)(2,1)S(1)} %bitcast.13, bf16[3584,512]{1,0:T(8,128)(2,1)S(1)} %bitcast.19, bf16[512,3584]{1,0:T(8,128)(2,1)S(1)} %bitcast.25, bf16[3584,512]{1,0:T(8,128)(2,1)S(1)} %shard_map.65.refs_5_.refs_4_, ...), custom_call_target="tpu_custom_call" | custom-call | tf_op jit(solution)/shard_map/pallas_call | solution.py:85
  81.4 1.2 %collective-permute-done.18.refs_0_ = bf16[32,3584]{1,0:T(8,128)(2,1)S(1)} collective-permute-done((bf16[32,3584]{1,0:T(8,128)(2,1)S(1)}, bf16[32,3584]{1,0:T(8,128)(2,1)S(1)}, u32[]{:S(2)}, u32[]{:S(2)}) %collective-permute-start.18) | collective-permute-done | bytes 229408 | tf_op jit(solution)/shard_map/ppermute | solution.py:172
  82.6 0.9 %shard_map.79 = bf16[64,3584]{1,0:T(8,128)(2,1)} custom-call(f32[64,3584]{1,0:T(8,128)S(1)} %shard_map.72.mine, bf16[64,3584]{1,0:T(8,128)(2,1)S(1)} %collective-permute-done.14.other, bf16[32,3584]{1,0:T(8,128)(2,1)S(1)} %collective-permute-done.18.refs_0_, bf16[32,3584]{1,0:T(8,128)(2,1)S(1)} %collective-permute-done.20.refs_1_), custom_call_target="tpu_custom_call" | custom-call | tf_op jit(solution)/shard_map/pallas_call | solution.py:150
  (20 shorter events, 0.3 us)
Async XLA Ops:
  0.8 1.0 %copy-start.3 = (bf16[2,32,3584]{2,1,0:T(8,128)(2,1)S(1)}, bf16[2,32,3584]{2,1,0:T(8,128)(2,1)}, u32[]{:S(2)}) copy-start(bf16[2,32,3584]{2,1,0:T(8,128)(2,1)} %param.6) | copy-start | bytes 1376260
  2.1 2.0 %collective-permute-start.1 = (bf16[64,3712]{1,0:T(8,128)(2,1)S(1)}, bf16[64,3712]{1,0:T(8,128)(2,1)S(1)}, u32[]{:S(2)}, u32[]{:S(2)}) collective-permute-start(bf16[64,3712]{1,0:T(8,128)(2,1)S(1)} %shard_map.64.refs_0_), channel_id=1, source_target_pairs={{0,1},{1,0},{2,3},{3,2},{4,5},{5,4},{6,7},{7,6},{8,9},{9,8},{10,11... | collective-permute-start | bytes 1425416 | tf_op jit(solution)/shard_map/ppermute | solution.py:175
  4.1 12.3 %collective-permute-start.2 = (bf16[3584,512]{1,0:T(8,128)(2,1)}, bf16[3584,512]{1,0:T(8,128)(2,1)}, u32[]{:S(2)}, u32[]{:S(2)}) collective-permute-start(bf16[3584,512]{1,0:T(8,128)(2,1)} %bitcast.8), channel_id=1, source_target_pairs={{0,1},{1,0},{2,3},{3,2},{4,5},{5,4},{6,7},{7,6},{8,9},{9,8},{10,11... | collective-permute-start | bytes 11010056 | tf_op jit(solution)/shard_map/ppermute | solution.py:175
  4.5 17.0 %collective-permute-start.4 = (bf16[3584,512]{1,0:T(8,128)(2,1)}, bf16[3584,512]{1,0:T(8,128)(2,1)}, u32[]{:S(2)}, u32[]{:S(2)}) collective-permute-start(bf16[3584,512]{1,0:T(8,128)(2,1)} %bitcast.14), channel_id=1, source_target_pairs={{0,1},{1,0},{2,3},{3,2},{4,5},{5,4},{6,7},{7,6},{8,9},{9,8},{10,11... | collective-permute-start | bytes 11010056 | tf_op jit(solution)/shard_map/ppermute | solution.py:175
  4.6 21.9 %collective-permute-start.6 = (bf16[512,3584]{1,0:T(8,128)(2,1)}, bf16[512,3584]{1,0:T(8,128)(2,1)}, u32[]{:S(2)}, u32[]{:S(2)}) collective-permute-start(bf16[512,3584]{1,0:T(8,128)(2,1)} %bitcast.20), channel_id=1, source_target_pairs={{0,1},{1,0},{2,3},{3,2},{4,5},{5,4},{6,7},{7,6},{8,9},{9,8},{10,11... | collective-permute-start | bytes 11010056 | tf_op jit(solution)/shard_map/ppermute | solution.py:175
  5.0 9.3 %collective-permute-start = (bf16[64,3712]{1,0:T(8,128)(2,1)S(1)}, bf16[64,3712]{1,0:T(8,128)(2,1)S(1)}, u32[]{:S(2)}, u32[]{:S(2)}) collective-permute-start(bf16[64,3712]{1,0:T(8,128)(2,1)S(1)} %shard_map.64.refs_0_), channel_id=1, source_target_pairs={{0,4},{1,3},{4,8},{5,1},{8,12},{9,5},{12,14},{13,9},{14,10},{15,13... | collective-permute-start | bytes 1425416 | tf_op jit(solution)/shard_map/ppermute | solution.py:169
  7.7 11.7 %collective-permute-start.3 = (bf16[64,3712]{1,0:T(8,128)(2,1)S(1)}, bf16[64,3712]{1,0:T(8,128)(2,1)S(1)}, u32[]{:S(2)}, u32[]{:S(2)}) collective-permute-start(bf16[64,3712]{1,0:T(8,128)(2,1)S(1)} %collective-permute-done.1), channel_id=1, source_target_pairs={{0,4},{1,3},{4,8},{5,1},{8,12},{9,5},{12,14},{13,9},{14,10},{15,13... | collective-permute-start | bytes 1425416 | tf_op jit(solution)/shard_map/ppermute | solution.py:169
  14.3 10.2 %collective-permute-start.5 = (bf16[64,3712]{1,0:T(8,128)(2,1)S(1)}, bf16[64,3712]{1,0:T(8,128)(2,1)S(1)}, u32[]{:S(2)}, u32[]{:S(2)}) collective-permute-start(bf16[64,3712]{1,0:T(8,128)(2,1)S(1)} %collective-permute-done.refs_0_), channel_id=1, source_target_pairs={{0,4},{1,3},{4,8},{5,1},{8,12},{9,5},{12,14},{13,9},{14,10},{15,13... | collective-permute-start | bytes 1425416 | tf_op jit(solution)/shard_map/ppermute | solution.py:169
  19.4 10.2 %collective-permute-start.7 = (bf16[64,3712]{1,0:T(8,128)(2,1)S(1)}, bf16[64,3712]{1,0:T(8,128)(2,1)S(1)}, u32[]{:S(2)}, u32[]{:S(2)}) collective-permute-start(bf16[64,3712]{1,0:T(8,128)(2,1)S(1)} %collective-permute-done.3.refs_1_), channel_id=1, source_target_pairs={{0,4},{1,3},{4,8},{5,1},{8,12},{9,5},{12,14},{13,9},{14,10},{15,13... | collective-permute-start | bytes 1425416 | tf_op jit(solution)/shard_map/ppermute | solution.py:169
  21.4 10.2 %copy-start.2 = (bf16[1,512,3584]{2,1,0:T(8,128)(2,1)S(1)}, bf16[1,512,3584]{2,1,0:T(8,128)(2,1)}, u32[]{:S(2)}) copy-start(bf16[1,512,3584]{2,1,0:T(8,128)(2,1)} %param.11) | copy-start | bytes 11010052
  23.6 8.0 %copy-start = (bf16[1,3584,512]{2,1,0:T(8,128)(2,1)S(1)}, bf16[1,3584,512]{2,1,0:T(8,128)(2,1)}, u32[]{:S(2)}) copy-start(bf16[1,3584,512]{2,1,0:T(8,128)(2,1)} %param.9) | copy-start | bytes 11010052
  23.7 8.0 %copy-start.1 = (bf16[1,3584,512]{2,1,0:T(8,128)(2,1)S(1)}, bf16[1,3584,512]{2,1,0:T(8,128)(2,1)}, u32[]{:S(2)}) copy-start(bf16[1,3584,512]{2,1,0:T(8,128)(2,1)} %param.10) | copy-start | bytes 11010052
  24.4 10.3 %collective-permute-start.8 = (bf16[64,3712]{1,0:T(8,128)(2,1)S(1)}, bf16[64,3712]{1,0:T(8,128)(2,1)S(1)}, u32[]{:S(2)}, u32[]{:S(2)}) collective-permute-start(bf16[64,3712]{1,0:T(8,128)(2,1)S(1)} %collective-permute-done.5.refs_0_), channel_id=1, source_target_pairs={{0,4},{1,3},{4,8},{5,1},{8,12},{9,5},{12,14},{13,9},{14,10},{15,13... | collective-permute-start | bytes 1425416 | tf_op jit(solution)/shard_map/ppermute | solution.py:169
  29.5 10.3 %collective-permute-start.9 = (bf16[64,3712]{1,0:T(8,128)(2,1)S(1)}, bf16[64,3712]{1,0:T(8,128)(2,1)S(1)}, u32[]{:S(2)}, u32[]{:S(2)}) collective-permute-start(bf16[64,3712]{1,0:T(8,128)(2,1)S(1)} %collective-permute-done.7.refs_1_), channel_id=1, source_target_pairs={{0,4},{1,3},{4,8},{5,1},{8,12},{9,5},{12,14},{13,9},{14,10},{15,13... | collective-permute-start | bytes 1425416 | tf_op jit(solution)/shard_map/ppermute | solution.py:169
  34.8 10.3 %collective-permute-start.10 = (bf16[64,3712]{1,0:T(8,128)(2,1)S(1)}, bf16[64,3712]{1,0:T(8,128)(2,1)S(1)}, u32[]{:S(2)}, u32[]{:S(2)}) collective-permute-start(bf16[64,3712]{1,0:T(8,128)(2,1)S(1)} %collective-permute-done.8.refs_0_), channel_id=1, source_target_pairs={{0,4},{1,3},{4,8},{5,1},{8,12},{9,5},{12,14},{13,9},{14,10},{15,13... | collective-permute-start | bytes 1425416 | tf_op jit(solution)/shard_map/ppermute | solution.py:169
  43.0 8.7 %collective-permute-start.11 = (bf16[64,3584]{1,0:T(8,128)(2,1)S(1)}, bf16[64,3584]{1,0:T(8,128)(2,1)S(1)}, u32[]{:S(2)}, u32[]{:S(2)}) collective-permute-start(bf16[64,3584]{1,0:T(8,128)(2,1)S(1)} %get-tuple-element.112), channel_id=1, source_target_pairs={{4,0},{3,1},{8,4},{1,5},{12,8},{5,9},{14,12},{9,13},{10,14},{13,15... | collective-permute-start | bytes 1376264 | tf_op jit(solution)/shard_map/ppermute | solution.py:172
  48.3 8.5 %collective-permute-start.15 = (bf16[64,3584]{1,0:T(8,128)(2,1)S(1)}, bf16[64,3584]{1,0:T(8,128)(2,1)S(1)}, u32[]{:S(2)}, u32[]{:S(2)}) collective-permute-start(bf16[64,3584]{1,0:T(8,128)(2,1)S(1)} %shard_map.71), channel_id=1, source_target_pairs={{4,0},{3,1},{8,4},{1,5},{12,8},{5,9},{14,12},{9,13},{10,14},{13,15... | collective-permute-start | bytes 1376264 | tf_op jit(solution)/shard_map/ppermute | solution.py:172
  51.8 9.9 %collective-permute-start.12 = (bf16[64,3584]{1,0:T(8,128)(2,1)S(1)}, bf16[64,3584]{1,0:T(8,128)(2,1)S(1)}, u32[]{:S(2)}, u32[]{:S(2)}) collective-permute-start(bf16[64,3584]{1,0:T(8,128)(2,1)S(1)} %shard_map.73), channel_id=1, source_target_pairs={{4,0},{3,1},{8,4},{1,5},{12,8},{5,9},{14,12},{9,13},{10,14},{13,15... | collective-permute-start | bytes 1376264 | tf_op jit(solution)/shard_map/ppermute | solution.py:172
  56.9 9.7 %collective-permute-start.16 = (bf16[64,3584]{1,0:T(8,128)(2,1)S(1)}, bf16[64,3584]{1,0:T(8,128)(2,1)S(1)}, u32[]{:S(2)}, u32[]{:S(2)}) collective-permute-start(bf16[64,3584]{1,0:T(8,128)(2,1)S(1)} %shard_map.75), channel_id=1, source_target_pairs={{4,0},{3,1},{8,4},{1,5},{12,8},{5,9},{14,12},{9,13},{10,14},{13,15... | collective-permute-start | bytes 1376264 | tf_op jit(solution)/shard_map/ppermute | solution.py:172
  61.8 9.7 %collective-permute-start.13 = (bf16[64,3584]{1,0:T(8,128)(2,1)S(1)}, bf16[64,3584]{1,0:T(8,128)(2,1)S(1)}, u32[]{:S(2)}, u32[]{:S(2)}) collective-permute-start(bf16[64,3584]{1,0:T(8,128)(2,1)S(1)} %shard_map.74), channel_id=1, source_target_pairs={{4,0},{3,1},{8,4},{1,5},{12,8},{5,9},{14,12},{9,13},{10,14},{13,15... | collective-permute-start | bytes 1376264 | tf_op jit(solution)/shard_map/ppermute | solution.py:172
  66.7 7.3 %collective-permute-start.19 = (bf16[32,3584]{1,0:T(8,128)(2,1)S(1)}, bf16[32,3584]{1,0:T(8,128)(2,1)S(1)}, u32[]{:S(2)}, u32[]{:S(2)}) collective-permute-start(bf16[32,3584]{1,0:T(8,128)(2,1)S(1)} %get-tuple-element.118), channel_id=1, source_target_pairs={{4,0},{3,1},{8,4},{1,5},{12,8},{5,9},{14,12},{9,13},{10,14},{13,15... | collective-permute-start | bytes 688136 | tf_op jit(solution)/shard_map/ppermute | solution.py:172
  68.5 8.0 %collective-permute-start.17 = (bf16[32,3584]{1,0:T(8,128)(2,1)S(1)}, bf16[32,3584]{1,0:T(8,128)(2,1)S(1)}, u32[]{:S(2)}, u32[]{:S(2)}) collective-permute-start(bf16[32,3584]{1,0:T(8,128)(2,1)S(1)} %get-tuple-element.117), channel_id=1, source_target_pairs={{4,0},{3,1},{8,4},{1,5},{12,8},{5,9},{14,12},{9,13},{10,14},{13,15... | collective-permute-start | bytes 688136 | tf_op jit(solution)/shard_map/ppermute | solution.py:172
  71.6 11.1 %collective-permute-start.14 = (bf16[64,3584]{1,0:T(8,128)(2,1)S(1)}, bf16[64,3584]{1,0:T(8,128)(2,1)S(1)}, u32[]{:S(2)}, u32[]{:S(2)}) collective-permute-start(bf16[64,3584]{1,0:T(8,128)(2,1)S(1)} %collective-permute-done.13), channel_id=1, source_target_pairs={{0,1},{1,0},{2,3},{3,2},{4,5},{5,4},{6,7},{7,6},{8,9},{9,8},{10,11... | collective-permute-start | bytes 1376264 | tf_op jit(solution)/shard_map/ppermute | solution.py:175
  74.1 7.4 %collective-permute-start.20 = (bf16[32,3584]{1,0:T(8,128)(2,1)S(1)}, bf16[32,3584]{1,0:T(8,128)(2,1)S(1)}, u32[]{:S(2)}, u32[]{:S(2)}) collective-permute-start(bf16[32,3584]{1,0:T(8,128)(2,1)S(1)} %shard_map.78), channel_id=1, source_target_pairs={{4,0},{3,1},{8,4},{1,5},{12,8},{5,9},{14,12},{9,13},{10,14},{13,15... | collective-permute-start | bytes 688136 | tf_op jit(solution)/shard_map/ppermute | solution.py:172
  76.5 6.1 %collective-permute-start.18 = (bf16[32,3584]{1,0:T(8,128)(2,1)S(1)}, bf16[32,3584]{1,0:T(8,128)(2,1)S(1)}, u32[]{:S(2)}, u32[]{:S(2)}) collective-permute-start(bf16[32,3584]{1,0:T(8,128)(2,1)S(1)} %shard_map.77), channel_id=1, source_target_pairs={{4,0},{3,1},{8,4},{1,5},{12,8},{5,9},{14,12},{9,13},{10,14},{13,15... | collective-permute-start | bytes 688136 | tf_op jit(solution)/shard_map/ppermute | solution.py:172

commit v5 on v4

--- a/solution.py
+++ b/solution.py
@@ -7,7 +7,7 @@
 from jax.experimental.pallas import tpu as pltpu
 from jax.sharding import PartitionSpec as P
 
-TILE = 256
+TILE = 512
 LANES = 128
 LEAST_ROWS = 128
 VMEM_LIMIT = 12 * 2**20
@@ -28,8 +28,9 @@
     copy.start()
     lane = lax.broadcasted_iota(jnp.int32, (rows, message.shape[1] - width), 1)
     table = jnp.zeros(lane.shape, jnp.int32)
-    for k in range(routes.shape[3]):
-        expert, weight = (routes[i, :, :, k : k + 1].reshape(rows, 1) for i in range(2))
+    steps = routes.shape[0] // 2
+    for k in range(routes.shape[2]):
+        expert, weight = (routes[i * steps : (i + 1) * steps, :, k : k + 1].reshape(rows, 1) for i in range(2))
         table += jnp.where(lane == expert, weight >> 8, 0) + jnp.where(lane == expert + n, weight & 255, 0)
     message[:, width:] = table.astype(jnp.float32).astype(jnp.bfloat16)
     copy.wait()
@@ -37,7 +38,7 @@
 
 def make_message(n, tokens, expert_ids, gate_fixed):
     rows, width = tokens.shape
-    routes = jnp.stack([expert_ids, gate_fixed])
+    routes = jnp.concatenate([expert_ids, gate_fixed])
     return pl.pallas_call(
         functools.partial(message_kernel, n),
         out_shape=jax.ShapeDtypeStruct((rows, width + -(-2 * n // LANES) * LANES), jnp.bfloat16),

time: 83.9 us -> 84 us (level)
  no operation moved by 1% of the time
where the time goes in v5:
time: 84 us; the launch traced here: 83.7 us
  starting transfers between devices  31.8 us (38%)
  waiting for transfers between devices  26 us (31%)
  Pallas kernels  23.8 us (28%)
  local copies, waits for them, and re-layouts  1.14 us (1%)
    ppermute x9, waiting for transfers between devices, home(): lax.ppermute(value, ('node', 'local'), [(to, source) for source, to in ri...  16.8 us
    pallas_call x5, Pallas kernels, run_experts(): pl.pallas_call(functools.partial(experts_kernel, len(inputs), n), out_sha...  15.9 us
    ppermute x9, starting transfers between devices, home(): lax.ppermute(value, ('node', 'local'), [(to, source) for source, to in ri...  15.9 us
    ppermute x7, starting transfers between devices, onward(): return lax.ppermute(value, ('node', 'local'), ring)  14.5 us
    ppermute x7, waiting for transfers between devices, onward(): return lax.ppermute(value, ('node', 'local'), ring)  7.68 us
    pallas_call x3, Pallas kernels, keep(): pl.pallas_call(keep_kernel, out_shape=jax.ShapeDtypeStruct(value.shape, v...  6.29 us
  transfers between devices with their start and end apart: 21, of which 13 were waited for; matrix products, arithmetic and copies ran while one was open for 0% of the time, Pallas kernels for 27%

profile of v5, /device:TPU:0, one launch (start us, length us, event | category | flops | bytes accessed | tf_op | source)
XLA Modules:
  0.0 83.7 jit_solution(63636953468461671)
XLA Ops:
  0.0 0.7 pad_add_fusion
  0.7 0.1 copy.9.routes
  0.8 1.0 %copy-done.3 = bf16[2,32,3584]{2,1,0:T(8,128)(2,1)S(1)} copy-done((bf16[2,32,3584]{2,1,0:T(8,128)(2,1)S(1)}, bf16[2,32,3584]{2,1,0:T(8,128)(2,1)}, u32[]{:S(2)}) %copy-start.3) | copy-done | bytes 458776
  1.8 0.3 shard_map.64.refs_0_
  2.1 0.5 collective-permute-start.1
  2.6 1.5 %collective-permute-done.1 = bf16[64,3712]{1,0:T(8,128)(2,1)S(1)} collective-permute-done((bf16[64,3712]{1,0:T(8,128)(2,1)S(1)}, bf16[64,3712]{1,0:T(8,128)(2,1)S(1)}, u32[]{:S(2)}, u32[]{:S(2)}) %collective-permute-start.1) | collective-permute-done | bytes 475168 | tf_op jit(solution)/shard_map/ppermute | solution.py:176
  4.1 0.4 collective-permute-start.2
  4.5 0.1 collective-permute-start.4
  4.6 0.4 collective-permute-start.6
  5.0 2.7 %collective-permute-start = (bf16[64,3712]{1,0:T(8,128)(2,1)S(1)}, bf16[64,3712]{1,0:T(8,128)(2,1)S(1)}, u32[]{:S(2)}, u32[]{:S(2)}) collective-permute-start(bf16[64,3712]{1,0:T(8,128)(2,1)S(1)} %shard_map.64.refs_0_), channel_id=1, source_target_pairs={{0,4},{1,3},{4,8},{5,1},{8,12},{9,5},{12,14},{13,9},{14,10},{15,13... | collective-permute-start | bytes 1425416 | tf_op jit(solution)/shard_map/ppermute | solution.py:170
  7.7 1.6 %collective-permute-start.3 = (bf16[64,3712]{1,0:T(8,128)(2,1)S(1)}, bf16[64,3712]{1,0:T(8,128)(2,1)S(1)}, u32[]{:S(2)}, u32[]{:S(2)}) collective-permute-start(bf16[64,3712]{1,0:T(8,128)(2,1)S(1)} %collective-permute-done.1), channel_id=1, source_target_pairs={{0,4},{1,3},{4,8},{5,1},{8,12},{9,5},{12,14},{13,9},{14,10},{15,13... | collective-permute-start | bytes 1425416 | tf_op jit(solution)/shard_map/ppermute | solution.py:170
  9.3 5.0 %collective-permute-done.refs_0_ = bf16[64,3712]{1,0:T(8,128)(2,1)S(1)} collective-permute-done((bf16[64,3712]{1,0:T(8,128)(2,1)S(1)}, bf16[64,3712]{1,0:T(8,128)(2,1)S(1)}, u32[]{:S(2)}, u32[]{:S(2)}) %collective-permute-start) | collective-permute-done | bytes 475168 | tf_op jit(solution)/shard_map/ppermute | solution.py:170
  14.3 2.1 %collective-permute-start.5 = (bf16[64,3712]{1,0:T(8,128)(2,1)S(1)}, bf16[64,3712]{1,0:T(8,128)(2,1)S(1)}, u32[]{:S(2)}, u32[]{:S(2)}) collective-permute-start(bf16[64,3712]{1,0:T(8,128)(2,1)S(1)} %collective-permute-done.refs_0_), channel_id=1, source_target_pairs={{0,4},{1,3},{4,8},{5,1},{8,12},{9,5},{12,14},{13,9},{14,10},{15,13... | collective-permute-start | bytes 1425416 | tf_op jit(solution)/shard_map/ppermute | solution.py:170
  16.3 2.0 %shard_map.65.refs_5_.refs_4_ = bf16[3584,512]{1,0:T(8,128)(2,1)S(1)} custom-call(bf16[3584,512]{1,0:T(8,128)(2,1)} %collective-permute-done.2.source), custom_call_target="tpu_custom_call" | custom-call | tf_op jit(solution)/shard_map/pallas_call | solution.py:104
  18.4 1.0 %collective-permute-done.3.refs_1_ = bf16[64,3712]{1,0:T(8,128)(2,1)S(1)} collective-permute-done((bf16[64,3712]{1,0:T(8,128)(2,1)S(1)}, bf16[64,3712]{1,0:T(8,128)(2,1)S(1)}, u32[]{:S(2)}, u32[]{:S(2)}) %collective-permute-start.3) | collective-permute-done | bytes 475168 | tf_op jit(solution)/shard_map/ppermute | solution.py:170
  19.4 2.1 %collective-permute-start.7 = (bf16[64,3712]{1,0:T(8,128)(2,1)S(1)}, bf16[64,3712]{1,0:T(8,128)(2,1)S(1)}, u32[]{:S(2)}, u32[]{:S(2)}) collective-permute-start(bf16[64,3712]{1,0:T(8,128)(2,1)S(1)} %collective-permute-done.3.refs_1_), channel_id=1, source_target_pairs={{0,4},{1,3},{4,8},{5,1},{8,12},{9,5},{12,14},{13,9},{14,10},{15,13... | collective-permute-start | bytes 1425416 | tf_op jit(solution)/shard_map/ppermute | solution.py:170
  21.4 2.2 %shard_map.66.refs_6_.refs_5_ = bf16[3584,512]{1,0:T(8,128)(2,1)S(1)} custom-call(bf16[3584,512]{1,0:T(8,128)(2,1)} %collective-permute-done.4.source), custom_call_target="tpu_custom_call" | custom-call | tf_op jit(solution)/shard_map/pallas_call | solution.py:104
  23.7 0.8 collective-permute-done.5.refs_0_
  24.4 2.1 %collective-permute-start.8 = (bf16[64,3712]{1,0:T(8,128)(2,1)S(1)}, bf16[64,3712]{1,0:T(8,128)(2,1)S(1)}, u32[]{:S(2)}, u32[]{:S(2)}) collective-permute-start(bf16[64,3712]{1,0:T(8,128)(2,1)S(1)} %collective-permute-done.5.refs_0_), channel_id=1, source_target_pairs={{0,4},{1,3},{4,8},{5,1},{8,12},{9,5},{12,14},{13,9},{14,10},{15,13... | collective-permute-start | bytes 1425416 | tf_op jit(solution)/shard_map/ppermute | solution.py:170
  26.5 2.0 %shard_map.67.refs_7_.refs_6_ = bf16[512,3584]{1,0:T(8,128)(2,1)S(1)} custom-call(bf16[512,3584]{1,0:T(8,128)(2,1)} %collective-permute-done.6.source), custom_call_target="tpu_custom_call" | custom-call | tf_op jit(solution)/shard_map/pallas_call | solution.py:104
  28.6 1.0 %collective-permute-done.7.refs_1_ = bf16[64,3712]{1,0:T(8,128)(2,1)S(1)} collective-permute-done((bf16[64,3712]{1,0:T(8,128)(2,1)S(1)}, bf16[64,3712]{1,0:T(8,128)(2,1)S(1)}, u32[]{:S(2)}, u32[]{:S(2)}) %collective-permute-start.7) | collective-permute-done | bytes 475168 | tf_op jit(solution)/shard_map/ppermute | solution.py:170
  29.5 2.1 %collective-permute-start.9 = (bf16[64,3712]{1,0:T(8,128)(2,1)S(1)}, bf16[64,3712]{1,0:T(8,128)(2,1)S(1)}, u32[]{:S(2)}, u32[]{:S(2)}) collective-permute-start(bf16[64,3712]{1,0:T(8,128)(2,1)S(1)} %collective-permute-done.7.refs_1_), channel_id=1, source_target_pairs={{0,4},{1,3},{4,8},{5,1},{8,12},{9,5},{12,14},{13,9},{14,10},{15,13... | collective-permute-start | bytes 1425416 | tf_op jit(solution)/shard_map/ppermute | solution.py:170
  31.6 3.2 %shard_map.68 = (f32[64,3584]{1,0:T(8,128)S(1)}, f32[64,3584]{1,0:T(8,128)S(1)}) custom-call(s32[1]{0:T(128)} %bitcast.me, bf16[64,3712]{1,0:T(8,128)(2,1)S(1)} %collective-permute-done.refs_0_, bf16[64,3712]{1,0:T(8,128)(2,1)S(1)} %collective-permute-done.3.refs_1_, bf16[3584,512]{1,0:T(8,128)(2,1)S(1)} %bitcast.7, bf16[3584,512]{1,0:T(8,128)(2,1)S(1)} %bitcast.13, ...), custom_call_target="tpu_custom_call" | custom-call | tf_op jit(solution)/shard_map/pallas_call | solution.py:86
  34.8 1.9 %collective-permute-start.10 = (bf16[64,3712]{1,0:T(8,128)(2,1)S(1)}, bf16[64,3712]{1,0:T(8,128)(2,1)S(1)}, u32[]{:S(2)}, u32[]{:S(2)}) collective-permute-start(bf16[64,3712]{1,0:T(8,128)(2,1)S(1)} %collective-permute-done.8.refs_0_), channel_id=1, source_target_pairs={{0,4},{1,3},{4,8},{5,1},{8,12},{9,5},{12,14},{13,9},{14,10},{15,13... | collective-permute-start | bytes 1425416 | tf_op jit(solution)/shard_map/ppermute | solution.py:170
  36.7 3.2 %shard_map.69 = (f32[64,3584]{1,0:T(8,128)S(1)}, f32[64,3584]{1,0:T(8,128)S(1)}) custom-call(s32[1]{0:T(128)} %bitcast.me, bf16[64,3712]{1,0:T(8,128)(2,1)S(1)} %collective-permute-done.5.refs_0_, bf16[64,3712]{1,0:T(8,128)(2,1)S(1)} %collective-permute-done.7.refs_1_, bf16[3584,512]{1,0:T(8,128)(2,1)S(1)} %bitcast.8, bf16[3584,512]{1,0:T(8,128)(2,1)S(1)} %bitcast.14, ...), custom_call_target="tpu_custom_call" | custom-call | tf_op jit(solution)/shard_map/pallas_call | solution.py:86
  39.9 3.2 %shard_map.70 = (f32[64,3584]{1,0:T(8,128)S(1)}, bf16[64,3584]{1,0:T(8,128)(2,1)S(1)}) custom-call(s32[1]{0:T(128)} %bitcast.me, bf16[64,3712]{1,0:T(8,128)(2,1)S(1)} %collective-permute-done.8.refs_0_, bf16[64,3712]{1,0:T(8,128)(2,1)S(1)} %collective-permute-done.9.refs_1_, bf16[3584,512]{1,0:T(8,128)(2,1)S(1)} %bitcast.9, bf16[3584,512]{1,0:T(8,128)(2,1)S(1)} %bitcast.15, ...), custom_call_target="tpu_custom_call" | custom-call | tf_op jit(solution)/shard_map/pallas_call | solution.py:86
  43.2 2.0 %collective-permute-start.11 = (bf16[64,3584]{1,0:T(8,128)(2,1)S(1)}, bf16[64,3584]{1,0:T(8,128)(2,1)S(1)}, u32[]{:S(2)}, u32[]{:S(2)}) collective-permute-start(bf16[64,3584]{1,0:T(8,128)(2,1)S(1)} %get-tuple-element.112), channel_id=1, source_target_pairs={{4,0},{3,1},{8,4},{1,5},{12,8},{5,9},{14,12},{9,13},{10,14},{13,15... | collective-permute-start | bytes 1376264 | tf_op jit(solution)/shard_map/ppermute | solution.py:173
  45.2 3.2 %shard_map.71 = bf16[64,3584]{1,0:T(8,128)(2,1)S(1)} custom-call(s32[1]{0:T(128)} %bitcast.me, bf16[64,3712]{1,0:T(8,128)(2,1)S(1)} %collective-permute-done.10.refs_0_, bf16[3584,512]{1,0:T(8,128)(2,1)S(1)} %bitcast.10, bf16[3584,512]{1,0:T(8,128)(2,1)S(1)} %bitcast.16, bf16[512,3584]{1,0:T(8,128)(2,1)S(1)} %bitcast.22, ...), custom_call_target="tpu_custom_call" | custom-call | tf_op jit(solution)/shard_map/pallas_call | solution.py:86
  48.3 1.7 %collective-permute-start.15 = (bf16[64,3584]{1,0:T(8,128)(2,1)S(1)}, bf16[64,3584]{1,0:T(8,128)(2,1)S(1)}, u32[]{:S(2)}, u32[]{:S(2)}) collective-permute-start(bf16[64,3584]{1,0:T(8,128)(2,1)S(1)} %shard_map.71), channel_id=1, source_target_pairs={{4,0},{3,1},{8,4},{1,5},{12,8},{5,9},{14,12},{9,13},{10,14},{13,15... | collective-permute-start | bytes 1376264 | tf_op jit(solution)/shard_map/ppermute | solution.py:173
  50.0 1.8 %collective-permute-done.11.came = bf16[64,3584]{1,0:T(8,128)(2,1)S(1)} collective-permute-done((bf16[64,3584]{1,0:T(8,128)(2,1)S(1)}, bf16[64,3584]{1,0:T(8,128)(2,1)S(1)}, u32[]{:S(2)}, u32[]{:S(2)}) %collective-permute-start.11) | collective-permute-done | bytes 458784 | tf_op jit(solution)/shard_map/ppermute | solution.py:173
  51.9 1.8 %collective-permute-start.12 = (bf16[64,3584]{1,0:T(8,128)(2,1)S(1)}, bf16[64,3584]{1,0:T(8,128)(2,1)S(1)}, u32[]{:S(2)}, u32[]{:S(2)}) collective-permute-start(bf16[64,3584]{1,0:T(8,128)(2,1)S(1)} %shard_map.73), channel_id=1, source_target_pairs={{4,0},{3,1},{8,4},{1,5},{12,8},{5,9},{14,12},{9,13},{10,14},{13,15... | collective-permute-start | bytes 1376264 | tf_op jit(solution)/shard_map/ppermute | solution.py:173
  53.8 3.1 %collective-permute-done.15.came = bf16[64,3584]{1,0:T(8,128)(2,1)S(1)} collective-permute-done((bf16[64,3584]{1,0:T(8,128)(2,1)S(1)}, bf16[64,3584]{1,0:T(8,128)(2,1)S(1)}, u32[]{:S(2)}, u32[]{:S(2)}) %collective-permute-start.15) | collective-permute-done | bytes 458784 | tf_op jit(solution)/shard_map/ppermute | solution.py:173
  56.9 0.1 shard_map.75
  57.0 1.7 %collective-permute-start.16 = (bf16[64,3584]{1,0:T(8,128)(2,1)S(1)}, bf16[64,3584]{1,0:T(8,128)(2,1)S(1)}, u32[]{:S(2)}, u32[]{:S(2)}) collective-permute-start(bf16[64,3584]{1,0:T(8,128)(2,1)S(1)} %shard_map.75), channel_id=1, source_target_pairs={{4,0},{3,1},{8,4},{1,5},{12,8},{5,9},{14,12},{9,13},{10,14},{13,15... | collective-permute-start | bytes 1376264 | tf_op jit(solution)/shard_map/ppermute | solution.py:173
  58.7 3.1 %collective-permute-done.12.came = bf16[64,3584]{1,0:T(8,128)(2,1)S(1)} collective-permute-done((bf16[64,3584]{1,0:T(8,128)(2,1)S(1)}, bf16[64,3584]{1,0:T(8,128)(2,1)S(1)}, u32[]{:S(2)}, u32[]{:S(2)}) %collective-permute-start.12) | collective-permute-done | bytes 458784 | tf_op jit(solution)/shard_map/ppermute | solution.py:173
  61.9 1.7 %collective-permute-start.13 = (bf16[64,3584]{1,0:T(8,128)(2,1)S(1)}, bf16[64,3584]{1,0:T(8,128)(2,1)S(1)}, u32[]{:S(2)}, u32[]{:S(2)}) collective-permute-start(bf16[64,3584]{1,0:T(8,128)(2,1)S(1)} %shard_map.74), channel_id=1, source_target_pairs={{4,0},{3,1},{8,4},{1,5},{12,8},{5,9},{14,12},{9,13},{10,14},{13,15... | collective-permute-start | bytes 1376264 | tf_op jit(solution)/shard_map/ppermute | solution.py:173
  63.6 3.1 %collective-permute-done.16.came = bf16[64,3584]{1,0:T(8,128)(2,1)S(1)} collective-permute-done((bf16[64,3584]{1,0:T(8,128)(2,1)S(1)}, bf16[64,3584]{1,0:T(8,128)(2,1)S(1)}, u32[]{:S(2)}, u32[]{:S(2)}) %collective-permute-start.16) | collective-permute-done | bytes 458784 | tf_op jit(solution)/shard_map/ppermute | solution.py:173
  66.7 0.1 shard_map.76
  66.8 1.7 %collective-permute-start.19 = (bf16[32,3584]{1,0:T(8,128)(2,1)S(1)}, bf16[32,3584]{1,0:T(8,128)(2,1)S(1)}, u32[]{:S(2)}, u32[]{:S(2)}) collective-permute-start(bf16[32,3584]{1,0:T(8,128)(2,1)S(1)} %get-tuple-element.118), channel_id=1, source_target_pairs={{4,0},{3,1},{8,4},{1,5},{12,8},{5,9},{14,12},{9,13},{10,14},{13,15... | collective-permute-start | bytes 688136 | tf_op jit(solution)/shard_map/ppermute | solution.py:173
  68.6 1.6 %collective-permute-start.17 = (bf16[32,3584]{1,0:T(8,128)(2,1)S(1)}, bf16[32,3584]{1,0:T(8,128)(2,1)S(1)}, u32[]{:S(2)}, u32[]{:S(2)}) collective-permute-start(bf16[32,3584]{1,0:T(8,128)(2,1)S(1)} %get-tuple-element.117), channel_id=1, source_target_pairs={{4,0},{3,1},{8,4},{1,5},{12,8},{5,9},{14,12},{9,13},{10,14},{13,15... | collective-permute-start | bytes 688136 | tf_op jit(solution)/shard_map/ppermute | solution.py:173
  70.1 1.5 %collective-permute-done.13 = bf16[64,3584]{1,0:T(8,128)(2,1)S(1)} collective-permute-done((bf16[64,3584]{1,0:T(8,128)(2,1)S(1)}, bf16[64,3584]{1,0:T(8,128)(2,1)S(1)}, u32[]{:S(2)}, u32[]{:S(2)}) %collective-permute-start.13) | collective-permute-done | bytes 458784 | tf_op jit(solution)/shard_map/ppermute | solution.py:173
  71.6 2.5 %collective-permute-done.19.came = bf16[32,3584]{1,0:T(8,128)(2,1)S(1)} collective-permute-done((bf16[32,3584]{1,0:T(8,128)(2,1)S(1)}, bf16[32,3584]{1,0:T(8,128)(2,1)S(1)}, u32[]{:S(2)}, u32[]{:S(2)}) %collective-permute-start.19) | collective-permute-done | bytes 229408 | tf_op jit(solution)/shard_map/ppermute | solution.py:173
  74.1 1.7 %collective-permute-start.20 = (bf16[32,3584]{1,0:T(8,128)(2,1)S(1)}, bf16[32,3584]{1,0:T(8,128)(2,1)S(1)}, u32[]{:S(2)}, u32[]{:S(2)}) collective-permute-start(bf16[32,3584]{1,0:T(8,128)(2,1)S(1)} %shard_map.78), channel_id=1, source_target_pairs={{4,0},{3,1},{8,4},{1,5},{12,8},{5,9},{14,12},{9,13},{10,14},{13,15... | collective-permute-start | bytes 688136 | tf_op jit(solution)/shard_map/ppermute | solution.py:173
  75.9 0.7 collective-permute-done.17.came
  76.6 1.7 %collective-permute-start.18 = (bf16[32,3584]{1,0:T(8,128)(2,1)S(1)}, bf16[32,3584]{1,0:T(8,128)(2,1)S(1)}, u32[]{:S(2)}, u32[]{:S(2)}) collective-permute-start(bf16[32,3584]{1,0:T(8,128)(2,1)S(1)} %shard_map.77), channel_id=1, source_target_pairs={{4,0},{3,1},{8,4},{1,5},{12,8},{5,9},{14,12},{9,13},{10,14},{13,15... | collective-permute-start | bytes 688136 | tf_op jit(solution)/shard_map/ppermute | solution.py:173
  78.3 3.1 %shard_map.72.mine = f32[64,3584]{1,0:T(8,128)S(1)} custom-call(s32[1]{0:T(128)} %bitcast.me, bf16[64,3712]{1,0:T(8,128)(2,1)S(1)} %shard_map.64.refs_0_, bf16[3584,512]{1,0:T(8,128)(2,1)S(1)} %bitcast.11, bf16[3584,512]{1,0:T(8,128)(2,1)S(1)} %bitcast.17, bf16[512,3584]{1,0:T(8,128)(2,1)S(1)} %bitcast.23, bf16[3584,512]{1,0:T(8,128)(2,1)S(1)} %shard_map.65.refs_5_.refs_4_, ...), custom_call_target="tpu_custom_call" | custom-call | tf_op jit(solution)/shard_map/pallas_call | solution.py:86
  81.5 1.2 %collective-permute-done.18.refs_0_ = bf16[32,3584]{1,0:T(8,128)(2,1)S(1)} collective-permute-done((bf16[32,3584]{1,0:T(8,128)(2,1)S(1)}, bf16[32,3584]{1,0:T(8,128)(2,1)S(1)}, u32[]{:S(2)}, u32[]{:S(2)}) %collective-permute-start.18) | collective-permute-done | bytes 229408 | tf_op jit(solution)/shard_map/ppermute | solution.py:173
  82.7 0.9 %shard_map.79 = bf16[64,3584]{1,0:T(8,128)(2,1)} custom-call(f32[64,3584]{1,0:T(8,128)S(1)} %shard_map.72.mine, bf16[64,3584]{1,0:T(8,128)(2,1)S(1)} %collective-permute-done.14.other, bf16[32,3584]{1,0:T(8,128)(2,1)S(1)} %collective-permute-done.18.refs_0_, bf16[32,3584]{1,0:T(8,128)(2,1)S(1)} %collective-permute-done.20.refs_1_), custom_call_target="tpu_custom_call" | custom-call | tf_op jit(solution)/shard_map/pallas_call | solution.py:151
  (20 shorter events, 0.3 us)
Async XLA Ops:
  0.8 1.0 %copy-start.3 = (bf16[2,32,3584]{2,1,0:T(8,128)(2,1)S(1)}, bf16[2,32,3584]{2,1,0:T(8,128)(2,1)}, u32[]{:S(2)}) copy-start(bf16[2,32,3584]{2,1,0:T(8,128)(2,1)} %param.6) | copy-start | bytes 1376260
  2.1 2.0 %collective-permute-start.1 = (bf16[64,3712]{1,0:T(8,128)(2,1)S(1)}, bf16[64,3712]{1,0:T(8,128)(2,1)S(1)}, u32[]{:S(2)}, u32[]{:S(2)}) collective-permute-start(bf16[64,3712]{1,0:T(8,128)(2,1)S(1)} %shard_map.64.refs_0_), channel_id=1, source_target_pairs={{0,1},{1,0},{2,3},{3,2},{4,5},{5,4},{6,7},{7,6},{8,9},{9,8},{10,11... | collective-permute-start | bytes 1425416 | tf_op jit(solution)/shard_map/ppermute | solution.py:176
  4.1 12.3 %collective-permute-start.2 = (bf16[3584,512]{1,0:T(8,128)(2,1)}, bf16[3584,512]{1,0:T(8,128)(2,1)}, u32[]{:S(2)}, u32[]{:S(2)}) collective-permute-start(bf16[3584,512]{1,0:T(8,128)(2,1)} %bitcast.6), channel_id=1, source_target_pairs={{0,1},{1,0},{2,3},{3,2},{4,5},{5,4},{6,7},{7,6},{8,9},{9,8},{10,11... | collective-permute-start | bytes 11010056 | tf_op jit(solution)/shard_map/ppermute | solution.py:176
  4.5 17.0 %collective-permute-start.4 = (bf16[3584,512]{1,0:T(8,128)(2,1)}, bf16[3584,512]{1,0:T(8,128)(2,1)}, u32[]{:S(2)}, u32[]{:S(2)}) collective-permute-start(bf16[3584,512]{1,0:T(8,128)(2,1)} %bitcast.12), channel_id=1, source_target_pairs={{0,1},{1,0},{2,3},{3,2},{4,5},{5,4},{6,7},{7,6},{8,9},{9,8},{10,11... | collective-permute-start | bytes 11010056 | tf_op jit(solution)/shard_map/ppermute | solution.py:176
  4.6 21.9 %collective-permute-start.6 = (bf16[512,3584]{1,0:T(8,128)(2,1)}, bf16[512,3584]{1,0:T(8,128)(2,1)}, u32[]{:S(2)}, u32[]{:S(2)}) collective-permute-start(bf16[512,3584]{1,0:T(8,128)(2,1)} %bitcast.18), channel_id=1, source_target_pairs={{0,1},{1,0},{2,3},{3,2},{4,5},{5,4},{6,7},{7,6},{8,9},{9,8},{10,11... | collective-permute-start | bytes 11010056 | tf_op jit(solution)/shard_map/ppermute | solution.py:176
  5.0 9.3 %collective-permute-start = (bf16[64,3712]{1,0:T(8,128)(2,1)S(1)}, bf16[64,3712]{1,0:T(8,128)(2,1)S(1)}, u32[]{:S(2)}, u32[]{:S(2)}) collective-permute-start(bf16[64,3712]{1,0:T(8,128)(2,1)S(1)} %shard_map.64.refs_0_), channel_id=1, source_target_pairs={{0,4},{1,3},{4,8},{5,1},{8,12},{9,5},{12,14},{13,9},{14,10},{15,13... | collective-permute-start | bytes 1425416 | tf_op jit(solution)/shard_map/ppermute | solution.py:170
  7.7 11.7 %collective-permute-start.3 = (bf16[64,3712]{1,0:T(8,128)(2,1)S(1)}, bf16[64,3712]{1,0:T(8,128)(2,1)S(1)}, u32[]{:S(2)}, u32[]{:S(2)}) collective-permute-start(bf16[64,3712]{1,0:T(8,128)(2,1)S(1)} %collective-permute-done.1), channel_id=1, source_target_pairs={{0,4},{1,3},{4,8},{5,1},{8,12},{9,5},{12,14},{13,9},{14,10},{15,13... | collective-permute-start | bytes 1425416 | tf_op jit(solution)/shard_map/ppermute | solution.py:170
  14.3 10.2 %collective-permute-start.5 = (bf16[64,3712]{1,0:T(8,128)(2,1)S(1)}, bf16[64,3712]{1,0:T(8,128)(2,1)S(1)}, u32[]{:S(2)}, u32[]{:S(2)}) collective-permute-start(bf16[64,3712]{1,0:T(8,128)(2,1)S(1)} %collective-permute-done.refs_0_), channel_id=1, source_target_pairs={{0,4},{1,3},{4,8},{5,1},{8,12},{9,5},{12,14},{13,9},{14,10},{15,13... | collective-permute-start | bytes 1425416 | tf_op jit(solution)/shard_map/ppermute | solution.py:170
  19.4 10.2 %collective-permute-start.7 = (bf16[64,3712]{1,0:T(8,128)(2,1)S(1)}, bf16[64,3712]{1,0:T(8,128)(2,1)S(1)}, u32[]{:S(2)}, u32[]{:S(2)}) collective-permute-start(bf16[64,3712]{1,0:T(8,128)(2,1)S(1)} %collective-permute-done.3.refs_1_), channel_id=1, source_target_pairs={{0,4},{1,3},{4,8},{5,1},{8,12},{9,5},{12,14},{13,9},{14,10},{15,13... | collective-permute-start | bytes 1425416 | tf_op jit(solution)/shard_map/ppermute | solution.py:170
  21.4 10.2 %copy-start.2 = (bf16[1,512,3584]{2,1,0:T(8,128)(2,1)S(1)}, bf16[1,512,3584]{2,1,0:T(8,128)(2,1)}, u32[]{:S(2)}) copy-start(bf16[1,512,3584]{2,1,0:T(8,128)(2,1)} %param.11) | copy-start | bytes 11010052
  23.6 8.0 %copy-start = (bf16[1,3584,512]{2,1,0:T(8,128)(2,1)S(1)}, bf16[1,3584,512]{2,1,0:T(8,128)(2,1)}, u32[]{:S(2)}) copy-start(bf16[1,3584,512]{2,1,0:T(8,128)(2,1)} %param.9) | copy-start | bytes 11010052
  23.7 8.0 %copy-start.1 = (bf16[1,3584,512]{2,1,0:T(8,128)(2,1)S(1)}, bf16[1,3584,512]{2,1,0:T(8,128)(2,1)}, u32[]{:S(2)}) copy-start(bf16[1,3584,512]{2,1,0:T(8,128)(2,1)} %param.10) | copy-start | bytes 11010052
  24.4 10.4 %collective-permute-start.8 = (bf16[64,3712]{1,0:T(8,128)(2,1)S(1)}, bf16[64,3712]{1,0:T(8,128)(2,1)S(1)}, u32[]{:S(2)}, u32[]{:S(2)}) collective-permute-start(bf16[64,3712]{1,0:T(8,128)(2,1)S(1)} %collective-permute-done.5.refs_0_), channel_id=1, source_target_pairs={{0,4},{1,3},{4,8},{5,1},{8,12},{9,5},{12,14},{13,9},{14,10},{15,13... | collective-permute-start | bytes 1425416 | tf_op jit(solution)/shard_map/ppermute | solution.py:170
  29.5 10.4 %collective-permute-start.9 = (bf16[64,3712]{1,0:T(8,128)(2,1)S(1)}, bf16[64,3712]{1,0:T(8,128)(2,1)S(1)}, u32[]{:S(2)}, u32[]{:S(2)}) collective-permute-start(bf16[64,3712]{1,0:T(8,128)(2,1)S(1)} %collective-permute-done.7.refs_1_), channel_id=1, source_target_pairs={{0,4},{1,3},{4,8},{5,1},{8,12},{9,5},{12,14},{13,9},{14,10},{15,13... | collective-permute-start | bytes 1425416 | tf_op jit(solution)/shard_map/ppermute | solution.py:170
  34.8 10.4 %collective-permute-start.10 = (bf16[64,3712]{1,0:T(8,128)(2,1)S(1)}, bf16[64,3712]{1,0:T(8,128)(2,1)S(1)}, u32[]{:S(2)}, u32[]{:S(2)}) collective-permute-start(bf16[64,3712]{1,0:T(8,128)(2,1)S(1)} %collective-permute-done.8.refs_0_), channel_id=1, source_target_pairs={{0,4},{1,3},{4,8},{5,1},{8,12},{9,5},{12,14},{13,9},{14,10},{15,13... | collective-permute-start | bytes 1425416 | tf_op jit(solution)/shard_map/ppermute | solution.py:170
  43.2 8.7 %collective-permute-start.11 = (bf16[64,3584]{1,0:T(8,128)(2,1)S(1)}, bf16[64,3584]{1,0:T(8,128)(2,1)S(1)}, u32[]{:S(2)}, u32[]{:S(2)}) collective-permute-start(bf16[64,3584]{1,0:T(8,128)(2,1)S(1)} %get-tuple-element.112), channel_id=1, source_target_pairs={{4,0},{3,1},{8,4},{1,5},{12,8},{5,9},{14,12},{9,13},{10,14},{13,15... | collective-permute-start | bytes 1376264 | tf_op jit(solution)/shard_map/ppermute | solution.py:173
  48.3 8.5 %collective-permute-start.15 = (bf16[64,3584]{1,0:T(8,128)(2,1)S(1)}, bf16[64,3584]{1,0:T(8,128)(2,1)S(1)}, u32[]{:S(2)}, u32[]{:S(2)}) collective-permute-start(bf16[64,3584]{1,0:T(8,128)(2,1)S(1)} %shard_map.71), channel_id=1, source_target_pairs={{4,0},{3,1},{8,4},{1,5},{12,8},{5,9},{14,12},{9,13},{10,14},{13,15... | collective-permute-start | bytes 1376264 | tf_op jit(solution)/shard_map/ppermute | solution.py:173
  51.9 9.9 %collective-permute-start.12 = (bf16[64,3584]{1,0:T(8,128)(2,1)S(1)}, bf16[64,3584]{1,0:T(8,128)(2,1)S(1)}, u32[]{:S(2)}, u32[]{:S(2)}) collective-permute-start(bf16[64,3584]{1,0:T(8,128)(2,1)S(1)} %shard_map.73), channel_id=1, source_target_pairs={{4,0},{3,1},{8,4},{1,5},{12,8},{5,9},{14,12},{9,13},{10,14},{13,15... | collective-permute-start | bytes 1376264 | tf_op jit(solution)/shard_map/ppermute | solution.py:173
  57.0 9.7 %collective-permute-start.16 = (bf16[64,3584]{1,0:T(8,128)(2,1)S(1)}, bf16[64,3584]{1,0:T(8,128)(2,1)S(1)}, u32[]{:S(2)}, u32[]{:S(2)}) collective-permute-start(bf16[64,3584]{1,0:T(8,128)(2,1)S(1)} %shard_map.75), channel_id=1, source_target_pairs={{4,0},{3,1},{8,4},{1,5},{12,8},{5,9},{14,12},{9,13},{10,14},{13,15... | collective-permute-start | bytes 1376264 | tf_op jit(solution)/shard_map/ppermute | solution.py:173
  61.9 9.7 %collective-permute-start.13 = (bf16[64,3584]{1,0:T(8,128)(2,1)S(1)}, bf16[64,3584]{1,0:T(8,128)(2,1)S(1)}, u32[]{:S(2)}, u32[]{:S(2)}) collective-permute-start(bf16[64,3584]{1,0:T(8,128)(2,1)S(1)} %shard_map.74), channel_id=1, source_target_pairs={{4,0},{3,1},{8,4},{1,5},{12,8},{5,9},{14,12},{9,13},{10,14},{13,15... | collective-permute-start | bytes 1376264 | tf_op jit(solution)/shard_map/ppermute | solution.py:173
  66.8 7.3 %collective-permute-start.19 = (bf16[32,3584]{1,0:T(8,128)(2,1)S(1)}, bf16[32,3584]{1,0:T(8,128)(2,1)S(1)}, u32[]{:S(2)}, u32[]{:S(2)}) collective-permute-start(bf16[32,3584]{1,0:T(8,128)(2,1)S(1)} %get-tuple-element.118), channel_id=1, source_target_pairs={{4,0},{3,1},{8,4},{1,5},{12,8},{5,9},{14,12},{9,13},{10,14},{13,15... | collective-permute-start | bytes 688136 | tf_op jit(solution)/shard_map/ppermute | solution.py:173
  68.6 8.0 %collective-permute-start.17 = (bf16[32,3584]{1,0:T(8,128)(2,1)S(1)}, bf16[32,3584]{1,0:T(8,128)(2,1)S(1)}, u32[]{:S(2)}, u32[]{:S(2)}) collective-permute-start(bf16[32,3584]{1,0:T(8,128)(2,1)S(1)} %get-tuple-element.117), channel_id=1, source_target_pairs={{4,0},{3,1},{8,4},{1,5},{12,8},{5,9},{14,12},{9,13},{10,14},{13,15... | collective-permute-start | bytes 688136 | tf_op jit(solution)/shard_map/ppermute | solution.py:173
  71.6 11.1 %collective-permute-start.14 = (bf16[64,3584]{1,0:T(8,128)(2,1)S(1)}, bf16[64,3584]{1,0:T(8,128)(2,1)S(1)}, u32[]{:S(2)}, u32[]{:S(2)}) collective-permute-start(bf16[64,3584]{1,0:T(8,128)(2,1)S(1)} %collective-permute-done.13), channel_id=1, source_target_pairs={{0,1},{1,0},{2,3},{3,2},{4,5},{5,4},{6,7},{7,6},{8,9},{9,8},{10,11... | collective-permute-start | bytes 1376264 | tf_op jit(solution)/shard_map/ppermute | solution.py:176
  74.1 7.4 %collective-permute-start.20 = (bf16[32,3584]{1,0:T(8,128)(2,1)S(1)}, bf16[32,3584]{1,0:T(8,128)(2,1)S(1)}, u32[]{:S(2)}, u32[]{:S(2)}) collective-permute-start(bf16[32,3584]{1,0:T(8,128)(2,1)S(1)} %shard_map.78), channel_id=1, source_target_pairs={{4,0},{3,1},{8,4},{1,5},{12,8},{5,9},{14,12},{9,13},{10,14},{13,15... | collective-permute-start | bytes 688136 | tf_op jit(solution)/shard_map/ppermute | solution.py:173
  76.6 6.1 %collective-permute-start.18 = (bf16[32,3584]{1,0:T(8,128)(2,1)S(1)}, bf16[32,3584]{1,0:T(8,128)(2,1)S(1)}, u32[]{:S(2)}, u32[]{:S(2)}) collective-permute-start(bf16[32,3584]{1,0:T(8,128)(2,1)S(1)} %shard_map.77), channel_id=1, source_target_pairs={{4,0},{3,1},{8,4},{1,5},{12,8},{5,9},{14,12},{9,13},{10,14},{13,15... | collective-permute-start | bytes 688136 | tf_op jit(solution)/shard_map/ppermute | solution.py:173
